TPU v7x, 128 devices: a whole 4x4x4 slice. The times are simulated.
128 devices in a mesh: section: 2 (over core), fsdp: 4 (over x), ctx: 16 (over z, y).
Axes of the slice: x: 4, y: 4, z: 4, core: 2. Of those that a mesh axis runs over, the one named last changes fastest.
Arguments:
- inputs: bfloat16 [8, 1024, 1536], P('fsdp', 'ctx'), may hold values from -6 to 6
- positions: int32 [8, 1024], P('fsdp', 'ctx'), may hold values from 0 to 1023, as said below
- out_grad: bfloat16 [8, 1024, 1536], P('fsdp', 'ctx'), may hold values from -6 to 6
- norm_attn: bfloat16 [2, 1536], P('section', 'fsdp'), may hold values from 0.099609375 to 1.8984375
- w_query: bfloat16 [2, 1536, 1536], P('section', 'fsdp'), may hold values from -0.15625 to 0.15625
- key_weight: bfloat16 [2, 1536, 768], P('section', 'fsdp'), may hold values from -0.15625 to 0.15625
- value_weight: bfloat16 [2, 1536, 768], P('section', 'fsdp'), may hold values from -0.15625 to 0.15625
- output_weight: bfloat16 [2, 1536, 1536], P('section', 'fsdp'), may hold values from -1.25 to 1.25
- norm_mlp: bfloat16 [2, 1536], P('section', 'fsdp'), may hold values from 0.099609375 to 1.8984375
- w_gate: bfloat16 [2, 1536, 4096], P('section', 'fsdp'), may hold values from -0.15625 to 0.15625
- w_up: bfloat16 [2, 1536, 4096], P('section', 'fsdp'), may hold values from -0.15625 to 0.15625
- w_down: bfloat16 [2, 4096, 1536], P('section', 'fsdp'), may hold values from -0.09375 to 0.09375
Outputs:
- section_out: bfloat16 [2, 8, 1024, 1536], P('section', 'fsdp', 'ctx')
- section_grad: bfloat16 [2, 8, 1024, 1536], P('section', 'fsdp', 'ctx')
- grad_norm_attn: float32 [2, 1536], P('section', 'fsdp')
- grad_query: float32 [2, 1536, 1536], P('section', 'fsdp')
- grad_key: float32 [2, 1536, 768], P('section', 'fsdp')
- grad_value: float32 [2, 1536, 768], P('section', 'fsdp')
- grad_out: float32 [2, 1536, 1536], P('section', 'fsdp')
- grad_norm_mlp: float32 [2, 1536], P('section', 'fsdp')
- grad_gate: float32 [2, 1536, 4096], P('section', 'fsdp')
- grad_up: float32 [2, 1536, 4096], P('section', 'fsdp')
- grad_down: float32 [2, 4096, 1536], P('section', 'fsdp')
Inputs may be any that keep to these rules, and one draw needn't show every extreme that they name: In every sequence each position appears once. The rows of a sequence fall into blocks of 32 rows of consecutive rising positions starting at a multiple of 32; the first half of each ctx device's rows holds block p and its second half block 2 N - 1 - p, with N the devices of ctx and p a different number for each device.
All inputs are finite; a program needn't handle non-finite values.
Results may differ from a plain program's by a relative error of at most 0.029.
Values may be sent and summed in bfloat16 or wider, within the bound.
A program may use at most 384 MiB of HBM per device.

v0:
```python
import jax
import jax.numpy as jnp
from jax import lax
from jax.sharding import PartitionSpec as P

QUERY_HEADS = 16
KEY_VALUE_HEADS = 8
HEAD_SIZE = 96


THETA = 100000.0
EPSILON = 1e-05


def from_behind(value, axis, steps):
    count = lax.axis_size(axis)
    leading, last = (max(0, -steps), min(count, count - steps))
    return lax.ppermute(value, axis, [(source, source + steps) for source in range(leading, last)])


def for_sending(value):

    def short(part):
        return part.astype(jnp.bfloat16) if part.dtype == jnp.float32 else part

    return jax.tree.map(short, value)


def rms_scale(values, gain_vec):
    return (
        values * lax.rsqrt(jnp.mean(values * values, axis=-1, keepdims=True) + EPSILON) * gain_vec
    )


def rotary_turn(values, token_locations, direction):
    half_width = values.shape[-1] // 2
    frequency = THETA ** (-(jnp.arange(half_width, dtype=jnp.float32) * 2.0 / values.shape[-1]))
    angles = token_locations.astype(jnp.float32)[:, None] * frequency[None, :]
    cosine = jnp.cos(angles)[:, None, :]
    sine_part = direction * jnp.sin(angles)[:, None, :]
    first_half = values[..., :half_width]
    second_half = values[..., half_width:]
    return jnp.concatenate(
        [
            first_half * cosine - second_half * sine_part,
            second_half * cosine + first_half * sine_part,
        ],
        axis=-1,
    )


def matrix_product(left_side, right_side):
    return jnp.dot(left_side, right_side, preferred_element_type=jnp.float32)


def matmul_tn(left_side, right_side):
    return lax.dot_general(
        left_side, right_side, (((0,), (0,)), ((), ())), preferred_element_type=jnp.float32
    )


def product_transposed(left_side, right_side):
    return lax.dot_general(
        left_side, right_side, (((1,), (1,)), ((), ())), preferred_element_type=jnp.float32
    )


def swiglu(gate_proj, up_proj):
    return jax.nn.silu(gate_proj) * up_proj


def score_block(query_rows, every_key_row, token_locations, all_places):
    count_of_rows = query_rows.shape[0]
    grouped_heads = query_rows.reshape(
        count_of_rows, KEY_VALUE_HEADS, QUERY_HEADS // KEY_VALUE_HEADS, HEAD_SIZE
    )
    scores = jnp.einsum(
        "pajv,eav->ajpe",
        grouped_heads,
        every_key_row.reshape(-1, KEY_VALUE_HEADS, HEAD_SIZE),
        preferred_element_type=jnp.float32,
    ) * HEAD_SIZE ** (-0.5)
    visible = token_locations[:, None] >= all_places[None, :]
    return jnp.where(visible, scores, -1e30)


def layer_forward(stream_in, token_locations, all_places, weights):
    gain_attn, w_query, key_weight, value_weight, output_weight, gain_mlp, w_gate, w_up, w_down = (
        weights
    )
    count_of_rows = stream_in.shape[0]
    stream = stream_in.astype(jnp.float32)
    normalized = rms_scale(stream, gain_attn.astype(jnp.float32)).astype(jnp.bfloat16)
    query_rows = rotary_turn(
        matrix_product(normalized, w_query).reshape(count_of_rows, QUERY_HEADS, HEAD_SIZE),
        token_locations,
        1.0,
    ).astype(jnp.bfloat16)
    rows_of_keys = (
        rotary_turn(
            matrix_product(normalized, key_weight).reshape(
                count_of_rows, KEY_VALUE_HEADS, HEAD_SIZE
            ),
            token_locations,
            1.0,
        )
        .astype(jnp.bfloat16)
        .reshape(count_of_rows, KEY_VALUE_HEADS * HEAD_SIZE)
    )
    rows_of_values = matrix_product(normalized, value_weight).astype(jnp.bfloat16)
    every_key_row, every_value_row = (
        lax.all_gather(rows_of_keys, "ctx", axis=0, tiled=True),
        lax.all_gather(rows_of_values, "ctx", axis=0, tiled=True),
    )
    scores = score_block(query_rows, every_key_row, token_locations, all_places)
    row_max = jnp.max(scores, axis=-1, keepdims=True)
    exponent = jnp.exp(scores - row_max)
    denominator = jnp.sum(exponent, axis=-1, keepdims=True)
    probabilities = (exponent / denominator).astype(jnp.bfloat16)
    log_total = row_max + jnp.log(denominator)
    attention = jnp.einsum(
        "kgrl,lkd->rkgd",
        probabilities,
        every_value_row.reshape(-1, KEY_VALUE_HEADS, HEAD_SIZE),
        preferred_element_type=jnp.float32,
    )
    attention = attention.reshape(count_of_rows, QUERY_HEADS * HEAD_SIZE).astype(jnp.bfloat16)
    stream_mid = stream + matrix_product(attention, output_weight)
    normed_mlp = rms_scale(stream_mid, gain_mlp.astype(jnp.float32)).astype(jnp.bfloat16)
    gate_proj = matrix_product(normed_mlp, w_gate)
    up_proj = matrix_product(normed_mlp, w_up)
    hidden = swiglu(gate_proj, up_proj).astype(jnp.bfloat16)
    result = (stream_mid + matrix_product(hidden, w_down)).astype(jnp.bfloat16)
    stored = (
        stream_in,
        token_locations,
        all_places,
        normalized,
        query_rows,
        every_key_row,
        every_value_row,
        log_total,
        attention,
        stream_mid,
        normed_mlp,
        gate_proj,
        up_proj,
        hidden,
    )
    return (result, stored)


def layer_backward(grad_result, stored, weights):
    gain_attn, w_query, key_weight, value_weight, output_weight, gain_mlp, w_gate, w_up, w_down = (
        weights
    )
    (
        stream_in,
        token_locations,
        all_places,
        normalized,
        query_rows,
        every_key_row,
        every_value_row,
        log_total,
        attention,
        stream_mid,
        normed_mlp,
        gate_proj,
        up_proj,
        hidden,
    ) = stored
    count_of_rows = stream_in.shape[0]
    grad_stream = grad_result.astype(jnp.float32)
    grad_down = matmul_tn(hidden, grad_result)
    grad_hidden = product_transposed(grad_result, w_down)
    _, swiglu_back = jax.vjp(swiglu, gate_proj, up_proj)
    grad_gate_f, grad_up_f = swiglu_back(grad_hidden)
    grad_gate_b = grad_gate_f.astype(jnp.bfloat16)
    grad_up_b = grad_up_f.astype(jnp.bfloat16)
    grad_gate = matmul_tn(normed_mlp, grad_gate_b)
    grad_up = matmul_tn(normed_mlp, grad_up_b)
    grad_normed_mlp = product_transposed(grad_gate_b, w_gate) + product_transposed(grad_up_b, w_up)
    _, norm_back_mlp = jax.vjp(rms_scale, stream_mid, gain_mlp.astype(jnp.float32))
    grad_mid_norm, grad_gain_mlp = norm_back_mlp(grad_normed_mlp)
    grad_mid = grad_stream + grad_mid_norm
    branch_gradient = grad_mid.astype(jnp.bfloat16)
    grad_wout = matmul_tn(attention, branch_gradient)
    grad_attention = (
        product_transposed(branch_gradient, output_weight)
        .astype(jnp.bfloat16)
        .reshape(count_of_rows, KEY_VALUE_HEADS, QUERY_HEADS // KEY_VALUE_HEADS, HEAD_SIZE)
    )
    scores = score_block(query_rows, every_key_row, token_locations, all_places)
    probabilities = jnp.exp(scores - log_total)
    heads_of_keys = every_key_row.reshape(-1, KEY_VALUE_HEADS, HEAD_SIZE)
    heads_of_values = every_value_row.reshape(-1, KEY_VALUE_HEADS, HEAD_SIZE)
    grouped_heads = query_rows.reshape(
        count_of_rows, KEY_VALUE_HEADS, QUERY_HEADS // KEY_VALUE_HEADS, HEAD_SIZE
    )
    grad_probs = jnp.einsum(
        "pajv,eav->ajpe", grad_attention, heads_of_values, preferred_element_type=jnp.float32
    )
    value_term = jnp.einsum(
        "kgrl,rkgd->lkd",
        probabilities.astype(jnp.bfloat16),
        grad_attention,
        preferred_element_type=jnp.float32,
    ).reshape(-1, KEY_VALUE_HEADS * HEAD_SIZE)
    row_dot = jnp.sum(probabilities * grad_probs, axis=-1, keepdims=True)
    grad_scores = (probabilities * (grad_probs - row_dot)).astype(jnp.bfloat16)
    grad_queries = jnp.einsum(
        "kgrl,lkd->rkgd", grad_scores, heads_of_keys, preferred_element_type=jnp.float32
    ) * HEAD_SIZE ** (-0.5)
    key_term = jnp.einsum(
        "kgrl,rkgd->lkd", grad_scores, grouped_heads, preferred_element_type=jnp.float32
    ).reshape(-1, KEY_VALUE_HEADS * HEAD_SIZE) * HEAD_SIZE ** (-0.5)
    key_gradient, grad_values = (
        lax.psum_scatter(
            key_term.astype(jnp.bfloat16), "ctx", scatter_dimension=0, tiled=True
        ).astype(jnp.float32),
        lax.psum_scatter(
            value_term.astype(jnp.bfloat16), "ctx", scatter_dimension=0, tiled=True
        ).astype(jnp.float32),
    )
    grad_query_proj = (
        rotary_turn(
            grad_queries.reshape(count_of_rows, QUERY_HEADS, HEAD_SIZE), token_locations, -1.0
        )
        .reshape(count_of_rows, QUERY_HEADS * HEAD_SIZE)
        .astype(jnp.bfloat16)
    )
    grad_key_proj = (
        rotary_turn(
            key_gradient.reshape(count_of_rows, KEY_VALUE_HEADS, HEAD_SIZE), token_locations, -1.0
        )
        .reshape(count_of_rows, KEY_VALUE_HEADS * HEAD_SIZE)
        .astype(jnp.bfloat16)
    )
    grad_value_proj = grad_values.astype(jnp.bfloat16)
    grad_query = matmul_tn(normalized, grad_query_proj)
    grad_key = matmul_tn(normalized, grad_key_proj)
    grad_value = matmul_tn(normalized, grad_value_proj)
    grad_normed = (
        product_transposed(grad_query_proj, w_query)
        + product_transposed(grad_key_proj, key_weight)
        + product_transposed(grad_value_proj, value_weight)
    )
    _, norm_back_attn = jax.vjp(
        rms_scale, stream_in.astype(jnp.float32), gain_attn.astype(jnp.float32)
    )
    grad_in_norm, grad_gain_attn = norm_back_attn(grad_normed)
    grad_input = (grad_mid + grad_in_norm).astype(jnp.bfloat16)
    return (
        grad_input,
        (
            grad_gain_attn,
            grad_query,
            grad_key,
            grad_value,
            grad_wout,
            grad_gain_mlp,
            grad_gate,
            grad_up,
            grad_down,
        ),
    )


def local(
    inputs,
    positions,
    out_grad,
    norm_attn,
    w_query,
    key_weight,
    value_weight,
    output_weight,
    norm_mlp,
    w_gate,
    w_up,
    w_down,
):
    micro_count = inputs.shape[0]
    section_idx = lax.axis_index("section")
    is_first = section_idx == 0

    def choose(first_value, second_value):
        return jnp.where(is_first, first_value, second_value)

    all_positions = lax.all_gather(positions, "ctx", axis=1, tiled=True)
    shards = (
        norm_attn,
        w_query,
        key_weight,
        value_weight,
        output_weight,
        norm_mlp,
        w_gate,
        w_up,
        w_down,
    )
    gathered = (
        lax.all_gather(shards[0], "fsdp", axis=1, tiled=True),
        lax.all_gather(shards[1], "fsdp", axis=1, tiled=True),
        lax.all_gather(shards[2], "fsdp", axis=1, tiled=True),
        lax.all_gather(shards[3], "fsdp", axis=1, tiled=True),
        lax.all_gather(shards[4], "fsdp", axis=1, tiled=True),
        lax.all_gather(shards[5], "fsdp", axis=1, tiled=True),
        lax.all_gather(shards[6], "fsdp", axis=1, tiled=True),
        lax.all_gather(shards[7], "fsdp", axis=1, tiled=True),
        lax.all_gather(shards[8], "fsdp", axis=1, tiled=True),
    )
    weights = tuple((member[0] for member in gathered))
    received = jnp.zeros_like(inputs[0])
    results = []
    stored_list = []
    for clock_idx in range(micro_count + 1):
        first_micro = min(clock_idx, micro_count - 1)
        second_micro = max(clock_idx - 1, 0)
        own_input = inputs[first_micro] if clock_idx < micro_count else jnp.zeros_like(inputs[0])
        stream_in = choose(own_input, received)
        token_locations = choose(positions[first_micro], positions[second_micro])
        every_place = choose(all_positions[first_micro], all_positions[second_micro])
        result, stored = layer_forward(stream_in, token_locations, every_place, weights)
        results.append(result)
        stored_list.append(stored)
        if clock_idx < micro_count:
            received = from_behind(result, "section", 1)
    section_out = choose(jnp.stack(results[:micro_count]), jnp.stack(results[1:]))[None]
    gathered = (
        lax.all_gather(shards[0], "fsdp", axis=1, tiled=True),
        lax.all_gather(shards[1], "fsdp", axis=1, tiled=True),
        lax.all_gather(shards[2], "fsdp", axis=1, tiled=True),
        lax.all_gather(shards[3], "fsdp", axis=1, tiled=True),
        lax.all_gather(shards[4], "fsdp", axis=1, tiled=True),
        lax.all_gather(shards[5], "fsdp", axis=1, tiled=True),
        lax.all_gather(shards[6], "fsdp", axis=1, tiled=True),
        lax.all_gather(shards[7], "fsdp", axis=1, tiled=True),
        lax.all_gather(shards[8], "fsdp", axis=1, tiled=True),
    )
    weights = tuple((member[0] for member in gathered))
    totals = None
    grads_in = []
    received = jnp.zeros_like(out_grad[0])
    for clock_idx in range(micro_count + 1):
        first_clock = max(clock_idx - 1, 0)
        second_clock = min(clock_idx + 1, micro_count)
        stored = jax.tree.map(choose, stored_list[first_clock], stored_list[second_clock])
        own_grad = out_grad[clock_idx] if clock_idx < micro_count else jnp.zeros_like(out_grad[0])
        grad_result = choose(received, own_grad)
        grad_input, layer_grads = layer_backward(grad_result, stored, weights)
        if totals is None:
            totals = layer_grads
        else:
            totals = tuple((before + after for before, after in zip(totals, layer_grads)))
        grads_in.append(grad_input)
        if clock_idx < micro_count:
            received = from_behind(grad_input, "section", -1)
    section_grad = choose(jnp.stack(grads_in[1:]), jnp.stack(grads_in[:micro_count]))[None]
    grad_parts = lax.psum_scatter(totals, ("fsdp", "ctx"), scatter_dimension=0, tiled=True)
    summed = jax.tree.map(
        lambda part, own: part.astype(own.dtype),
        lax.all_gather(for_sending(grad_parts), "ctx", axis=0, tiled=True),
        grad_parts,
    )
    return (section_out, section_grad) + tuple((member[None] for member in summed))


def solution(mesh):
    return jax.shard_map(
        local,
        mesh=mesh,
        in_specs=(
            P("fsdp", "ctx", None),
            P("fsdp", "ctx"),
            P("fsdp", "ctx", None),
            P("section", "fsdp"),
            P("section", "fsdp", None),
            P("section", "fsdp", None),
            P("section", "fsdp", None),
            P("section", "fsdp", None),
            P("section", "fsdp"),
            P("section", "fsdp", None),
            P("section", "fsdp", None),
            P("section", "fsdp", None),
        ),
        out_specs=(
            P("section", "fsdp", "ctx", None),
            P("section", "fsdp", "ctx", None),
            P("section", "fsdp"),
            P("section", "fsdp", None),
            P("section", "fsdp", None),
            P("section", "fsdp", None),
            P("section", "fsdp", None),
            P("section", "fsdp"),
            P("section", "fsdp", None),
            P("section", "fsdp", None),
            P("section", "fsdp", None),
        ),
        check_vma=False,
    )
```

profile of v0, /device:TPU:0, one launch (start us, length us, event | category | flops | bytes accessed | tf_op | source)
XLA Modules:
  0.0 3401.2 jit_solution(10878571615721547193)
XLA Ops:
  8.7 11.3 all_gather.84
  21.2 23.9 all-gather.20.cloned.1.call-done
  51.3 28.6 all-gather.24.cloned.1.call-done
  88.4 23.5 all-gather
  112.0 10.6 all_gather.92
  129.4 43.3 %all-gather.26.cloned.1.call-done = bf16[1024,768]{1,0:T(8,128)(2,1)} async-done(((bf16[64,768]{1,0:T(8,128)(2,1)}), bf16[1024,768]{1,0:T(8,128)(2,1)}) %all-gather.26.cloned.1.call-update) | async-done | bytes 1572880 | tf_op jit(solution)/shard_map/all_gather | solution.py:112
  174.5 51.6 %all-gather.28.cloned.1.call-done = bf16[1,1536,1536]{2,1,0:T(8,128)(2,1)} async-done(((bf16[1,384,1536]{2,1,0:T(8,128)(2,1)}), bf16[1,1536,1536]{2,1,0:T(8,128)(2,1)}) %all-gather.28.cloned.1.call-update) | async-done | bytes 4718608 | tf_op jit(solution)/shard_map/all_gather | solution.py:305
  226.1 6.6 copy.146
  242.1 38.6 %all-gather.30.cloned.1.call-done = bf16[1,1536,1536]{2,1,0:T(8,128)(2,1)} async-done(((bf16[1,384,1536]{2,1,0:T(8,128)(2,1)}), bf16[1,1536,1536]{2,1,0:T(8,128)(2,1)}) %all-gather.30.cloned.1.call-update) | async-done | bytes 4718608 | tf_op jit(solution)/shard_map/all_gather | solution.py:308
  284.2 117.2 %all-gather.32.cloned.1.call-done = bf16[1,1536,4096]{2,1,0:T(8,128)(2,1)} async-done(((bf16[1,384,4096]{2,1,0:T(8,128)(2,1)}), bf16[1,1536,4096]{2,1,0:T(8,128)(2,1)}) %all-gather.32.cloned.1.call-update) | async-done | bytes 12582928 | tf_op jit(solution)/shard_map/all_gather | solution.py:310
  401.4 6.9 fusion.34
  408.3 114.4 %all-gather.34.cloned.1.call-done = bf16[1,1536,4096]{2,1,0:T(8,128)(2,1)} async-done(((bf16[1,384,4096]{2,1,0:T(8,128)(2,1)}), bf16[1,1536,4096]{2,1,0:T(8,128)(2,1)}) %all-gather.34.cloned.1.call-update) | async-done | bytes 12582928 | tf_op jit(solution)/shard_map/all_gather | solution.py:311
  522.7 7.9 multiply_convert_fusion.5
  530.5 113.4 %all-gather.36.cloned.1.call-done = bf16[1,4096,1536]{2,1,0:T(8,128)(2,1)} async-done(((bf16[1,1024,1536]{2,1,0:T(8,128)(2,1)}), bf16[1,4096,1536]{2,1,0:T(8,128)(2,1)}) %all-gather.36.cloned.1.call-update) | async-done | bytes 12582928 | tf_op jit(solution)/shard_map/all_gather | solution.py:312
  643.9 6.8 fusion.147
  665.5 40.0 %all-gather.40.cloned.1.call-done = bf16[1024,768]{1,0:T(8,128)(2,1)} async-done(((bf16[64,768]{1,0:T(8,128)(2,1)}), bf16[1024,768]{1,0:T(8,128)(2,1)}) %all-gather.40.cloned.1.call-update) | async-done | bytes 1572880 | tf_op jit(solution)/shard_map/all_gather | solution.py:112
  713.6 38.0 %all-gather.38.cloned.1.call-done = bf16[1024,768]{1,0:T(8,128)(2,1)} async-done(((bf16[64,768]{1,0:T(8,128)(2,1)}), bf16[1024,768]{1,0:T(8,128)(2,1)}) %all-gather.38.cloned.1.call-update) | async-done | bytes 1572880 | tf_op jit(solution)/shard_map/all_gather | solution.py:113
  763.0 7.0 fusion.20
  772.5 9.9 fusion.206
  782.5 7.0 fusion.144
  800.8 9.2 fusion.16
  814.6 27.9 all-gather.44.cloned.1.call-done
  850.5 38.0 %all-gather.42.cloned.1.call-done = bf16[1024,768]{1,0:T(8,128)(2,1)} async-done(((bf16[64,768]{1,0:T(8,128)(2,1)}), bf16[1024,768]{1,0:T(8,128)(2,1)}) %all-gather.42.cloned.1.call-update) | async-done | bytes 1572880 | tf_op jit(solution)/shard_map/all_gather | solution.py:113
  904.4 10.1 multiply_reduce_fusion.2
  978.3 8.1 fusion.18
  989.7 32.6 reduce-scatter.40.cloned.1.call-done
  1027.7 70.6 %reduce-scatter.42.cloned.1.call-done = bf16[64,768]{1,0:T(8,128)(2,1)} async-done(((bf16[1024,768]{1,0:T(8,128)(2,1)}), bf16[64,768]{1,0:T(8,128)(2,1)}) %reduce-scatter.42.cloned.1.call-update) | async-done | bytes 98320
  1106.3 10.3 fusion.209
  1116.6 5.0 fusion.14
  1121.6 9.2 multiply_reduce_fusion.1
  1169.8 48.4 %reduce-scatter.44.cloned.1.call-done = bf16[64,768]{1,0:T(8,128)(2,1)} async-done(((bf16[1024,768]{1,0:T(8,128)(2,1)}), bf16[64,768]{1,0:T(8,128)(2,1)}) %reduce-scatter.44.cloned.1.call-update) | async-done | bytes 98320
  1225.0 69.3 %reduce-scatter.46.cloned.1.call-done = bf16[64,768]{1,0:T(8,128)(2,1)} async-done(((bf16[1024,768]{1,0:T(8,128)(2,1)}), bf16[64,768]{1,0:T(8,128)(2,1)}) %reduce-scatter.46.cloned.1.call-update) | async-done | bytes 98320
  1301.5 10.6 fusion.212
  1312.1 8.9 fusion.12
  1357.3 8.8 convolution_add_fusion.2
  1378.1 10.4 fusion.291
  1388.5 10.3 fusion.293
  1398.8 26.5 add_add_fusion.2
  1426.3 10.2 fusion.290
  1436.5 10.3 fusion.292
  1446.8 26.5 add_add_fusion.1
  1474.7 10.2 fusion.216
  1484.9 10.2 fusion.214
  1495.1 26.6 add_add_fusion
  1530.4 6.9 add_add_fusion.4
  1544.3 6.9 add_add_fusion.3
  1551.4 169.6 %reduce-scatter.26.cloned.1.call-done = f32[24,1536]{1,0:T(8,128)} async-done(((f32[1536,1536]{1,0:T(8,128)}), f32[24,1536]{1,0:T(8,128)}) %reduce-scatter.26.cloned.1.call-update) | async-done | bytes 147472 | tf_op jit(solution)/shard_map/reduce_scatter | solution.py:361
  1722.6 228.0 %reduce-scatter.32.cloned.1.call-done = f32[24,1536]{1,0:T(8,128)} async-done(((f32[1536,1536]{1,0:T(8,128)}), f32[24,1536]{1,0:T(8,128)}) %reduce-scatter.32.cloned.1.call-update) | async-done | bytes 147472 | tf_op jit(solution)/shard_map/reduce_scatter | solution.py:361
  1952.2 249.7 %reduce-scatter.34.cloned.1.call-done = f32[24,4096]{1,0:T(8,128)} async-done(((f32[1536,4096]{1,0:T(8,128)}), f32[24,4096]{1,0:T(8,128)}) %reduce-scatter.34.cloned.1.call-update) | async-done | bytes 393232 | tf_op jit(solution)/shard_map/reduce_scatter | solution.py:361
  2203.6 249.3 %reduce-scatter.36.cloned.1.call-done = f32[24,4096]{1,0:T(8,128)} async-done(((f32[1536,4096]{1,0:T(8,128)}), f32[24,4096]{1,0:T(8,128)}) %reduce-scatter.36.cloned.1.call-update) | async-done | bytes 393232 | tf_op jit(solution)/shard_map/reduce_scatter | solution.py:361
  2458.4 6.9 fusion.159
  2470.1 234.1 %reduce-scatter.38.cloned.1.call-done = f32[64,1536]{1,0:T(8,128)} async-done(((f32[4096,1536]{1,0:T(8,128)}), f32[64,1536]{1,0:T(8,128)}) %reduce-scatter.38.cloned.1.call-update) | async-done | bytes 393232 | tf_op jit(solution)/shard_map/reduce_scatter | solution.py:361
  2710.9 345.3 %all-reduce.4 = (bf16[1536]{0:T(1024)(128)(2,1)S(1)}, bf16[1536]{0:T(1024)(128)(2,1)S(1)}) all-reduce(f32[1536]{0:T(1024)S(1)} %add_add_fusion.12, f32[1536]{0:T(1024)} %add_add_fusion.11), channel_id=8, replica_groups=mesh['section'=2,'fsdp'=4,'ctx'=16] {'fsdp','ctx'}, use_global_device_ids=true, to_apply=%region_36.37.clone | all-reduce | flops 3072 | bytes 18432
  3056.8 35.5 %all-reduce.5 = (bf16[384]{0:T(512)(128)(2,1)S(1)}, bf16[384]{0:T(512)(128)(2,1)S(1)}) all-reduce(bf16[384]{0:T(512)(128)(2,1)S(1)} %dynamic-update-slice, bf16[384]{0:T(512)(128)(2,1)S(1)} %dynamic-update-slice.1), channel_id=1, replica_groups=mesh['section'=2,'fsdp'=4,'ctx'=16] {'ctx'}, use_global_device_ids=true, to_apply=%add | all-reduce | flops 768 | bytes 3072
  3097.6 54.9 %reduce-scatter.30.cloned.1.call-done = f32[24,768]{1,0:T(8,128)} async-done(((f32[1536,768]{1,0:T(8,128)}), f32[24,768]{1,0:T(8,128)}) %reduce-scatter.30.cloned.1.call-update) | async-done | bytes 73744 | tf_op jit(solution)/shard_map/reduce_scatter | solution.py:361
  3153.4 22.2 all_gather.102
  3175.6 23.9 all_gather.103
  3204.7 35.9 %all-gather.48.cloned.1.call-done = bf16[384,1536]{1,0:T(8,128)(2,1)} async-done(((bf16[24,1536]{1,0:T(8,128)(2,1)}), bf16[384,1536]{1,0:T(8,128)(2,1)}) %all-gather.48.cloned.1.call-update) | async-done | bytes 1179664 | tf_op jit(solution)/shard_map/all_gather | solution.py:364
  3243.6 47.1 %all-gather.50.cloned.1.call-done = bf16[384,4096]{1,0:T(8,128)(2,1)} async-done(((bf16[24,4096]{1,0:T(8,128)(2,1)}), bf16[384,4096]{1,0:T(8,128)(2,1)}) %all-gather.50.cloned.1.call-update) | async-done | bytes 3145744 | tf_op jit(solution)/shard_map/all_gather | solution.py:364
  3290.8 5.4 bitcast_convert_fusion.2
  3296.1 43.6 %all-gather.52.cloned.1.call-done = bf16[384,4096]{1,0:T(8,128)(2,1)} async-done(((bf16[24,4096]{1,0:T(8,128)(2,1)}), bf16[384,4096]{1,0:T(8,128)(2,1)}) %all-gather.52.cloned.1.call-update) | async-done | bytes 3145744 | tf_op jit(solution)/shard_map/all_gather | solution.py:364
  3339.7 5.4 bitcast_convert_fusion.1
  3345.0 43.7 %all-gather.54.cloned.1.call-done = bf16[1024,1536]{1,0:T(8,128)(2,1)} async-done(((bf16[64,1536]{1,0:T(8,128)(2,1)}), bf16[1024,1536]{1,0:T(8,128)(2,1)}) %all-gather.54.cloned.1.call-update) | async-done | bytes 3145744 | tf_op jit(solution)/shard_map/all_gather | solution.py:364
  3388.7 5.5 bitcast_convert_fusion
  (678 shorter events, 348.1 us)
Async XLA Ops:
  7.2 38.0 %all-gather.20.cloned.1.call-start = ((), (), s32[]{:S(2)}) async-start(), calls=%async_computation.13 | async-start | bytes 2949120 | tf_op jit(solution)/shard_map/all_gather | solution.py:307
  7.9 72.0 %all-gather.24.cloned.1.call-start = ((), (), s32[]{:S(2)}) async-start(), calls=%async_computation.15 | async-start | bytes 2949120 | tf_op jit(solution)/shard_map/all_gather | solution.py:306
  8.7 118.2 %all-gather.22.cloned.1.call-start = ((), (), s32[]{:S(2)}) async-start(), calls=%async_computation.14 | async-start | bytes 1671168 | tf_op jit(solution)/shard_map/all_gather | solution.py:113
  20.1 1337.2 %copy-start.62 = (f32[1536]{0:T(1024)}, f32[1536]{0:T(1024)S(1)}, u32[]{:S(2)}) copy-start(f32[1536]{0:T(1024)S(1)} %convert_reduce_fusion.1) | copy-start | bytes 18436
  21.2 211.5 %copy-start.133 = (f32[64]{0:T(128)}, f32[64]{0:T(128)S(1)}, u32[]{:S(2)}) copy-start(f32[64]{0:T(128)S(1)} %add_rsqrt_fusion.5) | copy-start | bytes 772
  48.2 124.6 %all-gather.26.cloned.1.call-start = ((), (), s32[]{:S(2)}) async-start(), calls=%async_computation.16 | async-start | bytes 1671168 | tf_op jit(solution)/shard_map/all_gather | solution.py:112
  85.0 141.2 %all-gather.28.cloned.1.call-start = ((), (), s32[]{:S(2)}) async-start(), calls=%async_computation.17 | async-start | bytes 5898240 | tf_op jit(solution)/shard_map/all_gather | solution.py:305
  85.5 195.2 %all-gather.30.cloned.1.call-start = ((), (), s32[]{:S(2)}) async-start(), calls=%async_computation.18 | async-start | bytes 5898240 | tf_op jit(solution)/shard_map/all_gather | solution.py:308
  86.1 315.3 %all-gather.32.cloned.1.call-start = ((), (), s32[]{:S(2)}) async-start(), calls=%async_computation.19 | async-start | bytes 15728640 | tf_op jit(solution)/shard_map/all_gather | solution.py:310
  86.9 435.8 %all-gather.34.cloned.1.call-start = ((), (), s32[]{:S(2)}) async-start(), calls=%async_computation.20 | async-start | bytes 15728640 | tf_op jit(solution)/shard_map/all_gather | solution.py:311
  87.6 556.3 %all-gather.36.cloned.1.call-start = ((), (), s32[]{:S(2)}) async-start(), calls=%async_computation.21 | async-start | bytes 15728640 | tf_op jit(solution)/shard_map/all_gather | solution.py:312
  88.4 617.1 %all-gather.40.cloned.1.call-start = ((), (), s32[]{:S(2)}) async-start(), calls=%async_computation.23 | async-start | bytes 1671168 | tf_op jit(solution)/shard_map/all_gather | solution.py:112
  241.6 166.7 %copy-start.101 = (bf16[8,96,2,64]{1,3,2,0:T(8,128)(2,1)}, bf16[8,96,2,64]{1,3,2,0:T(8,128)(2,1)S(1)}, u32[]{:S(2)}) copy-start(bf16[8,96,2,64]{1,3,2,0:T(8,128)(2,1)S(1)} %fusion.194) | copy-start | bytes 589828
  284.1 359.8 %copy-start.51 = (f32[64,1536]{1,0:T(8,128)}, f32[64,1536]{1,0:T(8,128)S(1)}, u32[]{:S(2)}) copy-start(f32[64,1536]{1,0:T(8,128)S(1)} %get-tuple-element.144) | copy-start | bytes 1179652
  284.2 238.5 %copy-start.24 = (bf16[64,1536]{1,0:T(8,128)(2,1)}, bf16[64,1536]{1,0:T(8,128)(2,1)S(1)}, u32[]{:S(2)}) copy-start(bf16[64,1536]{1,0:T(8,128)(2,1)S(1)} %multiply_convert_fusion.8) | copy-start | bytes 589828
  408.3 122.2 %copy-start.41 = (f32[64,4096]{1,0:T(8,128)}, f32[64,4096]{1,0:T(8,128)S(1)}, u32[]{:S(2)}) copy-start(f32[64,4096]{1,0:T(8,128)S(1)} %fusion.34) | copy-start | bytes 3145732
  530.5 113.4 %copy-start.26 = (bf16[64,4096]{1,0:T(8,128)(2,1)}, bf16[64,4096]{1,0:T(8,128)(2,1)S(1)}, u32[]{:S(2)}) copy-start(bf16[64,4096]{1,0:T(8,128)(2,1)S(1)} %get-tuple-element.145) | copy-start | bytes 1572868
  650.8 3.1 collective-permute-start
  655.4 701.8 %copy-start.7 = (bf16[64,1536]{1,0:T(8,128)(2,1)}, bf16[64,1536]{1,0:T(8,128)(2,1)S(1)}, u32[]{:S(2)}) copy-start(bf16[64,1536]{1,0:T(8,128)(2,1)S(1)} %get-tuple-element.42) | copy-start | bytes 589828
  659.4 92.1 %all-gather.38.cloned.1.call-start = ((), (), s32[]{:S(2)}) async-start(), calls=%async_computation.22 | async-start | bytes 1671168 | tf_op jit(solution)/shard_map/all_gather | solution.py:113
  660.8 181.7 %all-gather.44.cloned.1.call-start = ((), (), s32[]{:S(2)}) async-start(), calls=%async_computation.25 | async-start | bytes 1671168 | tf_op jit(solution)/shard_map/all_gather | solution.py:112
  789.5 2.4 collective-permute-start.1
  791.9 565.4 %copy-start.9 = (bf16[64,1536]{1,0:T(8,128)(2,1)}, bf16[64,1536]{1,0:T(8,128)(2,1)S(1)}, u32[]{:S(2)}) copy-start(bf16[64,1536]{1,0:T(8,128)(2,1)S(1)} %collective-permute-done.1) | copy-start | bytes 589828
  799.0 89.6 %all-gather.42.cloned.1.call-start = ((), (), s32[]{:S(2)}) async-start(), calls=%async_computation.24 | async-start | bytes 1671168 | tf_op jit(solution)/shard_map/all_gather | solution.py:113
  800.2 222.0 %reduce-scatter.40.cloned.1.call-start = ((), (), s32[]{:S(2)}) async-start(), calls=%async_computation.38 | async-start | bytes 1671168
  904.3 82.0 %copy-start.19 = (bf16[64,1536]{1,0:T(8,128)(2,1)}, bf16[64,1536]{1,0:T(8,128)(2,1)S(1)}, u32[]{:S(2)}) copy-start(bf16[64,1536]{1,0:T(8,128)(2,1)S(1)} %get-tuple-element.89) | copy-start | bytes 589828
  949.2 149.2 %reduce-scatter.42.cloned.1.call-start = ((), (), s32[]{:S(2)}) async-start(), calls=%async_computation.39 | async-start | bytes 1671168
  961.4 256.7 %reduce-scatter.44.cloned.1.call-start = ((), (), s32[]{:S(2)}) async-start(), calls=%async_computation.40 | async-start | bytes 1671168
  1023.3 77.7 %copy-start.168 = (f32[64]{0:T(128)S(1)}, f32[64]{0:T(128)}, u32[]{:S(2)}) copy-start(f32[64]{0:T(128)} %get-tuple-element.40) | copy-start | bytes 772
  1023.4 77.7 %copy-start.58 = (f32[64,1536]{1,0:T(8,128)S(1)}, f32[64,1536]{1,0:T(8,128)}, u32[]{:S(2)}) copy-start(f32[64,1536]{1,0:T(8,128)} %copy-done.57) | copy-start | bytes 1179652
  1024.3 79.4 %copy-start.170 = (f32[64]{0:T(128)S(1)}, f32[64]{0:T(128)}, u32[]{:S(2)}) copy-start(f32[64]{0:T(128)} %get-tuple-element.87) | copy-start | bytes 772
  1024.3 77.9 %copy-start.91 = (bf16[64,8,96]{0,2,1:T(8,128)(2,1)}, bf16[64,8,96]{0,2,1:T(8,128)(2,1)S(1)}, u32[]{:S(2)}) copy-start(bf16[64,8,96]{0,2,1:T(8,128)(2,1)S(1)} %maximum_convert_fusion.3) | copy-start | bytes 294916
  1102.2 3.3 collective-permute-start.2
  1145.1 149.2 %reduce-scatter.46.cloned.1.call-start = ((), (), s32[]{:S(2)}) async-start(), calls=%async_computation.41 | async-start | bytes 1671168
  1152.4 376.7 %reduce-scatter.48.cloned.1.call-start = ((), (), s32[]{:S(2)}) async-start(), calls=%async_computation.42 | async-start | bytes 1671168
  1164.8 129.5 %copy-start.1 = (bf16[1,1536,768]{2,1,0:T(8,128)(2,1)S(1)}, bf16[1,1536,768]{2,1,0:T(8,128)(2,1)}, u32[]{:S(2)}) copy-start(bf16[1,1536,768]{2,1,0:T(8,128)(2,1)} %all-gather.20.cloned.1.call-done) | copy-start | bytes 7077892
  1219.9 77.0 %copy-start.166 = (f32[64]{0:T(128)S(1)}, f32[64]{0:T(128)}, u32[]{:S(2)}) copy-start(f32[64]{0:T(128)} %get-tuple-element.99) | copy-start | bytes 772
  1220.9 78.9 %copy-start.169 = (f32[64]{0:T(128)S(1)}, f32[64]{0:T(128)}, u32[]{:S(2)}) copy-start(f32[64]{0:T(128)} %get-tuple-element.85) | copy-start | bytes 772
  1298.1 3.3 collective-permute-start.3
  1340.8 203.5 %reduce-scatter.50.cloned.1.call-start = ((), (), s32[]{:S(2)}) async-start(), calls=%async_computation.43 | async-start | bytes 1671168
  1348.3 372.7 %reduce-scatter.26.cloned.1.call-start = ((), (), s32[]{:S(2)}) async-start(), calls=%async_computation.26 | async-start | bytes 9584640 | tf_op jit(solution)/shard_map/reduce_scatter | solution.py:361
  1366.2 584.4 %reduce-scatter.32.cloned.1.call-start = ((), (), s32[]{:S(2)}) async-start(), calls=%async_computation.30 | async-start | bytes 9584640 | tf_op jit(solution)/shard_map/reduce_scatter | solution.py:361
  1376.9 824.9 %reduce-scatter.34.cloned.1.call-start = ((), (), s32[]{:S(2)}) async-start(), calls=%async_computation.32 | async-start | bytes 25559040 | tf_op jit(solution)/shard_map/reduce_scatter | solution.py:361
  1425.3 1027.6 %reduce-scatter.36.cloned.1.call-start = ((), (), s32[]{:S(2)}) async-start(), calls=%async_computation.34 | async-start | bytes 25559040 | tf_op jit(solution)/shard_map/reduce_scatter | solution.py:361
  1473.4 1230.8 %reduce-scatter.38.cloned.1.call-start = ((), (), s32[]{:S(2)}) async-start(), calls=%async_computation.36 | async-start | bytes 25559040 | tf_op jit(solution)/shard_map/reduce_scatter | solution.py:361
  1521.8 1574.9 %reduce-scatter.28.cloned.1.call-start = ((), (), s32[]{:S(2)}) async-start(), calls=%async_computation.28 | async-start | bytes 4792320 | tf_op jit(solution)/shard_map/reduce_scatter | solution.py:361
  1537.3 1615.2 %reduce-scatter.30.cloned.1.call-start = ((), (), s32[]{:S(2)}) async-start(), calls=%async_computation.29 | async-start | bytes 4792320 | tf_op jit(solution)/shard_map/reduce_scatter | solution.py:361
  1551.3 903.4 %copy-start.173 = (u32[128]{0:T(128)S(1)}, u32[128]{0:T(128)}, u32[]{:S(2)}) copy-start(u32[128]{0:T(128)} %constant.88) | copy-start | bytes 1540
  1551.3 904.7 %copy-start.172 = (u32[128]{0:T(128)S(1)}, u32[128]{0:T(128)}, u32[]{:S(2)}) copy-start(u32[128]{0:T(128)} %constant.76) | copy-start | bytes 1540
  1551.3 905.9 %copy-start.164 = (f32[64]{0:T(128)S(1)}, f32[64]{0:T(128)}, u32[]{:S(2)}) copy-start(f32[64]{0:T(128)} %get-tuple-element.27) | copy-start | bytes 772
  1551.3 906.5 %copy-start.146 = (f32[1536]{0:T(1024)S(1)}, f32[1536]{0:T(1024)}, u32[]{:S(2)}) copy-start(f32[1536]{0:T(1024)} %get-tuple-element.13) | copy-start | bytes 18436
  1551.3 906.5 %copy-start.148 = (f32[1536]{0:T(1024)S(1)}, f32[1536]{0:T(1024)}, u32[]{:S(2)}) copy-start(f32[1536]{0:T(1024)} %get-tuple-element.11) | copy-start | bytes 18436
  1551.3 906.5 %copy-start.150 = (f32[1536]{0:T(1024)S(1)}, f32[1536]{0:T(1024)}, u32[]{:S(2)}) copy-start(f32[1536]{0:T(1024)} %get-tuple-element.15) | copy-start | bytes 18436
  1551.3 907.1 %copy-start.72 = (f32[64,1536]{1,0:T(8,128)S(1)}, f32[64,1536]{1,0:T(8,128)}, u32[]{:S(2)}) copy-start(f32[64,1536]{1,0:T(8,128)} %copy-done.71) | copy-start | bytes 1179652
  1551.3 1650.4 %all-gather.46.cloned.1.call-start = ((), (), s32[]{:S(2)}) async-start(), calls=%async_computation.27 | async-start | bytes 1253376 | tf_op jit(solution)/shard_map/all_gather | solution.py:364
  1722.5 1518.1 %all-gather.48.cloned.1.call-start = ((), (), s32[]{:S(2)}) async-start(), calls=%async_computation.31 | async-start | bytes 1253376 | tf_op jit(solution)/shard_map/all_gather | solution.py:364
  1952.1 1338.6 %all-gather.50.cloned.1.call-start = ((), (), s32[]{:S(2)}) async-start(), calls=%async_computation.33 | async-start | bytes 3342336 | tf_op jit(solution)/shard_map/all_gather | solution.py:364
  2203.6 1136.1 %all-gather.52.cloned.1.call-start = ((), (), s32[]{:S(2)}) async-start(), calls=%async_computation.35 | async-start | bytes 3342336 | tf_op jit(solution)/shard_map/all_gather | solution.py:364
  2454.6 934.1 %all-gather.54.cloned.1.call-start = ((), (), s32[]{:S(2)}) async-start(), calls=%async_computation.37 | async-start | bytes 3342336 | tf_op jit(solution)/shard_map/all_gather | solution.py:364
  2466.1 242.4 %copy-start.2 = (bf16[1,1536,768]{2,1,0:T(8,128)(2,1)S(1)}, bf16[1,1536,768]{2,1,0:T(8,128)(2,1)}, u32[]{:S(2)}) copy-start(bf16[1,1536,768]{2,1,0:T(8,128)(2,1)} %all-gather.20.cloned.1.call-done) | copy-start | bytes 7077892
  2466.1 242.4 %copy-start.95 = (bf16[64,1536]{1,0:T(8,128)(2,1)S(1)}, bf16[64,1536]{1,0:T(8,128)(2,1)}, u32[]{:S(2)}) copy-start(bf16[64,1536]{1,0:T(8,128)(2,1)} %get-tuple-element.28) | copy-start | bytes 589828
  2470.1 240.8 %copy-start.147 = (f32[1536]{0:T(1024)S(1)}, f32[1536]{0:T(1024)}, u32[]{:S(2)}) copy-start(f32[1536]{0:T(1024)} %get-tuple-element.19) | copy-start | bytes 18436
  2470.1 624.0 %copy-start.56 = (f32[64,1536]{1,0:T(8,128)S(1)}, f32[64,1536]{1,0:T(8,128)}, u32[]{:S(2)}) copy-start(f32[64,1536]{1,0:T(8,128)} %copy-done.54) | copy-start | bytes 1179652
  2708.5 386.4 %copy-start.115 = (bf16[64,1536]{1,0:T(8,128)(2,1)S(1)}, bf16[64,1536]{1,0:T(8,128)(2,1)}, u32[]{:S(2)}) copy-start(bf16[64,1536]{1,0:T(8,128)(2,1)} %copy-done.114) | copy-start | bytes 589828
  (157 other events, 1196.4 us)
Sparse Core Ops, SparseCore 0:
  9.7 35.4 all-gather.19
  46.8 33.0 all-gather.23
  82.6 44.1 all-gather.21
  129.4 43.3 all-gather.25
  174.3 51.8 all-gather.27
  227.6 53.0 all-gather.29
  282.4 119.0 all-gather.31
  403.1 119.5 all-gather.33
  524.3 119.5 all-gather.35
  659.6 45.9 all-gather.39
  708.2 43.3 all-gather.37
  799.1 43.3 all-gather.43
  845.2 43.3 all-gather.41
  949.3 72.9 reduce-scatter.39
  1025.4 72.9 reduce-scatter.41
  1145.2 72.9 reduce-scatter.43
  1221.2 73.0 reduce-scatter.45
  1340.9 73.0 reduce-scatter.47
  1417.3 72.8 reduce-scatter.49
  1494.6 226.2 reduce-scatter.25
  1726.2 224.3 reduce-scatter.31
  1955.3 246.5 reduce-scatter.33
  2206.6 246.3 reduce-scatter.35
  2457.5 246.6 reduce-scatter.37
  2709.2 219.1 reduce-scatter.27
  2933.3 219.1 reduce-scatter.29
  3155.1 41.4 all-gather.45
  3198.7 41.9 all-gather.47
  3243.4 47.3 all-gather.49
  3292.7 46.8 all-gather.51
  3341.8 46.8 all-gather.53
where the time goes:
time: 3410 us; the launch traced here: 3400 us
  waiting for transfers between devices  2260 us (66%)
  blocking collectives  472 us (14%)
  matrix products  465 us (14%)
  local copies, waits for them, and re-layouts  93.7 us (3%)
  other arithmetic  78.6 us (2%)
    reduce_scatter x7, waiting for transfers between devices, local(): lax.psum_scatter(totals, ('fsdp', 'ctx'), scatter_dimension=0, tiled=True)  1190 us
    unnamed x2, blocking collectives  381 us
    unnamed x37, waiting for transfers between devices  226 us
    dot_general x21, matrix products, matmul_tn(): lax.dot_general(left_side, right_side, (((0,), (0,)), ((), ())), preferre...  191 us
    all_gather x5, waiting for transfers between devices, local(): lax.all_gather(for_sending(grad_parts), 'ctx', axis=0, tiled=True)  170 us
    dot_general x21, matrix products, product_transposed(): lax.dot_general(left_side, right_side, (((1,), (1,)), ((), ())), preferre...  121 us
    all_gather x1, waiting for transfers between devices, local(): lax.all_gather(shards[6], 'fsdp', axis=1, tiled=True)  117 us
    all_gather x1, waiting for transfers between devices, local(): lax.all_gather(shards[7], 'fsdp', axis=1, tiled=True)  114 us
  transfers between devices with their start and end apart: 35, of which 30 were waited for; matrix products, arithmetic and copies ran while one was open for 12% of the time, Pallas kernels for 0%

commit v1 on v0

v1 whole, which is shorter than its diff:
```python
import jax
import jax.numpy as jnp
from jax import lax
from jax.experimental import pallas as pl
from jax.experimental.pallas import tpu as pltpu
from jax.sharding import PartitionSpec as P

QUERY_HEADS = 16
KEY_VALUE_HEADS = 8
HEAD_SIZE = 96
WIDTH = 1536
FF = 4096
THETA = 100000.0
EPSILON = 1e-05
MESH = pl.DeviceIdType.MESH
N_X = 4
N_C = 16
BF = jnp.bfloat16
F32 = jnp.float32


def mm(a, b):
    return jnp.dot(a, b, preferred_element_type=F32)


def mm_tn(a, b):
    return lax.dot_general(a, b, (((0,), (0,)), ((), ())), preferred_element_type=F32)


def mm_nt(a, b):
    return lax.dot_general(a, b, (((1,), (1,)), ((), ())), preferred_element_type=F32)


def exchange(arrays, outs, axis, n, stage, cid):
    count = len(arrays)

    def kernel(*refs):
        srcs, dsts = refs[:count], refs[count : 2 * count]
        send, recv, local_sem = refs[2 * count :]
        me = lax.axis_index(axis)

        def run():
            barrier = pltpu.get_barrier_semaphore()
            for k in range(1, n):
                pl.semaphore_signal(
                    barrier,
                    inc=1,
                    device_id={axis: lax.rem(me + k, n)},
                    device_id_type=MESH,
                )
            pl.semaphore_wait(barrier, n - 1)
            copies = []
            for k in range(1, n):
                peer = lax.rem(me + k, n)
                for i in range(count):
                    copy = pltpu.make_async_remote_copy(
                        src_ref=outs[i][1](srcs[i], peer),
                        dst_ref=outs[i][2](dsts[i], me),
                        send_sem=send.at[i, k - 1],
                        recv_sem=recv.at[i, k - 1],
                        device_id={axis: peer},
                        device_id_type=MESH,
                    )
                    copy.start()
                    copies.append(copy)
            for i in range(count):
                copy = pltpu.make_async_copy(
                    outs[i][1](srcs[i], me), outs[i][2](dsts[i], me), local_sem.at[i]
                )
                copy.start()
                copies.append(copy)
            for copy in copies:
                copy.wait()

        if stage is None:
            run()
        else:
            pl.when(lax.axis_index("section") == stage)(run)

    return pl.pallas_call(
        kernel,
        out_shape=[jax.ShapeDtypeStruct(o[0], a.dtype) for a, o in zip(arrays, outs)],
        in_specs=[pl.BlockSpec(memory_space=pl.ANY)] * count,
        out_specs=[pl.BlockSpec(memory_space=pl.ANY)] * count,
        scratch_shapes=[
            pltpu.SemaphoreType.DMA((count, n - 1)),
            pltpu.SemaphoreType.DMA((count, n - 1)),
            pltpu.SemaphoreType.DMA((count,)),
        ],
        compiler_params=pltpu.CompilerParams(collective_id=cid, has_side_effects=True),
    )(*arrays)


def slot(ref, index):
    return ref.at[index]


def gather_x(v, stage, cid):
    r = exchange([v], [((N_X,) + v.shape, lambda ref, p: ref, slot)], "fsdp", N_X, stage, cid)[0]
    return r.reshape((N_X * v.shape[0],) + v.shape[1:])


def reduce_x(partial, stage, cid):
    v = partial.astype(BF).reshape(N_X, -1, partial.shape[-1])
    r = exchange([v], [(v.shape, slot, slot)], "fsdp", N_X, stage, cid)[0]
    return jnp.sum(r.astype(F32), axis=0)


def swap_c(v, stage, cid):
    return exchange([v], [(v.shape, slot, slot)], "ctx", N_C, stage, cid)[0]


def hop(v, source, cid):
    def kernel(src, dst, send, recv):
        me = lax.axis_index("section")
        barrier = pltpu.get_barrier_semaphore()
        pl.semaphore_signal(barrier, inc=1, device_id={"section": 1 - me}, device_id_type=MESH)
        pl.semaphore_wait(barrier, 1)
        copy = pltpu.make_async_remote_copy(
            src_ref=src,
            dst_ref=dst,
            send_sem=send,
            recv_sem=recv,
            device_id={"section": 1 - me},
            device_id_type=MESH,
        )

        @pl.when(me == source)
        def _():
            copy.start()
            copy.wait_send()

        @pl.when(me != source)
        def _():
            copy.wait_recv()

    return pl.pallas_call(
        kernel,
        out_shape=jax.ShapeDtypeStruct(v.shape, v.dtype),
        in_specs=[pl.BlockSpec(memory_space=pl.ANY)],
        out_specs=pl.BlockSpec(memory_space=pl.ANY),
        scratch_shapes=[pltpu.SemaphoreType.DMA, pltpu.SemaphoreType.DMA],
        compiler_params=pltpu.CompilerParams(collective_id=cid, has_side_effects=True),
    )(v)


def rms(v, gain):
    return v * lax.rsqrt(jnp.mean(v * v, axis=-1, keepdims=True) + EPSILON) * gain


def rotate(u, table, sign):
    cosine, sine = (t[:, None, None, :] for t in table)
    sine = sine * sign
    rows, groups, _ = u.shape
    heads = u.reshape(rows, groups, 4, 96)
    a, b = heads[:, :, :3, :48], heads[:, :, :3, 48:]
    turned = jnp.concatenate([a * cosine - b * sine, b * cosine + a * sine], axis=-1)
    return jnp.concatenate([turned, heads[:, :, 3:]], axis=2).reshape(rows, groups, 384)


def local(
    inputs,
    positions,
    out_grad,
    norm_attn,
    w_query,
    key_weight,
    value_weight,
    output_weight,
    norm_mlp,
    w_gate,
    w_up,
    w_down,
):
    section = lax.axis_index("section")
    x_idx = lax.axis_index("fsdp")
    c_idx = lax.axis_index("ctx")
    is_first = section == 0

    pos8 = lax.all_gather(positions, "fsdp", axis=0, tiled=True)
    pos_all = lax.all_gather(pos8, "ctx", axis=1, tiled=True)
    pos_seq = lax.dynamic_index_in_dim(pos_all, c_idx // 2, 0, keepdims=False)
    freq = THETA ** (-(jnp.arange(48, dtype=F32) * 2.0 / 96))

    def table_of(p):
        ang = p.reshape(-1).astype(F32)[:, None] * freq[None, :]
        return jnp.cos(ang), jnp.sin(ang)

    table_c = table_of(pos8)
    table_s = table_of(pos_seq)
    gains = lax.all_gather(jnp.concatenate([norm_attn, norm_mlp], 0), "fsdp", axis=1, tiled=True)
    gain_attn, gain_mlp = gains[0].astype(F32), gains[1].astype(F32)

    wqkv_shard = jnp.concatenate(
        [
            w_query[0].reshape(384, 8, 192),
            key_weight[0].reshape(384, 8, 96),
            value_weight[0].reshape(384, 8, 96),
        ],
        axis=2,
    ).reshape(384, 4, 768)
    wqkv_shard = wqkv_shard.transpose(1, 0, 2)

    def cols(ref, p):
        return ref.at[:, pl.ds(pl.multiple_of(p * 1024, 1024), 1024)]

    def rows(ref, p):
        return ref.at[pl.ds(pl.multiple_of(p * 384, 384), 384)]

    wqkv, wg, wu = exchange(
        [wqkv_shard, w_gate[0], w_up[0]],
        [((1536, 768), slot, rows), ((1536, 1024), cols, rows), ((1536, 1024), cols, rows)],
        "fsdp",
        N_X,
        None,
        0,
    )
    wo = output_weight[0]
    wd = w_down[0]

    visible = pos_seq[:, None] >= pos_seq[None, :]
    scale = HEAD_SIZE ** (-0.5)

    def forward(stage, xin, base):
        x32 = xin.astype(F32)
        nf = gather_x(rms(x32, gain_attn).astype(BF), stage, base)
        u = mm(nf, wqkv).reshape(512, 2, 384)
        r = rotate(u, table_c, 1.0).astype(BF)
        send = r.reshape(8, 64, 2, 384).transpose(0, 2, 1, 3).reshape(16, 64, 384)
        qkv = swap_c(send, stage, base + 1).reshape(1024, 384)
        q = qkv[:, :192].reshape(1024, 2, 96)
        k = qkv[:, 192:288]
        v = qkv[:, 288:]
        scores = jnp.einsum("qgd,kd->gqk", q, k, preferred_element_type=F32) * scale
        scores = jnp.where(visible[None], scores, -1e30)
        top = jnp.max(scores, axis=-1, keepdims=True)
        e = jnp.exp(scores - top)
        total = jnp.sum(e, axis=-1, keepdims=True)
        probs = (e / total).astype(BF)
        lse = top + jnp.log(total)
        att = jnp.einsum("gqk,kd->qgd", probs, v, preferred_element_type=F32).astype(BF)
        att = swap_c(att.reshape(16, 64, 192), stage, base + 2)
        att = att.reshape(8, 2, 64, 192).transpose(0, 2, 1, 3).reshape(512, 384)
        mid = x32 + reduce_x(mm(att, wo), stage, base + 3)
        n2 = gather_x(rms(mid, gain_mlp).astype(BF), stage, base + 4)
        gate = mm(n2, wg)
        up = mm(n2, wu)
        hidden = (jax.nn.silu(gate) * up).astype(BF)
        out = (mid + reduce_x(mm(hidden, wd), stage, base + 5)).astype(BF)
        return out, (x32, nf, q, k, v, lse, att, mid, n2, gate, up, hidden)

    def backward(stage, dy, kept, base):
        x32, nf, q, k, v, lse, att, mid, n2, gate, up, hidden = kept
        dyf = gather_x(dy, stage, base)
        dhidden = mm_nt(dyf, wd)
        sig = jax.nn.sigmoid(gate)
        dgate = (dhidden * up * (sig * (1.0 + gate * (1.0 - sig)))).astype(BF)
        dup = (dhidden * (gate * sig)).astype(BF)
        dn2 = reduce_x(mm_nt(dgate, wg) + mm_nt(dup, wu), stage, base + 1)
        _, back_mlp = jax.vjp(rms, mid, gain_mlp)
        dmid, g_mlp = back_mlp(dn2)
        dmid = dmid + dy.astype(F32)
        dbr = gather_x(dmid.astype(BF), stage, base + 2)
        datt = mm_nt(dbr, wo).astype(BF)
        send = datt.reshape(8, 64, 2, 192).transpose(0, 2, 1, 3).reshape(16, 64, 192)
        da = swap_c(send, stage, base + 3).reshape(1024, 2, 96)
        scores = jnp.einsum("qgd,kd->gqk", q, k, preferred_element_type=F32) * scale
        probs = jnp.exp(jnp.where(visible[None], scores, -1e30) - lse)
        dprobs = jnp.einsum("qgd,kd->gqk", da, v, preferred_element_type=F32)
        dv = jnp.einsum("gqk,qgd->kd", probs.astype(BF), da, preferred_element_type=F32)
        dot = jnp.sum(probs * dprobs, axis=-1, keepdims=True)
        ds = (probs * (dprobs - dot)).astype(BF)
        dq = jnp.einsum("gqk,kd->qgd", ds, k, preferred_element_type=F32) * scale
        dk = jnp.einsum("gqk,qgd->kd", ds, q, preferred_element_type=F32) * scale
        dqkv = jnp.concatenate([dq.reshape(1024, 192), dk, dv], axis=1)
        dqkv = rotate(dqkv[:, None], table_s, -1.0).astype(BF).reshape(16, 64, 384)
        dqkv = swap_c(dqkv, stage, base + 4)
        dqkv = dqkv.reshape(8, 2, 64, 384).transpose(0, 2, 1, 3).reshape(512, 768)
        dn = reduce_x(mm_nt(dqkv, wqkv), stage, base + 5)
        _, back_attn = jax.vjp(rms, x32, gain_attn)
        dx, g_attn = back_attn(dn)
        dx = (dx + dmid).astype(BF)
        return dx, (g_attn, g_mlp, nf, dqkv, att, dbr, n2, dgate, dup, hidden, dyf)

    def choose(a, b):
        return jax.tree.map(lambda p, q: jnp.where(is_first, p, q), a, b)

    x_own = inputs.reshape(128, WIDTH)
    out0, kept0 = forward(0, x_own, 1)
    out1, kept1 = forward(1, hop(out0, 0, 7), 8)
    dx1, parts1 = backward(1, out_grad.reshape(128, WIDTH), kept1, 14)
    dx0, parts0 = backward(0, hop(dx1, 1, 20), kept0, 21)
    section_out = choose(out0, out1).reshape(1, 2, 64, WIDTH)
    section_grad = choose(dx0, dx1).reshape(1, 2, 64, WIDTH)
    g_attn, g_mlp, nf, dqkv, att, dbr, n2, dgate, dup, hidden, dyf = choose(parts0, parts1)

    wide = jnp.concatenate([mm_tn(n2, dgate), mm_tn(n2, dup), mm_tn(nf, dqkv)], axis=1).astype(BF)
    down = mm_tn(hidden, dyf).astype(BF)
    gout = mm_tn(att, dbr).astype(BF)
    wide = lax.psum_scatter(wide, "ctx", scatter_dimension=0, tiled=True)
    down = lax.psum_scatter(down, "ctx", scatter_dimension=0, tiled=True)
    gout = lax.psum_scatter(gout, "ctx", scatter_dimension=0, tiled=True)
    perm = [
        (x * 16 + c, (c // 4) * 16 + 4 * x + c % 4) for x in range(N_X) for c in range(N_C)
    ]
    wide = lax.ppermute(wide, ("fsdp", "ctx"), perm)
    wide = lax.all_gather(wide, "ctx", axis=0, tiled=True)
    down = lax.all_gather(down, "ctx", axis=0, tiled=True)
    gout = lax.all_gather(gout, "ctx", axis=0, tiled=True)
    wide = wide.reshape(4, 384, 2816).transpose(1, 0, 2).astype(F32)
    g_gate = wide[:, :, :1024].reshape(1, 384, FF)
    g_up = wide[:, :, 1024:2048].reshape(1, 384, FF)
    heads = wide[:, :, 2048:].reshape(384, 8, 384)
    g_query = heads[:, :, :192].reshape(1, 384, 1536)
    g_key = heads[:, :, 192:288].reshape(1, 384, 768)
    g_value = heads[:, :, 288:].reshape(1, 384, 768)
    g_gain = lax.psum(jnp.stack([g_attn, g_mlp]), ("fsdp", "ctx"))
    g_gain = lax.dynamic_slice_in_dim(g_gain, x_idx * 384, 384, 1)
    return (
        section_out,
        section_grad,
        g_gain[0:1],
        g_query,
        g_key,
        g_value,
        gout.astype(F32)[None],
        g_gain[1:2],
        g_gate,
        g_up,
        down.astype(F32)[None],
    )


def solution(mesh):
    rows = P("section", "fsdp", None)
    return jax.shard_map(
        local,
        mesh=mesh,
        in_specs=(
            P("fsdp", "ctx", None),
            P("fsdp", "ctx"),
            P("fsdp", "ctx", None),
            P("section", "fsdp"),
            rows,
            rows,
            rows,
            rows,
            P("section", "fsdp"),
            rows,
            rows,
            rows,
        ),
        out_specs=(
            P("section", "fsdp", "ctx", None),
            P("section", "fsdp", "ctx", None),
            P("section", "fsdp"),
            rows,
            rows,
            rows,
            rows,
            P("section", "fsdp"),
            rows,
            rows,
            rows,
        ),
        check_vma=False,
    )
```

time: 3410 us -> 1400 us (0.41)
  waiting for transfers between devices: 2260 us -> 153 us
  Pallas kernels: 0 us -> 432 us
  matrix products: 465 us -> 119 us
  local copies, waits for them, and re-layouts: 93.7 us -> 181 us
  blocking collectives: 472 us -> 391 us
    reduce_scatter x7 -> x2, waiting for transfers between devices: 1190 us -> 153 us  [the longest x1 88.1 us: local(): wide = lax.psum_scatter(wide, 'ctx', scatter_dimension=0, tiled=True)]
    all_gather x18 -> x3, waiting for transfers between devices: 849 us -> 0.01 us  [the longest x1 0.01 us: local(): gout = lax.all_gather(gout, 'ctx', axis=0, tiled=True)]
    pallas_call x0 -> x27, Pallas kernels: none -> 432 us  [the longest x25 287 us: exchange(): pl.pallas_call(kernel, out_shape=[jax.ShapeDtypeStruct(o[0], a.dtype) for...]
    unnamed x2 -> x0, blocking collectives: 381 us -> none
    dot_general x84 -> x37, matrix products: 465 us -> 119 us  [the longest x10 37.4 us: mm(): return jnp.dot(a, b, preferred_element_type=F32)]
    psum x0 -> x1, blocking collectives: none -> 345 us  [local(): g_gain = lax.psum(jnp.stack([g_attn, g_mlp]), ('fsdp', 'ctx'))]
    unnamed x37 -> x7, waiting for transfers between devices: 226 us -> 0.6 us
    slice x3 -> x16, local copies, waits for them, and re-layouts: 1.52 us -> 49.7 us  [the longest x2 18.7 us: local(): g_up = wide[:, :, 1024:2048].reshape(1, 384, FF)]
  transfers between devices with their start and end apart: 35 -> 7, of which waited for: 30 -> 2; matrix products, arithmetic and copies ran while one was open for 12% -> 7% of each run, Pallas kernels for 0% -> 5%
where the time goes in v1:
time: 1400 us; the launch traced here: 1390 us
  Pallas kernels  432 us (31%)
  blocking collectives  391 us (28%)
  local copies, waits for them, and re-layouts  181 us (13%)
  waiting for transfers between devices  153 us (11%)
  matrix products  119 us (8%)
  other arithmetic  95.8 us (7%)
  between operations  16.2 us (1%)
    psum x1, blocking collectives, local(): g_gain = lax.psum(jnp.stack([g_attn, g_mlp]), ('fsdp', 'ctx'))  345 us
    pallas_call x25, Pallas kernels, exchange(): pl.pallas_call(kernel, out_shape=[jax.ShapeDtypeStruct(o[0], a.dtype) for...  287 us
    pallas_call x2, Pallas kernels, hop(): pl.pallas_call(kernel, out_shape=jax.ShapeDtypeStruct(v.shape, v.dtype),...  145 us
    reduce_scatter x1, waiting for transfers between devices, local(): wide = lax.psum_scatter(wide, 'ctx', scatter_dimension=0, tiled=True)  88.1 us
    reduce_scatter x1, waiting for transfers between devices, local(): down = lax.psum_scatter(down, 'ctx', scatter_dimension=0, tiled=True)  64.5 us
    unnamed x206, local copies, waits for them, and re-layouts  53.9 us
    dot_general x10, matrix products, mm(): return jnp.dot(a, b, preferred_element_type=F32)  37.4 us
    dot_general x10, matrix products, mm_nt(): lax.dot_general(a, b, (((1,), (1,)), ((), ())), preferred_element_type=F32)  33.3 us
  transfers between devices with their start and end apart: 7, of which 2 were waited for; matrix products, arithmetic and copies ran while one was open for 7% of the time, Pallas kernels for 5%

profile of v1, /device:TPU:0, one launch (start us, length us, event | category | flops | bytes accessed | tf_op | source)
XLA Modules:
  0.0 1393.6 jit_solution(5849112256174863641)
XLA Ops:
  7.3 10.2 all-gather
  17.5 25.1 %all-gather.1 = s32[16,64,8]{1,2,0:T(8,128)S(1)} all-gather(s32[1,64,8]{1,2,0:T(8,128)S(1)} %bitcast.398), channel_id=1, replica_groups=mesh['section'=2,'fsdp'=4,'ctx'=16] {'ctx'}, dimensions={0}, use_global_device_ids=true | all-gather | bytes 34816 | tf_op jit(solution)/shard_map/all_gather | solution.py:181
  45.0 10.4 all_gather.18
  59.2 38.9 %shard_map.203 = bf16[4,128,1536]{2,1,0:T(8,128)(2,1)} custom-call(bf16[128,1536]{1,0:T(8,128)(2,1)} %fusion.77.refs_0_), custom_call_target="tpu_custom_call" | custom-call | tf_op jit(solution)/shard_map/pallas_call | solution.py:80
  104.8 3.3 pad_maximum_fusion.1
  108.0 4.3 copy.186
  112.3 70.5 %shard_map.204 = (bf16[1536,768]{1,0:T(8,128)(2,1)}, bf16[1536,1024]{1,0:T(8,128)(2,1)}, bf16[1536,1024]{1,0:T(8,128)(2,1)}) custom-call(bf16[4,384,768]{2,1,0:T(8,128)(2,1)} %bitcast.313, bf16[384,4096]{1,0:T(8,128)(2,1)} %bitcast.352, bf16[384,4096]{1,0:T(8,128)(2,1)} %bitcast.353), custom_call_target="tpu_custom_call" | custom-call | tf_op jit(solution)/shard_map/pallas_call | solution.py:80
  182.8 4.3 copy.187
  187.2 3.5 fusion.96
  200.0 12.0 shard_map.205
  215.1 3.5 fusion.94
  228.4 10.5 shard_map.206
  242.6 3.4 convolution_convert_fusion.7
  246.0 14.5 %shard_map.207 = bf16[4,128,1536]{2,1,0:T(8,128)(2,1)} custom-call(bf16[4,128,1536]{2,1,0:T(8,128)(2,1)} %bitcast.325), custom_call_target="tpu_custom_call" | custom-call | tf_op jit(solution)/shard_map/pallas_call | solution.py:80
  268.4 15.1 %shard_map.208 = bf16[4,128,1536]{2,1,0:T(8,128)(2,1)} custom-call(bf16[128,1536]{1,0:T(8,128)(2,1)} %multiply_convert_fusion.7.refs_0_), custom_call_target="tpu_custom_call" | custom-call | tf_op jit(solution)/shard_map/pallas_call | solution.py:80
  283.6 4.3 fusion.97
  287.9 3.2 multiply_convert_fusion.5
  294.1 14.9 %shard_map.209 = bf16[4,128,1536]{2,1,0:T(8,128)(2,1)} custom-call(bf16[4,128,1536]{2,1,0:T(8,128)(2,1)} %bitcast.378), custom_call_target="tpu_custom_call" | custom-call | tf_op jit(solution)/shard_map/pallas_call | solution.py:80
  317.7 3.6 fusion.98
  333.8 3.4 fusion.95
  340.5 3.4 fusion.49
  352.7 3.5 convolution_convert_fusion.6
  360.4 5.6 fusion.100
  366.1 3.1 fusion.99
  369.3 6.3 multiply_convert_fusion.2
  378.2 3.0 fusion.32
  385.7 3.5 convolution_convert_fusion.10
  397.8 5.5 fusion.3
  403.3 4.8 fusion.5
  431.0 143.5 %shard_map.223.refs_0_ = bf16[128,1536]{1,0:T(8,128)(2,1)} custom-call(bf16[128,1536]{1,0:T(8,128)(2,1)} %fusion.66.src), custom_call_target="tpu_custom_call" | custom-call | tf_op jit(solution)/shard_map/pallas_call | solution.py:137
  574.5 14.6 %shard_map.224 = bf16[4,128,1536]{2,1,0:T(8,128)(2,1)} custom-call(bf16[128,1536]{1,0:T(8,128)(2,1)} %shard_map.223.refs_0_), custom_call_target="tpu_custom_call" | custom-call | tf_op jit(solution)/shard_map/pallas_call | solution.py:80
  589.2 5.3 multiply_convert_fusion
  597.1 3.0 fusion.33
  600.1 15.1 %shard_map.225 = bf16[4,128,1536]{2,1,0:T(8,128)(2,1)} custom-call(bf16[4,128,1536]{2,1,0:T(8,128)(2,1)} %bitcast.373), custom_call_target="tpu_custom_call" | custom-call | tf_op jit(solution)/shard_map/pallas_call | solution.py:80
  623.7 14.5 %shard_map.226 = bf16[4,128,1536]{2,1,0:T(8,128)(2,1)} custom-call(bf16[128,1536]{1,0:T(8,128)(2,1)} %fusion.90.refs_0_), custom_call_target="tpu_custom_call" | custom-call | tf_op jit(solution)/shard_map/pallas_call | solution.py:80
  638.2 3.0 broadcast_select_fusion.4
  641.3 3.5 broadcast_select_fusion.1
  646.8 3.4 convolution_convert_fusion.8
  650.3 5.3 convolution_convert_fusion
  655.8 3.5 convolution_convert_fusion.9
  663.3 11.3 shard_map.227
  679.6 5.8 fusion
  700.2 12.3 shard_map.228
  721.8 4.2 pad_maximum_fusion
  726.0 11.7 copy.240
  738.3 64.5 %reduce-scatter.8.cloned.1.call-done = bf16[64,1536]{1,0:T(8,128)(2,1)} async-done(((bf16[1024,1536]{1,0:T(8,128)(2,1)}), bf16[64,1536]{1,0:T(8,128)(2,1)}) %reduce-scatter.8.cloned.1.call-update) | async-done | bytes 196624 | tf_op jit(solution)/shard_map/reduce_scatter | solution.py:301
  802.9 88.1 %reduce-scatter.10.cloned.1.call-done = bf16[96,2816]{1,0:T(8,128)(2,1)} async-done(((bf16[1536,2816]{1,0:T(8,128)(2,1)}), bf16[96,2816]{1,0:T(8,128)(2,1)}) %reduce-scatter.10.cloned.1.call-update) | async-done | bytes 540688 | tf_op jit(solution)/shard_map/reduce_scatter | solution.py:300
  891.0 5.8 collective-permute-start
  901.7 39.9 %shard_map.229 = bf16[4,128,1536]{2,1,0:T(8,128)(2,1)} custom-call(bf16[4,128,1536]{2,1,0:T(8,128)(2,1)} %bitcast.374), custom_call_target="tpu_custom_call" | custom-call | tf_op jit(solution)/shard_map/pallas_call | solution.py:80
  947.0 4.2 fusion.29
  952.6 345.4 %psum.7 = f32[2,1536]{1,0:T(2,128)} all-reduce(f32[2,1536]{1,0:T(2,128)} %pad_maximum_fusion.8), channel_id=1, replica_groups=mesh['section'=2,'fsdp'=4,'ctx'=16] {'fsdp','ctx'}, use_global_device_ids=true, to_apply=%region_26.27 | all-reduce | flops 3072 | bytes 24576 | tf_op jit(solution)/shard_map/psum | solution.py:317
  1301.4 3.0 fusion.78
  1304.4 3.0 bitcast_convert_fusion.1
  1307.3 5.5 bitcast_convert_fusion
  1312.8 10.9 convert_bitcast_fusion
  1323.7 12.1 fusion.91
  1335.8 4.8 slice.136
  1340.6 6.1 copy.222
  1346.7 3.5 slice.137
  1351.8 6.6 copy.223
  1358.3 6.6 copy.228
  1364.9 6.6 copy.224
  1371.4 6.6 copy.229
  1378.0 3.0 copy.225
  (356 shorter events, 193.7 us)
Async XLA Ops:
  7.2 284.0 %copy-start = (bf16[1,1024,1536]{2,1,0:T(8,128)(2,1)S(1)}, bf16[1,1024,1536]{2,1,0:T(8,128)(2,1)}, u32[]{:S(2)}) copy-start(bf16[1,1024,1536]{2,1,0:T(8,128)(2,1)} %param.23) | copy-start | bytes 9437188
  7.2 730.5 %reduce-scatter.12.cloned.1.call-start = ((), (), s32[]{:S(2)}) async-start(), calls=%async_computation.8 | async-start | bytes 1253376
  7.3 183.5 %copy-start.61 = (f32[48]{0:T(128)}, f32[48]{0:T(128)S(1)}, u32[]{:S(2)}) copy-start(f32[48]{0:T(128)S(1)} %negate_power_fusion) | copy-start | bytes 580
  42.7 2.3 copy-start.46
  57.3 43.2 %copy-start.79 = (f32[128]{0:T(128)}, f32[128]{0:T(128)S(1)}, u32[]{:S(2)}) copy-start(f32[128]{0:T(128)S(1)} %add.147) | copy-start | bytes 1540
  57.3 43.2 %copy-start.67 = (f32[128]{0:T(128)}, f32[128]{0:T(128)S(1)}, u32[]{:S(2)}) copy-start(f32[128]{0:T(128)S(1)} %rsqrt.50) | copy-start | bytes 1540
  215.1 3.5 copy-start.34
  218.6 3.3 copy-start.1
  218.7 3.3 copy-start.50
  246.0 17.2 %copy-start.8 = (bf16[2,64,1536]{2,1,0:T(8,128)(2,1)S(1)}, bf16[2,64,1536]{2,1,0:T(8,128)(2,1)}, u32[]{:S(2)}) copy-start(bf16[2,64,1536]{2,1,0:T(8,128)(2,1)} %param.12) | copy-start | bytes 1179652
  283.6 4.3 copy-start.37
  283.6 4.3 copy-start.73
  287.9 3.2 copy-start.82
  291.1 2.9 copy-start.91
  317.6 3.6 copy-start.42
  317.7 3.6 copy-start.44
  337.2 3.2 copy-start.2
  360.4 5.6 copy-start.39
  360.4 5.6 copy-start.76
  369.3 6.3 copy-start.77
  375.6 2.6 copy-start.74
  381.3 2.7 copy-start.72
  381.3 3.3 copy-start.23
  397.8 5.5 copy-start.45
  397.8 13.8 slice-start.2
  403.3 8.3 slice-start.3
  408.1 2.0 copy-start.36
  421.0 2.2 copy-start.27
  426.2 2.0 copy-start.18
  426.3 3.4 copy-start.70
  426.3 3.4 copy-start.11
  426.3 3.4 copy-start.21
  426.3 3.4 copy-start.24
  426.3 3.4 copy-start.54
  426.3 3.4 copy-start.58
  426.3 3.4 copy-start.66
  589.2 5.3 copy-start.78
  594.5 2.6 copy-start.75
  615.3 2.7 copy-start.5
  638.2 3.0 copy-start.22
  650.2 152.6 %reduce-scatter.8.cloned.1.call-start = ((), (), s32[]{:S(2)}) async-start(), calls=%async_computation.5 | async-start | bytes 3342336 | tf_op jit(solution)/shard_map/reduce_scatter | solution.py:301
  655.6 235.4 %reduce-scatter.10.cloned.1.call-start = ((), (), s32[]{:S(2)}) async-start(), calls=%async_computation.7 | async-start | bytes 9191424 | tf_op jit(solution)/shard_map/reduce_scatter | solution.py:300
  678.7 6.7 slice-start
  679.6 5.8 slice-start.1
  685.4 2.5 copy-start.35
  689.4 2.0 copy-start.25
  712.5 3.0 copy-start.33
  715.5 2.2 copy-start.86
  715.5 2.5 copy-start.90
  737.7 566.7 %all-gather.8.cloned.1.call-start = ((), (), s32[]{:S(2)}) async-start(), calls=%async_computation.4 | async-start | bytes 1253376 | tf_op jit(solution)/shard_map/all_gather | solution.py:309
  738.2 569.1 %all-gather.10.cloned.1.call-start = ((), (), s32[]{:S(2)}) async-start(), calls=%async_computation.6 | async-start | bytes 3342336 | tf_op jit(solution)/shard_map/all_gather | solution.py:308
  802.8 510.0 %all-gather.6.cloned.1.call-start = ((), (), s32[]{:S(2)}) async-start(), calls=%async_computation.3 | async-start | bytes 9191424 | tf_op jit(solution)/shard_map/all_gather | solution.py:307
  891.0 5.8 collective-permute-start
  896.9 2.2 copy-start.28
  941.6 1.9 copy-start.6
  1298.0 3.3 copy-start.80
  1298.0 3.3 copy-start.81
  1298.0 3.3 copy-start.7
  1298.0 3.3 copy-start.12
  1298.0 3.3 copy-start.15
  1298.0 3.3 copy-start.56
  1298.0 3.3 copy-start.64
  1298.0 3.3 copy-start.68
  1346.7 3.5 copy-start.16
  (39 other events, 47.9 us)
Sparse Core Ops, SparseCore 0:
  650.3 73.4 reduce-scatter.11
  727.7 75.0 reduce-scatter.7
  806.2 84.7 reduce-scatter.9
  893.2 53.5 all-gather.7
  949.0 47.5 all-gather.9
  998.9 71.5 all-gather.5

commit v2 on v1

--- a/solution.py
+++ b/solution.py
@@ -158,6 +158,354 @@
     return jnp.concatenate([turned, heads[:, :, 3:]], axis=2).reshape(rows, groups, 384)
 
 
+def remote(src, dst, send, recv, device):
+    return pltpu.make_async_remote_copy(
+        src_ref=src, dst_ref=dst, send_sem=send, recv_sem=recv, device_id=device, device_id_type=MESH
+    )
+
+
+def part(start, size):
+    return pl.ds(pl.multiple_of(start, size), size)
+
+
+GRADS = {"gate": (96, 1024), "up": (96, 1024), "down": (64, 1536), "qkv": (96, 768), "out": (96, 384)}
+RINGS = {"gate": ("y", 1), "up": ("y", -1), "down": ("z", 1), "qkv": ("z", -1), "out": ("z", -1)}
+
+
+def grad_kernel(n2, nf, dgu, dqkv, att, dbr, hidden, dyf, gains, *refs):
+    names = list(GRADS)
+    held = dict(zip(names, refs[:5]))
+    o_gain = refs[5]
+    own = dict(zip(names, refs[6:11]))
+    first = dict(zip(names, refs[11:16]))
+    second = dict(zip(names, refs[16:21]))
+    gain_in, send, recv, local_sem, send_g, recv_g = refs[21:]
+    x = lax.axis_index("fsdp")
+    c = lax.axis_index("ctx")
+    y, z = lax.rem(c, 4), c // 4
+    where = {"x": x, "y": y, "z": z}
+
+    def near(axis, step):
+        if axis == "x":
+            return {"fsdp": lax.rem(x + step + 4, 4)}
+        if axis == "y":
+            return {"ctx": 4 * z + lax.rem(y + step + 4, 4)}
+        return {"ctx": 4 * lax.rem(z + step + 4, 4) + y}
+
+    mirror = {"y": {"fsdp": y, "ctx": 4 * z + x}, "z": {"fsdp": z, "ctx": 4 * x + y}}
+
+    barrier = pltpu.get_barrier_semaphore()
+    for axis in "xyz":
+        for step in (1, 2, 3):
+            pl.semaphore_signal(barrier, inc=1, device_id=near(axis, step), device_id_type=MESH)
+    for axis in "yz":
+        pl.semaphore_signal(barrier, inc=1, device_id=mirror[axis], device_id_type=MESH)
+    pl.semaphore_wait(barrier, 11)
+
+    def ring(name):
+        axis, d = RINGS[name]
+        other = "z" if axis == "y" else "y"
+        return names.index(name), axis, other, d, where[axis], where[other]
+
+    def at(i, d, s):
+        return lax.rem(i - d * s + 8, 4)
+
+    def copy_first(name, s, q):
+        f, axis, other, d, i, j = ring(name)
+        p = at(j, d, 1 + q)
+        return remote(
+            own[name].at[at(i, d, 1 + s), p],
+            first[name].at[s, p],
+            send.at[f, 4 * s + q],
+            recv.at[f, 4 * s + q],
+            near(axis, d),
+        )
+
+    def copy_second(name, s):
+        f, axis, other, d, i, j = ring(name)
+        return remote(
+            own[name].at[i, at(j, d, 1 + s)],
+            second[name].at[s],
+            send.at[f, 12 + s],
+            recv.at[f, 12 + s],
+            near(other, d),
+        )
+
+    def copy_mirror(name):
+        f, axis, other, d, i, j = ring(name)
+        return remote(
+            own[name].at[i, j], held[name].at[x, j], send.at[f, 15], recv.at[f, 15], mirror[axis]
+        )
+
+    def copy_own(name):
+        f, axis, other, d, i, j = ring(name)
+        group = x if name in ("gate", "up", "qkv") else i
+        return pltpu.make_async_copy(own[name].at[i, j], held[name].at[group, j], local_sem.at[f])
+
+    def copy_small(name, s):
+        f, axis, other, d, i, j = ring(name)
+        place = held[name].at[i, at(j, d, s)]
+        return remote(place, place, send.at[f, 16 + s], recv.at[f, 16 + s], near(other, d))
+
+    def copy_big(name, s, q):
+        f, axis, other, d, i, j = ring(name)
+        place = held[name].at[at(i, d, s), at(j, d, q)]
+        n = 20 + 4 * s + q
+        return remote(place, place, send.at[f, n], recv.at[f, n], near(axis, d))
+
+    def gain_copy(n, k):
+        axis = "xyz"[n]
+        if n == 0:
+            src = gains.at[:, part(lax.rem(x + k, 4) * 384, 384)]
+        else:
+            src = gain_in.at[n, 0]
+        return remote(src, gain_in.at[n, k], send_g.at[n, k], recv_g.at[n, k], near(axis, k))
+
+    def gain_start(n):
+        for k in (1, 2, 3):
+            gain_copy(n, k).start()
+
+    def gain_sum(n):
+        mine = gains[:, part(x * 384, 384)] if n == 0 else gain_in[n, 0]
+        for k in (1, 2, 3):
+            gain_copy(n, k).wait()
+        return mine + gain_in[n, 1] + gain_in[n, 2] + gain_in[n, 3]
+
+    gain_start(0)
+
+    total = mm_tn(att[...], dbr[...]).astype(BF)
+    for g in range(4):
+        for p in range(4):
+            own["out"][g, p] = total[96 * g : 96 * g + 96, 384 * p : 384 * p + 384]
+
+    def compute(s, carry):
+        def group(name):
+            f, axis, other, d, i, j = ring(name)
+            return at(i, d, 1 + s)
+
+        g = group("gate")
+        own["gate"][g] = mm_tn(n2[:, part(g * 384, 384)], dgu[:, :1024]).astype(BF).reshape(4, 96, 1024)
+        g = group("up")
+        own["up"][g] = mm_tn(n2[:, part(g * 384, 384)], dgu[:, 1024:]).astype(BF).reshape(4, 96, 1024)
+        g = group("down")
+        own["down"][g] = mm_tn(hidden[:, part(g * 256, 256)], dyf[...]).astype(BF).reshape(4, 64, 1536)
+        g = group("qkv")
+        own["qkv"][g] = mm_tn(nf[:, part(g * 384, 384)], dqkv[...]).astype(BF).reshape(4, 96, 768)
+
+        @pl.when(s == 0)
+        def _():
+            for q in range(4):
+                for name in names:
+                    copy_first(name, 0, q).start()
+
+        return carry
+
+    lax.fori_loop(0, 4, compute, 0)
+    gain_in[1, 0] = gain_sum(0)
+    gain_start(1)
+
+    def add_first(t, carry):
+        s, q = t // 4, lax.rem(t, 4)
+        for name in names:
+            f, axis, other, d, i, j = ring(name)
+            copy_first(name, s, q).wait_recv()
+            g, p = at(i, d, 2 + s), at(j, d, 1 + q)
+            own[name][g, p] = own[name][g, p] + first[name][s, p]
+
+            @pl.when(s < 2)
+            def _(name=name):
+                copy_first(name, s + 1, q).start()
+
+            @pl.when(t == 8)
+            def _(name=name):
+                copy_second(name, 0).start()
+
+        return carry
+
+    lax.fori_loop(0, 12, add_first, 0)
+    gain_in[2, 0] = gain_sum(1)
+    gain_start(2)
+
+    def add_second(s, carry):
+        for name in names:
+            f, axis, other, d, i, j = ring(name)
+            copy_second(name, s).wait_recv()
+            p = at(j, d, 2 + s)
+            own[name][i, p] = own[name][i, p] + second[name][s]
+
+            @pl.when(s < 2)
+            def _(name=name):
+                copy_second(name, s + 1).start()
+
+        return carry
+
+    lax.fori_loop(0, 3, add_second, 0)
+
+    for name in ("gate", "up", "qkv"):
+        axis = RINGS[name][0]
+
+        @pl.when(where[axis] != x)
+        def _(name=name):
+            copy_mirror(name).start()
+
+        @pl.when(where[axis] == x)
+        def _(name=name):
+            copy_own(name).start()
+
+    for name in ("down", "out"):
+        copy_own(name).start()
+    for name in ("down", "out"):
+        copy_own(name).wait()
+    for name in ("gate", "up", "qkv"):
+        axis = RINGS[name][0]
+
+        @pl.when(where[axis] != x)
+        def _(name=name):
+            copy_mirror(name).wait()
+
+        @pl.when(where[axis] == x)
+        def _(name=name):
+            copy_own(name).wait()
+
+    def hand_small(q, carry):
+        for name in names:
+
+            @pl.when(q > 0)
+            def _(name=name):
+                copy_small(name, q - 1).wait_recv()
+
+            @pl.when(q < 3)
+            def _(name=name):
+                copy_small(name, q).start()
+
+            copy_big(name, 0, q).start()
+        return carry
+
+    lax.fori_loop(0, 4, hand_small, 0)
+
+    def hand_big(t, carry):
+        s, q = t // 4, lax.rem(t, 4)
+        for name in names:
+            copy_big(name, s, q).wait_recv()
+
+            @pl.when(s < 2)
+            def _(name=name):
+                copy_big(name, s + 1, q).start()
+
+        return carry
+
+    lax.fori_loop(0, 12, hand_big, 0)
+    o_gain[...] = gain_sum(2)
+
+    def sent(t, carry):
+        s, q = t // 4, lax.rem(t, 4)
+        for name in names:
+            copy_first(name, s, q).wait_send()
+            copy_big(name, s, q).wait_send()
+        return carry
+
+    lax.fori_loop(0, 12, sent, 0)
+
+    def sent_small(s, carry):
+        for name in names:
+            copy_second(name, s).wait_send()
+            copy_small(name, s).wait_send()
+        return carry
+
+    lax.fori_loop(0, 3, sent_small, 0)
+
+
+def reduce_grads(n2, nf, dgu, dqkv, att, dbr, hidden, dyf, gains, cid):
+    vm = pl.BlockSpec(memory_space=pltpu.VMEM)
+    hbm = pl.BlockSpec(memory_space=pl.ANY)
+    dma = pltpu.SemaphoreType.DMA
+    sizes = list(GRADS.values())
+    return pl.pallas_call(
+        grad_kernel,
+        out_shape=[jax.ShapeDtypeStruct((4, 4) + s, BF) for s in sizes]
+        + [jax.ShapeDtypeStruct((8, 384), F32)],
+        in_specs=[vm] * 9,
+        out_specs=[hbm] * 5 + [vm],
+        scratch_shapes=[pltpu.VMEM((4, 4) + s, BF) for s in sizes]
+        + [pltpu.VMEM((3, 4) + s, BF) for s in sizes]
+        + [pltpu.VMEM((3,) + s, BF) for s in sizes]
+        + [
+            pltpu.VMEM((3, 4, 8, 384), F32),
+            dma((5, 32)),
+            dma((5, 32)),
+            dma((5,)),
+            dma((3, 4)),
+            dma((3, 4)),
+        ],
+        name="reduce_grads",
+        compiler_params=pltpu.CompilerParams(
+            collective_id=cid, has_side_effects=True, vmem_limit_bytes=60 << 20
+        ),
+    )(n2, nf, dgu, dqkv, att, dbr, hidden, dyf, gains)
+
+
+def widen_kernel(w_gate, w_up, w_down, w_qkv, w_out, gate, up, query, key, value, g_out, g_down):
+    g_down[...] = w_down[...].astype(F32)
+    keys, values = [], []
+    for x in range(N_X):
+        gate[:, 1024 * x : 1024 * x + 1024] = w_gate[x, 0].astype(F32)
+        up[:, 1024 * x : 1024 * x + 1024] = w_up[x, 0].astype(F32)
+        g_out[:, 384 * x : 384 * x + 384] = w_out[0, x].astype(F32)
+        heads = w_qkv[x, 0].astype(F32)
+        query[:, 384 * x : 384 * x + 384] = jnp.concatenate(
+            [heads[:, :192], heads[:, 384:576]], axis=1
+        )
+        keys += [heads[:, 192:288], heads[:, 576:672]]
+        values += [heads[:, 288:384], heads[:, 672:768]]
+    key[...] = jnp.concatenate(keys, axis=1)
+    value[...] = jnp.concatenate(values, axis=1)
+
+
+def widen(gate, up, down, qkv, out):
+    steps = 8
+
+    def spec(r, cols):
+        return pl.BlockSpec((r, cols), lambda i: (i, 0))
+
+    def shape(r, cols):
+        return jax.ShapeDtypeStruct((r, cols), F32)
+
+    def blocks(cols):
+        return pl.BlockSpec((4, 1, 48, cols), lambda i: (0, i // 2, i % 2, 0))
+
+    return pl.pallas_call(
+        widen_kernel,
+        grid=(steps,),
+        out_shape=[
+            shape(384, FF),
+            shape(384, FF),
+            shape(384, 1536),
+            shape(384, 768),
+            shape(384, 768),
+            shape(384, 1536),
+            shape(1024, 1536),
+        ],
+        in_specs=[
+            blocks(1024),
+            blocks(1024),
+            spec(128, 1536),
+            blocks(768),
+            pl.BlockSpec((1, 4, 48, 384), lambda i: (i // 2, 0, i % 2, 0)),
+        ],
+        out_specs=[
+            spec(48, FF),
+            spec(48, FF),
+            spec(48, 1536),
+            spec(48, 768),
+            spec(48, 768),
+            spec(48, 1536),
+            spec(128, 1536),
+        ],
+        name="widen",
+        compiler_params=pltpu.CompilerParams(vmem_limit_bytes=60 << 20),
+    )(gate, up, down.reshape(1024, 1536), qkv, out)
+
+
 def local(
     inputs,
     positions,
@@ -294,40 +642,23 @@
     section_grad = choose(dx0, dx1).reshape(1, 2, 64, WIDTH)
     g_attn, g_mlp, nf, dqkv, att, dbr, n2, dgate, dup, hidden, dyf = choose(parts0, parts1)
 
-    wide = jnp.concatenate([mm_tn(n2, dgate), mm_tn(n2, dup), mm_tn(nf, dqkv)], axis=1).astype(BF)
-    down = mm_tn(hidden, dyf).astype(BF)
-    gout = mm_tn(att, dbr).astype(BF)
-    wide = lax.psum_scatter(wide, "ctx", scatter_dimension=0, tiled=True)
-    down = lax.psum_scatter(down, "ctx", scatter_dimension=0, tiled=True)
-    gout = lax.psum_scatter(gout, "ctx", scatter_dimension=0, tiled=True)
-    perm = [
-        (x * 16 + c, (c // 4) * 16 + 4 * x + c % 4) for x in range(N_X) for c in range(N_C)
-    ]
-    wide = lax.ppermute(wide, ("fsdp", "ctx"), perm)
-    wide = lax.all_gather(wide, "ctx", axis=0, tiled=True)
-    down = lax.all_gather(down, "ctx", axis=0, tiled=True)
-    gout = lax.all_gather(gout, "ctx", axis=0, tiled=True)
-    wide = wide.reshape(4, 384, 2816).transpose(1, 0, 2).astype(F32)
-    g_gate = wide[:, :, :1024].reshape(1, 384, FF)
-    g_up = wide[:, :, 1024:2048].reshape(1, 384, FF)
-    heads = wide[:, :, 2048:].reshape(384, 8, 384)
-    g_query = heads[:, :, :192].reshape(1, 384, 1536)
-    g_key = heads[:, :, 192:288].reshape(1, 384, 768)
-    g_value = heads[:, :, 288:].reshape(1, 384, 768)
-    g_gain = lax.psum(jnp.stack([g_attn, g_mlp]), ("fsdp", "ctx"))
-    g_gain = lax.dynamic_slice_in_dim(g_gain, x_idx * 384, 384, 1)
+    gains = jnp.concatenate([g_attn[None], g_mlp[None], jnp.zeros((6, WIDTH), F32)], axis=0)
+    *summed, g_gain = reduce_grads(
+        n2, nf, jnp.concatenate([dgate, dup], axis=1), dqkv, att, dbr, hidden, dyf, gains, 27
+    )
+    g_gate, g_up, g_query, g_key, g_value, g_out, g_down = widen(*summed)
     return (
         section_out,
         section_grad,
         g_gain[0:1],
-        g_query,
-        g_key,
-        g_value,
-        gout.astype(F32)[None],
+        g_query[None],
+        g_key[None],
+        g_value[None],
+        g_out[None],
         g_gain[1:2],
-        g_gate,
-        g_up,
-        down.astype(F32)[None],
+        g_gate[None],
+        g_up[None],
+        g_down[None],
     )
 
 

time: 1400 us -> 898 us (0.64)
  blocking collectives: 391 us -> 45.5 us
  waiting for transfers between devices: 153 us -> 0 us
  Pallas kernels: 432 us -> 555 us
  local copies, waits for them, and re-layouts: 181 us -> 101 us
  matrix products: 119 us -> 102 us
  other arithmetic: 95.8 us -> 79.4 us
    psum x1 -> x0, blocking collectives: 345 us -> none  [local(): g_gain = lax.psum(jnp.stack([g_attn, g_mlp]), ('fsdp', 'ctx'))]
    reduce_scatter x2 -> x0, waiting for transfers between devices: 153 us -> none  [the longest x1 88.1 us: local(): wide = lax.psum_scatter(wide, 'ctx', scatter_dimension=0, tiled=True)]
    pallas_call x0 -> x2, Pallas kernels: none -> 144 us  [the longest x1 129 us: reduce_grads(): pl.pallas_call(grad_kernel, out_shape=[jax.ShapeDtypeStruct((4, 4) + s, B...]
    slice x7 -> x0, local copies, waits for them, and re-layouts: 41.2 us -> none  [the longest x2 18.7 us: local(): g_up = wide[:, :, 1024:2048].reshape(1, 384, FF)]
    unnamed x206 -> x183, local copies, waits for them, and re-layouts: 53.9 us -> 17.9 us
    pallas_call x25, Pallas kernels: 287 us -> 267 us  [exchange(): pl.pallas_call(kernel, out_shape=[jax.ShapeDtypeStruct(o[0], a.dtype) for...]
  transfers between devices with their start and end apart: 7 -> 0, of which waited for: 2 -> 0; matrix products, arithmetic and copies ran while one was open for 7% -> 0% of each run, Pallas kernels for 5% -> 0%
where the time goes in v2:
time: 898 us; the launch traced here: 885 us
  Pallas kernels  555 us (62%)
  matrix products  102 us (11%)
  local copies, waits for them, and re-layouts  101 us (11%)
  other arithmetic  79.4 us (9%)
  blocking collectives  45.5 us (5%)
    pallas_call x25, Pallas kernels, exchange(): pl.pallas_call(kernel, out_shape=[jax.ShapeDtypeStruct(o[0], a.dtype) for...  267 us
    pallas_call x2, Pallas kernels, hop(): pl.pallas_call(kernel, out_shape=jax.ShapeDtypeStruct(v.shape, v.dtype),...  145 us
    pallas_call x1, Pallas kernels, reduce_grads(): pl.pallas_call(grad_kernel, out_shape=[jax.ShapeDtypeStruct((4, 4) + s, B...  129 us
    dot_general x10, matrix products, mm(): return jnp.dot(a, b, preferred_element_type=F32)  35 us
    dot_general x10, matrix products, mm_nt(): lax.dot_general(a, b, (((1,), (1,)), ((), ())), preferred_element_type=F32)  28.6 us
    all_gather x1, blocking collectives, local(): pos_all = lax.all_gather(pos8, 'ctx', axis=1, tiled=True)  25.1 us

profile of v2, /device:TPU:0, one launch (start us, length us, event | category | flops | bytes accessed | tf_op | source)
XLA Modules:
  0.0 885.5 jit_solution(1177335361692996611)
XLA Ops:
  4.1 10.0 %all-gather = s32[4,2,64]{2,1,0:T(2,128)S(1)} all-gather(s32[1,2,64]{2,1,0:T(2,128)} %bitcast.364), channel_id=1, replica_groups=mesh['section'=2,'fsdp'=4,'ctx'=16] {'fsdp'}, dimensions={0}, use_global_device_ids=true | all-gather | bytes 2560 | tf_op jit(solution)/shard_map/all_gather | solution.py:528
  14.3 10.4 %all_gather.9 = bf16[2,1536]{1,0:T(2,128)(2,1)S(1)} all-gather(bf16[2,384]{1,0:T(2,128)(2,1)S(1)} %pad_maximum_fusion.8), channel_id=1, replica_groups=mesh['section'=2,'fsdp'=4,'ctx'=16] {'fsdp'}, dimensions={1}, use_global_device_ids=true | all-gather | bytes 7680 | tf_op jit(solution)/shard_map/all_gather | solution.py:539
  24.7 25.1 %all-gather.1 = s32[16,64,8]{1,2,0:T(8,128)S(1)} all-gather(s32[1,64,8]{1,2,0:T(8,128)S(1)} %bitcast.363), channel_id=1, replica_groups=mesh['section'=2,'fsdp'=4,'ctx'=16] {'ctx'}, dimensions={0}, use_global_device_ids=true | all-gather | bytes 34816 | tf_op jit(solution)/shard_map/all_gather | solution.py:529
  60.3 21.6 %shard_map.203 = bf16[4,128,1536]{2,1,0:T(8,128)(2,1)} custom-call(bf16[128,1536]{1,0:T(8,128)(2,1)} %fusion.69.refs_0_), custom_call_target="tpu_custom_call" | custom-call | tf_op jit(solution)/shard_map/pallas_call | solution.py:80
  81.9 2.4 copy.92
  84.3 3.3 pad_maximum_fusion
  87.6 4.3 copy.95
  91.9 86.9 %shard_map.204 = (bf16[1536,768]{1,0:T(8,128)(2,1)}, bf16[1536,1024]{1,0:T(8,128)(2,1)}, bf16[1536,1024]{1,0:T(8,128)(2,1)}) custom-call(bf16[4,384,768]{2,1,0:T(8,128)(2,1)} %bitcast.291, bf16[384,4096]{1,0:T(8,128)(2,1)} %bitcast.328, bf16[384,4096]{1,0:T(8,128)(2,1)} %bitcast.329), custom_call_target="tpu_custom_call" | custom-call | tf_op jit(solution)/shard_map/pallas_call | solution.py:80
  178.8 4.3 copy.96
  183.1 3.6 fusion.86
  190.2 2.7 convert_element_type.206
  195.0 11.6 %shard_map.205 = bf16[16,64,384]{2,1,0:T(8,128)(2,1)} custom-call(bf16[16,64,384]{2,1,0:T(8,128)(2,1)} %bitcast.330), custom_call_target="tpu_custom_call" | custom-call | tf_op jit(solution)/shard_map/pallas_call | solution.py:80
  209.7 3.5 fusion.84
  216.5 2.6 fusion.46
  222.3 10.5 %shard_map.206 = bf16[16,64,192]{2,1,0:T(8,128)(2,1)} custom-call(bf16[16,64,192]{2,1,0:T(8,128)(2,1)} %reshape.499.refs_0_), custom_call_target="tpu_custom_call" | custom-call | tf_op jit(solution)/shard_map/pallas_call | solution.py:80
  232.8 2.4 copy.149
  236.6 3.5 convolution_convert_fusion.3
  240.1 15.0 %shard_map.207 = bf16[4,128,1536]{2,1,0:T(8,128)(2,1)} custom-call(bf16[4,128,1536]{2,1,0:T(8,128)(2,1)} %bitcast.305), custom_call_target="tpu_custom_call" | custom-call | tf_op jit(solution)/shard_map/pallas_call | solution.py:80
  263.0 14.7 %shard_map.208 = bf16[4,128,1536]{2,1,0:T(8,128)(2,1)} custom-call(bf16[128,1536]{1,0:T(8,128)(2,1)} %multiply_convert_fusion.7.refs_0_), custom_call_target="tpu_custom_call" | custom-call | tf_op jit(solution)/shard_map/pallas_call | solution.py:80
  277.7 4.3 fusion.87
  282.0 3.2 multiply_convert_fusion.5
  285.2 2.9 fusion.26
  288.1 15.2 %shard_map.209 = bf16[4,128,1536]{2,1,0:T(8,128)(2,1)} custom-call(bf16[4,128,1536]{2,1,0:T(8,128)(2,1)} %bitcast.356), custom_call_target="tpu_custom_call" | custom-call | tf_op jit(solution)/shard_map/pallas_call | solution.py:80
  312.1 3.6 fusion.88
  319.2 2.7 convert_element_type.219
  328.2 3.4 fusion.85
  334.9 3.4 fusion.47
  342.6 2.4 copy.148
  348.9 3.5 convolution_convert_fusion.2
  357.3 4.3 fusion.89
  361.6 3.1 broadcast_select_fusion.3
  364.8 3.8 multiply_convert_fusion.2
  368.5 2.9 fusion.29
  371.6 2.7 convert_reduce_fusion.4
  374.2 3.9 fusion.90
  378.2 3.0 fusion.32
  385.7 3.5 convolution_convert_fusion.5
  397.7 5.0 fusion.41
  402.7 5.3 fusion.3
  408.1 2.5 fusion.5
  415.1 2.3 copy.120
  417.4 2.7 convert_element_type.240.refs_0_
  422.7 2.6 convolution_convert_fusion.1
  430.2 143.0 %shard_map.223.refs_0_ = bf16[128,1536]{1,0:T(8,128)(2,1)} custom-call(bf16[128,1536]{1,0:T(8,128)(2,1)} %fusion.58.src), custom_call_target="tpu_custom_call" | custom-call | tf_op jit(solution)/shard_map/pallas_call | solution.py:137
  573.2 15.3 %shard_map.224 = bf16[4,128,1536]{2,1,0:T(8,128)(2,1)} custom-call(bf16[128,1536]{1,0:T(8,128)(2,1)} %shard_map.223.refs_0_), custom_call_target="tpu_custom_call" | custom-call | tf_op jit(solution)/shard_map/pallas_call | solution.py:80
  588.6 5.0 bitcast_select_fusion.2
  594.8 2.7 broadcast_select_fusion.4
  599.4 3.0 fusion.33
  603.8 14.7 %shard_map.225 = bf16[4,128,1536]{2,1,0:T(8,128)(2,1)} custom-call(bf16[4,128,1536]{2,1,0:T(8,128)(2,1)} %bitcast.352), custom_call_target="tpu_custom_call" | custom-call | tf_op jit(solution)/shard_map/pallas_call | solution.py:80
  624.5 2.5 fusion.82.refs_0_
  627.0 15.0 %shard_map.226 = bf16[4,128,1536]{2,1,0:T(8,128)(2,1)} custom-call(bf16[128,1536]{1,0:T(8,128)(2,1)} %fusion.82.refs_0_), custom_call_target="tpu_custom_call" | custom-call | tf_op jit(solution)/shard_map/pallas_call | solution.py:80
  642.0 4.9 broadcast_select_fusion.1
  652.7 11.4 %shard_map.227 = bf16[16,64,192]{2,1,0:T(8,128)(2,1)} custom-call(bf16[16,64,192]{2,1,0:T(8,128)(2,1)} %bitcast.347), custom_call_target="tpu_custom_call" | custom-call | tf_op jit(solution)/shard_map/pallas_call | solution.py:80
  668.2 5.0 fusion.38
  673.2 5.3 fusion
  678.6 2.5 fusion.2
  685.6 2.3 copy.128
  687.9 2.7 convert_element_type.253.refs_0_
  690.6 13.5 %shard_map.228 = bf16[16,64,384]{2,1,0:T(8,128)(2,1)} custom-call(bf16[16,64,384]{2,1,0:T(8,128)(2,1)} %convert_element_type.253.refs_0_), custom_call_target="tpu_custom_call" | custom-call | tf_op jit(solution)/shard_map/pallas_call | solution.py:80
  706.4 2.6 convolution_convert_fusion
  710.0 19.1 %shard_map.229 = bf16[4,128,1536]{2,1,0:T(8,128)(2,1)} custom-call(bf16[4,128,1536]{2,1,0:T(8,128)(2,1)} %bitcast.353), custom_call_target="tpu_custom_call" | custom-call | tf_op jit(solution)/shard_map/pallas_call | solution.py:80
  735.3 3.9 fusion.70
  739.9 129.5 %reduce_grads.1 = (bf16[4,4,96,1024]{3,2,1,0:T(8,128)(2,1)}, bf16[4,4,96,1024]{3,2,1,0:T(8,128)(2,1)}, bf16[4,4,64,1536]{3,2,1,0:T(8,128)(2,1)}, bf16[4,4,96,768...) custom-call(bf16[512,1536]{1,0:T(8,128)(2,1)} %get-tuple-element.96.n2, ...), custom_call_target="tpu_custom_call" | custom-call | tf_op jit(solution)/shard_map/reduce_grads/pallas_call | solution.py:423
  870.7 14.5 %widen.1 = (f32[384,4096]{1,0:T(8,128)}, f32[384,4096]{1,0:T(8,128)}, f32[384,1536]{1,0:T(8,128)}, f32[384,768]{1,0:T(8,128)}, f32[384,768]{1,0:T(8,128)}, /*index=5*/f32[384,1536]{1,0:T(8,128)}, f32[1024,1536]{1,0:T(8,128)}) custom-call(bf16[4,4,96,1024]{3,2,1,0:T(8,128)(2,1)} %get-tuple-element.31.w_gate, bf16[4,4,96,1024]{3,2,1,0:T(8,128)(2,1)} %get-tuple-element.32.w_up, ...), custom_call_target="tpu_custom_call" | custom-call | tf_op jit(solution)/shard_map/widen/pallas_call | solution.py:476
  (301 shorter events, 134.0 us)
Async XLA Ops:
  0.6 284.6 %copy-start = (bf16[1,1024,1536]{2,1,0:T(8,128)(2,1)S(1)}, bf16[1,1024,1536]{2,1,0:T(8,128)(2,1)}, u32[]{:S(2)}) copy-start(bf16[1,1024,1536]{2,1,0:T(8,128)(2,1)} %param.23) | copy-start | bytes 9437188
  3.4 10.8 %copy-start.74 = (f32[128]{0:T(128)}, f32[128]{0:T(128)S(1)}, u32[]{:S(2)}) copy-start(f32[128]{0:T(128)S(1)} %add.136) | copy-start | bytes 1540
  3.4 56.9 %copy-start.63 = (f32[128]{0:T(128)}, f32[128]{0:T(128)S(1)}, u32[]{:S(2)}) copy-start(f32[128]{0:T(128)S(1)} %rsqrt.50) | copy-start | bytes 1540
  51.0 135.7 %copy-start.42 = (f32[512,48]{0,1:T(8,128)}, f32[512,48]{0,1:T(8,128)S(1)}, u32[]{:S(2)}) copy-start(f32[512,48]{0,1:T(8,128)S(1)} %get-tuple-element.76) | copy-start | bytes 294916
  183.1 3.6 copy-start.44
  209.7 3.5 copy-start.39
  213.2 3.3 copy-start.1
  236.6 3.5 copy-start.26
  240.1 17.6 %copy-start.7 = (bf16[2,64,1536]{2,1,0:T(8,128)(2,1)S(1)}, bf16[2,64,1536]{2,1,0:T(8,128)(2,1)}, u32[]{:S(2)}) copy-start(bf16[2,64,1536]{2,1,0:T(8,128)(2,1)} %param.12) | copy-start | bytes 1179652
  277.6 4.3 copy-start.19
  277.7 4.3 copy-start.69
  282.0 3.2 copy-start.75
  285.2 2.9 copy-start.79
  312.0 3.6 copy-start.43
  312.1 3.6 copy-start.45
  331.6 3.3 copy-start.2
  357.3 4.3 copy-start.20
  357.3 4.3 copy-start.70
  357.3 4.3 copy-start.80
  361.6 3.1 copy-start.18
  371.6 2.7 copy-start.77
  374.2 3.9 copy-start.71
  374.2 3.9 copy-start.82
  381.2 2.7 copy-start.68
  381.3 3.3 copy-start.27
  397.7 5.0 copy-start.25
  397.7 5.0 copy-start.29
  397.7 5.0 copy-start.47
  397.7 10.4 %slice-start.2 = ((s8[8388608]{0:T(1024)(128)(4,1)}), s8[4194304]{0:T(1024)(128)(4,1)S(1)}, s32[]{:S(2)}) async-start(s8[8388608]{0:T(1024)(128)(4,1)} %bitcast.284), calls=%async_computation.2 | async-start | bytes 8388608
  402.7 5.3 slice-start.3
  408.1 2.5 copy-start.41
  420.5 2.2 copy-start.33
  422.7 2.6 copy-start.31
  425.4 2.0 copy-start.14
  425.4 3.5 copy-start.66
  425.4 3.5 copy-start.10
  425.4 3.5 copy-start.17
  425.4 3.5 copy-start.28
  425.4 3.5 copy-start.54
  425.4 3.5 copy-start.57
  425.4 3.5 copy-start.62
  588.5 5.1 copy-start.21
  588.5 5.1 copy-start.76
  588.5 5.1 copy-start.78
  588.6 6.0 copy-start.81
  588.6 6.2 copy-start.83
  594.8 2.7 copy-start.73
  618.5 2.7 copy-start.5
  642.0 5.0 copy-start.22
  642.0 5.0 copy-start.23
  668.2 5.0 copy-start.24
  668.2 5.0 copy-start.30
  668.2 5.0 copy-start.46
  668.2 10.4 %slice-start = ((s8[8388608]{0:T(1024)(128)(4,1)}), s8[4194304]{0:T(1024)(128)(4,1)S(1)}, s32[]{:S(2)}) async-start(s8[8388608]{0:T(1024)(128)(4,1)} %bitcast.282), calls=%async_computation | async-start | bytes 8388608
  673.2 5.4 slice-start.1
  678.6 2.5 copy-start.40
  704.2 2.2 copy-start.34
  706.4 2.6 copy-start.32
  729.1 1.9 copy-start.6
  729.2 1.9 copy-start.12
  729.2 1.9 copy-start.58
  735.2 3.9 copy-start.50
  735.2 3.9 copy-start.51
  735.2 3.9 copy-start.64
  (24 other events, 25.6 us)

commit v3 on v2

--- a/solution.py
+++ b/solution.py
@@ -29,133 +29,6 @@
 
 def mm_nt(a, b):
     return lax.dot_general(a, b, (((1,), (1,)), ((), ())), preferred_element_type=F32)
-
-
-def exchange(arrays, outs, axis, n, stage, cid):
-    count = len(arrays)
-
-    def kernel(*refs):
-        srcs, dsts = refs[:count], refs[count : 2 * count]
-        send, recv, local_sem = refs[2 * count :]
-        me = lax.axis_index(axis)
-
-        def run():
-            barrier = pltpu.get_barrier_semaphore()
-            for k in range(1, n):
-                pl.semaphore_signal(
-                    barrier,
-                    inc=1,
-                    device_id={axis: lax.rem(me + k, n)},
-                    device_id_type=MESH,
-                )
-            pl.semaphore_wait(barrier, n - 1)
-            copies = []
-            for k in range(1, n):
-                peer = lax.rem(me + k, n)
-                for i in range(count):
-                    copy = pltpu.make_async_remote_copy(
-                        src_ref=outs[i][1](srcs[i], peer),
-                        dst_ref=outs[i][2](dsts[i], me),
-                        send_sem=send.at[i, k - 1],
-                        recv_sem=recv.at[i, k - 1],
-                        device_id={axis: peer},
-                        device_id_type=MESH,
-                    )
-                    copy.start()
-                    copies.append(copy)
-            for i in range(count):
-                copy = pltpu.make_async_copy(
-                    outs[i][1](srcs[i], me), outs[i][2](dsts[i], me), local_sem.at[i]
-                )
-                copy.start()
-                copies.append(copy)
-            for copy in copies:
-                copy.wait()
-
-        if stage is None:
-            run()
-        else:
-            pl.when(lax.axis_index("section") == stage)(run)
-
-    return pl.pallas_call(
-        kernel,
-        out_shape=[jax.ShapeDtypeStruct(o[0], a.dtype) for a, o in zip(arrays, outs)],
-        in_specs=[pl.BlockSpec(memory_space=pl.ANY)] * count,
-        out_specs=[pl.BlockSpec(memory_space=pl.ANY)] * count,
-        scratch_shapes=[
-            pltpu.SemaphoreType.DMA((count, n - 1)),
-            pltpu.SemaphoreType.DMA((count, n - 1)),
-            pltpu.SemaphoreType.DMA((count,)),
-        ],
-        compiler_params=pltpu.CompilerParams(collective_id=cid, has_side_effects=True),
-    )(*arrays)
-
-
-def slot(ref, index):
-    return ref.at[index]
-
-
-def gather_x(v, stage, cid):
-    r = exchange([v], [((N_X,) + v.shape, lambda ref, p: ref, slot)], "fsdp", N_X, stage, cid)[0]
-    return r.reshape((N_X * v.shape[0],) + v.shape[1:])
-
-
-def reduce_x(partial, stage, cid):
-    v = partial.astype(BF).reshape(N_X, -1, partial.shape[-1])
-    r = exchange([v], [(v.shape, slot, slot)], "fsdp", N_X, stage, cid)[0]
-    return jnp.sum(r.astype(F32), axis=0)
-
-
-def swap_c(v, stage, cid):
-    return exchange([v], [(v.shape, slot, slot)], "ctx", N_C, stage, cid)[0]
-
-
-def hop(v, source, cid):
-    def kernel(src, dst, send, recv):
-        me = lax.axis_index("section")
-        barrier = pltpu.get_barrier_semaphore()
-        pl.semaphore_signal(barrier, inc=1, device_id={"section": 1 - me}, device_id_type=MESH)
-        pl.semaphore_wait(barrier, 1)
-        copy = pltpu.make_async_remote_copy(
-            src_ref=src,
-            dst_ref=dst,
-            send_sem=send,
-            recv_sem=recv,
-            device_id={"section": 1 - me},
-            device_id_type=MESH,
-        )
-
-        @pl.when(me == source)
-        def _():
-            copy.start()
-            copy.wait_send()
-
-        @pl.when(me != source)
-        def _():
-            copy.wait_recv()
-
-    return pl.pallas_call(
-        kernel,
-        out_shape=jax.ShapeDtypeStruct(v.shape, v.dtype),
-        in_specs=[pl.BlockSpec(memory_space=pl.ANY)],
-        out_specs=pl.BlockSpec(memory_space=pl.ANY),
-        scratch_shapes=[pltpu.SemaphoreType.DMA, pltpu.SemaphoreType.DMA],
-        compiler_params=pltpu.CompilerParams(collective_id=cid, has_side_effects=True),
-    )(v)
-
-
-def rms(v, gain):
-    return v * lax.rsqrt(jnp.mean(v * v, axis=-1, keepdims=True) + EPSILON) * gain
-
-
-def rotate(u, table, sign):
-    cosine, sine = (t[:, None, None, :] for t in table)
-    sine = sine * sign
-    rows, groups, _ = u.shape
-    heads = u.reshape(rows, groups, 4, 96)
-    a, b = heads[:, :, :3, :48], heads[:, :, :3, 48:]
-    turned = jnp.concatenate([a * cosine - b * sine, b * cosine + a * sine], axis=-1)
-    return jnp.concatenate([turned, heads[:, :, 3:]], axis=2).reshape(rows, groups, 384)
 
 
 def remote(src, dst, send, recv, device):
@@ -506,6 +379,709 @@
     )(gate, up, down.reshape(1024, 1536), qkv, out)
 
 
+X_GAIN, X_POS, X_IN, X_DY, X_QKV, X_GATE, X_UP, X_SUM1, X_N2, X_SUM2, X_SUM3, X_DBR, X_SUM4 = range(13)
+C_POS, C_QKV, C_ATT, C_DATT, C_DQKV = range(5)
+H_OUT, H_DX = range(2)
+SCALE = HEAD_SIZE ** (-0.5)
+
+
+def spread(w, heads):
+    blank = jnp.zeros((w.shape[0], 16), w.dtype)
+    pieces = []
+    for h in heads:
+        pieces += [w[:, 96 * h : 96 * h + 48], blank, w[:, 96 * h + 48 : 96 * h + 96], blank]
+    return pieces
+
+
+def as_column(row):
+    eye = lax.broadcasted_iota(jnp.int32, (128, 128), 0) == lax.broadcasted_iota(
+        jnp.int32, (128, 128), 1
+    )
+    return jnp.sum(jnp.where(eye, jnp.broadcast_to(row, (128, 128)), 0.0), axis=1, keepdims=True)
+
+
+def turn(u, cosine, sine):
+    return u * cosine + pltpu.roll(u, 64, 1) * sine
+
+
+def layer_kernel(
+    xin,
+    dyin,
+    pos,
+    freq,
+    gains,
+    wq,
+    wk,
+    wv,
+    wo,
+    wd,
+    wg,
+    wu,
+    out,
+    dx,
+    nf,
+    n2,
+    dgu,
+    dqkv,
+    att,
+    dbr,
+    hidden,
+    dyf,
+    ggain,
+    wsend,
+    wqkv,
+    wgf,
+    wuf,
+    wop,
+    xall,
+    gain,
+    posx,
+    posv,
+    posc,
+    posr,
+    posk,
+    cos_c,
+    sin_c,
+    cos_s,
+    sin_s,
+    qsend,
+    qs,
+    vt,
+    kt,
+    lse,
+    osend,
+    attp,
+    mid,
+    gate,
+    up,
+    own,
+    psend,
+    prec,
+    dsend,
+    das,
+    dk,
+    dv,
+    dqs,
+    dqp,
+    xs,
+    xr,
+    cs,
+    cr,
+    hs,
+    hr,
+):
+    section = lax.axis_index("section")
+    x = lax.axis_index("fsdp")
+    c = lax.axis_index("ctx")
+    first, second = section == 0, section == 1
+    my_rows = part(128 * x, 128)
+
+    barrier = pltpu.get_barrier_semaphore()
+    for k in range(1, 4):
+        pl.semaphore_signal(
+            barrier, inc=1, device_id={"fsdp": lax.rem(x + k, 4)}, device_id_type=MESH
+        )
+    for k in range(4):
+        pl.semaphore_signal(
+            barrier,
+            inc=1,
+            device_id={"section": 1 - section, "fsdp": lax.rem(x + k, 4)},
+            device_id_type=MESH,
+        )
+
+    def greet(k, carry):
+        pl.semaphore_signal(
+            barrier, inc=1, device_id={"ctx": lax.rem(c + k, 16)}, device_id_type=MESH
+        )
+        return carry
+
+    lax.fori_loop(1, 16, greet, 0)
+    pl.semaphore_wait(barrier, 22)
+
+    def ahead(k):
+        return lax.rem(x + k, 4)
+
+    def behind(k):
+        return lax.rem(x - k + 4, 4)
+
+    def over_x(e, k, src, dst):
+        return remote(src, dst, xs.at[e, k], xr.at[e, k], {"fsdp": ahead(k)})
+
+    def over_c(e, to, src, dst):
+        k = lax.rem(to - c + 16, 16)
+        return remote(src, dst, cs.at[e, k], cr.at[e, k], {"ctx": to})
+
+    def across(e, k, src, dst):
+        return remote(
+            src, dst, hs.at[e, k], hr.at[e, k], {"section": 1 - section, "fsdp": ahead(k)}
+        )
+
+    def rows_to_all(e, ref, k):
+        return over_x(e, k, ref.at[my_rows], ref.at[my_rows])
+
+    def sum_copy(e, k):
+        n = (X_SUM1, X_SUM2, X_SUM3, X_SUM4).index(e)
+        return over_x(e, k, psend.at[n % 2, ahead(k)], prec.at[n % 2, k])
+
+    def gain_copy(k):
+        place = gain.at[:, part(384 * x, 384)]
+        return over_x(X_GAIN, k, gains, place)
+
+    def pos_copy(k):
+        return over_x(X_POS, k, pos, posx.at[x])
+
+    def in_copy(k):
+        return over_x(X_IN, k, xin, xall.at[my_rows])
+
+    def dy_copy(k):
+        return over_x(X_DY, k, dyin, dyf.at[my_rows])
+
+    def qkv_copy(k):
+        return over_x(X_QKV, k, wsend.at[ahead(k)], wqkv.at[part(384 * x, 384)])
+
+    def wide_copy(e, k):
+        src, dst = (wg, wgf) if e == X_GATE else (wu, wuf)
+        return over_x(e, k, src.at[:, part(1024 * ahead(k), 1024)], dst.at[part(384 * x, 384)])
+
+    for k in (2, 1, 3):
+        pos_copy(k).start()
+        gain_copy(k).start()
+    gain[:, part(384 * x, 384)] = gains[...]
+    posx[x] = pos[...]
+
+    for b in range(4):
+        pieces = []
+        for j in range(2):
+            pieces += spread(wq[:, 384 * b + 192 * j : 384 * b + 192 * j + 192], (0, 1))
+            pieces += spread(wk[:, 96 * (2 * b + j) : 96 * (2 * b + j) + 96], (0,))
+            pieces += [
+                wv[:, 96 * (2 * b + j) : 96 * (2 * b + j) + 96],
+                jnp.zeros((384, 32), BF),
+            ]
+        wsend[b] = jnp.concatenate(pieces, axis=1)
+    for k in (2, 1, 3):
+        qkv_copy(k).start()
+    wqkv[part(384 * x, 384), :] = wsend[x]
+
+    @pl.when(first)
+    def _():
+        for k in (2, 1, 3):
+            in_copy(k).start()
+        xall[my_rows, :] = xin[...]
+
+    @pl.when(second)
+    def _():
+        for k in (2, 1, 3):
+            dy_copy(k).start()
+        dyf[my_rows, :] = dyin[...]
+
+    own_wide = [
+        pltpu.make_async_copy(
+            src.at[:, part(1024 * x, 1024)], dst.at[part(384 * x, 384)], xs.at[e, 0]
+        )
+        for e, src, dst in ((X_GATE, wg, wgf), (X_UP, wu, wuf))
+    ]
+    for copy in own_wide:
+        copy.start()
+
+    wop[...] = jnp.zeros_like(wop)
+    for h in range(4):
+        wop[128 * h : 128 * h + 96, :] = wo[96 * h : 96 * h + 96, :]
+
+    lane = lax.broadcasted_iota(jnp.int32, (1, 128), 1)
+    sign = jnp.where(lane < 64, -1.0, 1.0)
+    for k in (1, 3, 2):
+        pos_copy(k).wait()
+    for b in range(4):
+        block = posx[b]
+        posv[b, 0] = block
+        posv[b, 1] = pltpu.roll(block, 64, 1)
+
+    def pos_to(to):
+        return over_c(C_POS, to, posv.at[to // 4, lax.rem(to, 4) // 2], posc.at[c])
+
+    def send_pos(k, carry):
+        pos_to(lax.rem(c + k, 16)).start()
+        return carry
+
+    lax.fori_loop(1, 16, send_pos, 0)
+    posc[c] = posv[c // 4, lax.rem(c, 4) // 2]
+    for b in range(4):
+        angle = as_column(posx[b][0:1, :]) * freq[0:1, :]
+        cos_c[128 * b : 128 * b + 128, :] = jnp.cos(angle)
+        sin_c[128 * b : 128 * b + 128, :] = jnp.sin(angle) * sign
+
+    def await_pos(k, carry):
+        pos_to(lax.rem(c + k, 16)).wait()
+        return carry
+
+    lax.fori_loop(1, 16, await_pos, 0)
+
+    def tables(i, carry):
+        row = jnp.where(lane < 64, posc[2 * i][0:1, :], pltpu.roll(posc[2 * i + 1], 64, 1)[0:1, :])
+        block = part(128 * i, 128)
+        posr[0:1, block] = row
+        column = as_column(row)
+        posk[block, :] = jnp.broadcast_to(column, (128, 128))
+        angle = column * freq[0:1, :]
+        cos_s[block, :] = jnp.cos(angle)
+        sin_s[block, :] = jnp.sin(angle) * sign
+        return carry
+
+    lax.fori_loop(0, 8, tables, 0)
+    for k in (1, 3, 2):
+        gain_copy(k).wait()
+    for k in (1, 3, 2):
+        qkv_copy(k).wait()
+    for k in (2, 1, 3):
+        wide_copy(X_GATE, k).start()
+        wide_copy(X_UP, k).start()
+    gain_attn, gain_mlp = gain[0:1, :], gain[1:2, :]
+
+    def out_copy(k):
+        return across(H_OUT, k, out, xall.at[my_rows])
+
+    def to_pair(ref, e, b, i, width, dst):
+        src = ref.at[part(128 * b + 64 * (i // 2), 64), pl.ds(width * (i % 2), width)]
+        return over_c(e, 4 * b + i, src, dst.at[part(64 * c, 64)])
+
+    def from_pairs(e, width, b):
+        for i in range(4):
+            to = 4 * b + i
+
+            @pl.when(to != c)
+            def _(to=to):
+                k = lax.rem(c - to + 16, 16)
+                place = (qs if width == 512 else das).at[part(64 * to, 64)]
+                pltpu.make_async_copy(place, place, cr.at[e, k]).wait()
+
+    def project(k, carry):
+        b = behind(k)
+        rows = part(128 * b, 128)
+
+        @pl.when(jnp.logical_and(first, k > 0))
+        def _():
+            in_copy(k).wait_recv()
+
+        @pl.when(second)
+        def _():
+            out_copy(k).wait_recv()
+
+        value = xall[rows, :].astype(F32)
+        normed = (
+            value
+            * lax.rsqrt(jnp.mean(value * value, axis=-1, keepdims=True) + EPSILON)
+            * gain_attn
+        ).astype(BF)
+        nf[rows, :] = normed
+        u = mm(normed, wqkv[...])
+        cosine, sine = cos_c[rows, :], sin_c[rows, :]
+        for h in range(8):
+            head = u[:, 128 * h : 128 * h + 128]
+            if h % 4 != 3:
+                head = turn(head, cosine, sine)
+            qsend[rows, 128 * h : 128 * h + 128] = head.astype(BF)
+        for i in range(4):
+
+            @pl.when(4 * b + i != c)
+            def _(i=i):
+                to_pair(qsend, C_QKV, b, i, 512, qs).start()
+
+            @pl.when(4 * b + i == c)
+            def _(i=i):
+                qs[part(64 * c, 64), :] = qsend[
+                    part(128 * b + 64 * (i // 2), 64), 512 * (i % 2) : 512 * (i % 2) + 512
+                ]
+
+        return carry
+
+    lax.fori_loop(0, 4, project, 0)
+
+    def await_qkv(k, carry):
+        place = qs.at[part(64 * lax.rem(c - k + 16, 16), 64)]
+        over_c(C_QKV, lax.rem(c + k, 16), place, place).wait_recv()
+        return carry
+
+    lax.fori_loop(1, 16, await_qkv, 0)
+
+    vt[...] = qs[:, 384:512].T
+    kt[...] = qs[:, 256:384].T
+
+    def masked(q, cols):
+        st = mm_nt(qs[:, 256:384], q) * SCALE
+        return jnp.where(posk[:, 0:1] <= posr[0:1, cols], st, -1e30)
+
+    def att_place():
+        return attp.at[part(64 * (c // 2), 64), part(256 * lax.rem(c, 2), 256)]
+
+    def att_to(to):
+        return over_c(C_ATT, to, osend.at[part(64 * to, 64)], att_place())
+
+    def attend(n, carry):
+        rows = part(256 * n, 256)
+        for g in range(2):
+            st = masked(qs[rows, 128 * g : 128 * g + 128], rows)
+            top = jnp.max(st, axis=0, keepdims=True)
+            e = jnp.exp(st - top)
+            total = jnp.sum(e, axis=0, keepdims=True)
+            lse[g : g + 1, rows] = top + jnp.log(total)
+            pt = (e * (1.0 / total)).astype(BF)
+            osend[rows, 128 * g : 128 * g + 128] = mm(vt[...], pt).T.astype(BF)
+        for i in range(4):
+            to = 4 * n + i
+
+            @pl.when(to != c)
+            def _(to=to):
+                att_to(to).start()
+
+            @pl.when(to == c)
+            def _(to=to):
+                attp[part(64 * (c // 2), 64), part(256 * lax.rem(c, 2), 256)] = osend[
+                    part(64 * to, 64), :
+                ]
+
+        return carry
+
+    lax.fori_loop(0, 4, attend, 0)
+
+    def await_att(b):
+        for i in range(4):
+            to = 4 * b + i
+
+            @pl.when(to != c)
+            def _(to=to, i=i):
+                k = lax.rem(c - to + 16, 16)
+                place = attp.at[part(64 * (2 * b + i // 2), 64), pl.ds(256 * (i % 2), 256)]
+                remote(place, place, cs.at[C_ATT, k], cr.at[C_ATT, k], {"ctx": lax.rem(c + k, 16)}).wait_recv()
+
+    def give(n, e, k, b, value):
+        @pl.when(k < 4)
+        def _():
+            psend[n % 2, b] = value.astype(BF)
+            sum_copy(e, k).start()
+
+        @pl.when(k == 4)
+        def _():
+            own[...] = value
+
+    def take(n, e):
+        total = own[...]
+        for k in (1, 3, 2):
+            sum_copy(e, k).wait_recv()
+            total = total + prec[n % 2, k].astype(F32)
+        return total
+
+    def combine(k, carry):
+        b = lax.rem(x + k, 4)
+        await_att(b)
+        give(0, X_SUM1, k, b, mm(attp[part(128 * b, 128), :], wop[...]))
+        return carry
+
+    lax.fori_loop(1, 5, combine, 0)
+    middle = xall[my_rows, :].astype(F32) + take(0, X_SUM1)
+    mid[...] = middle
+    n2[my_rows, :] = (
+        middle * lax.rsqrt(jnp.mean(middle * middle, axis=-1, keepdims=True) + EPSILON) * gain_mlp
+    ).astype(BF)
+    for k in (2, 1, 3):
+        rows_to_all(X_N2, n2, k).start()
+
+    for copy in own_wide:
+        copy.wait()
+    for k in (1, 3, 2):
+        wide_copy(X_GATE, k).wait()
+        wide_copy(X_UP, k).wait()
+
+    def pair(blocks, ref):
+        return jnp.concatenate([ref[part(128 * b, 128), :] for b in blocks], axis=0)
+
+    def feed(ks, final):
+        blocks = [behind(k) for k in ks]
+        a = pair(blocks, n2)
+        ga, u = mm(a, wgf[...]), mm(a, wuf[...])
+        h = (ga * (1.0 / (1.0 + jnp.exp(-ga))) * u).astype(BF)
+        result = mm(h, wd[...])
+        for n, (k, b) in enumerate(zip(ks, blocks)):
+            rows, piece = part(128 * b, 128), slice(128 * n, 128 * n + 128)
+            gate[rows, :] = ga[piece]
+            up[rows, :] = u[piece]
+            hidden[rows, :] = h[piece]
+            if k == 0:
+                own[...] = result[piece]
+            else:
+                psend[1, b] = result[piece].astype(BF)
+                sum_copy(X_SUM2, 4 - k).start()
+
+    rows_to_all(X_N2, n2, 1).wait_recv()
+    feed((1, 0), False)
+    rows_to_all(X_N2, n2, 3).wait_recv()
+    rows_to_all(X_N2, n2, 2).wait_recv()
+    feed((2, 3), True)
+    out[...] = (mid[...] + take(1, X_SUM2)).astype(BF)
+
+    @pl.when(first)
+    def _():
+        for k in range(4):
+            out_copy(k).start()
+
+    def dx_copy(k):
+        return across(H_DX, k, dx, dyf.at[my_rows])
+
+    @pl.when(first)
+    def _():
+        for k in range(4):
+            dx_copy(k).wait_recv()
+
+    @pl.when(second)
+    def _():
+        for k in (1, 3, 2):
+            dy_copy(k).wait_recv()
+
+    def feed_back(ks):
+        blocks = [ahead(k) for k in ks]
+        dh = mm_nt(pair(blocks, dyf), wd[...])
+        ga, u = pair(blocks, gate), pair(blocks, up)
+        s = 1.0 / (1.0 + jnp.exp(-ga))
+        dga = (dh * u * (s * (1.0 + ga * (1.0 - s)))).astype(BF)
+        du = (dh * (ga * s)).astype(BF)
+        result = mm_nt(dga, wgf[...]) + mm_nt(du, wuf[...])
+        for n, (k, b) in enumerate(zip(ks, blocks)):
+            rows, piece = part(128 * b, 128), slice(128 * n, 128 * n + 128)
+            dgu[rows, 0:1024] = dga[piece]
+            dgu[rows, 1024:2048] = du[piece]
+            if k == 0:
+                own[...] = result[piece]
+            else:
+                psend[0, b] = result[piece].astype(BF)
+                sum_copy(X_SUM3, k).start()
+
+    for k in (1, 2, 3):
+        sum_copy(X_SUM1, k).wait_send()
+    feed_back((2, 1))
+    feed_back((3, 0))
+
+    def norm_back(value, grad, gain_row):
+        r = lax.rsqrt(jnp.mean(value * value, axis=-1, keepdims=True) + EPSILON)
+        unit = value * r
+        t = grad * gain_row
+        back = r * (t - unit * jnp.mean(t * unit, axis=-1, keepdims=True))
+        return back, jnp.sum(grad * unit, axis=0, keepdims=True)
+
+    back, g_mlp = norm_back(mid[...], take(2, X_SUM3), gain_mlp)
+    dmid = dyf[my_rows, :].astype(F32) + back
+    mid[...] = dmid
+    ggain[...] = jnp.zeros_like(ggain)
+    ggain[1:2, :] = g_mlp
+    dbr[my_rows, :] = dmid.astype(BF)
+    for k in (2, 1, 3):
+        rows_to_all(X_DBR, dbr, k).start()
+
+    def branch(k, carry):
+        b = behind(k)
+        rows = part(128 * b, 128)
+
+        @pl.when(k > 0)
+        def _():
+            rows_to_all(X_DBR, dbr, k).wait_recv()
+
+        dsend[rows, :] = mm_nt(dbr[rows, :], wop[...]).astype(BF)
+        for i in range(4):
+
+            @pl.when(4 * b + i != c)
+            def _(i=i):
+                to_pair(dsend, C_DATT, b, i, 256, das).start()
+
+            @pl.when(4 * b + i == c)
+            def _(i=i):
+                das[part(64 * c, 64), :] = dsend[
+                    part(128 * b + 64 * (i // 2), 64), 256 * (i % 2) : 256 * (i % 2) + 256
+                ]
+
+        return carry
+
+    lax.fori_loop(0, 4, branch, 0)
+
+    def await_das(k, carry):
+        place = das.at[part(64 * lax.rem(c - k + 16, 16), 64)]
+        over_c(C_DATT, lax.rem(c + k, 16), place, place).wait_recv()
+        return carry
+
+    lax.fori_loop(1, 16, await_das, 0)
+    dk[...] = jnp.zeros_like(dk)
+    dv[...] = jnp.zeros_like(dv)
+
+    def attend_back(n, carry):
+        rows = part(256 * n, 256)
+        for g in range(2):
+            cols = slice(128 * g, 128 * g + 128)
+            q, da = qs[rows, cols], das[rows, cols]
+            p = jnp.exp(masked(q, rows) - lse[g : g + 1, rows])
+            dp = mm_nt(qs[:, 384:512], da)
+            dv[...] += mm(p.astype(BF), da)
+            ds = (p * (dp - jnp.sum(p * dp, axis=0, keepdims=True))).astype(BF)
+            dk[...] += mm(ds, q)
+            dq = mm(kt[...], ds).T * SCALE
+            dqs[rows, cols] = turn(dq, cos_s[rows, :], -sin_s[rows, :]).astype(BF)
+        return carry
+
+    lax.fori_loop(0, 4, attend_back, 0)
+    dqs[:, 256:384] = turn(dk[...] * SCALE, cos_s[...], -sin_s[...]).astype(BF)
+    dqs[:, 384:512] = dv[...].astype(BF)
+
+    def dqkv_to(to):
+        place = dqp.at[part(64 * (c // 2), 64), part(512 * lax.rem(c, 2), 512)]
+        return over_c(C_DQKV, to, dqs.at[part(64 * to, 64)], place)
+
+    def send_dqkv(k, carry):
+        dqkv_to(lax.rem(c + k, 16)).start()
+        return carry
+
+    lax.fori_loop(1, 16, send_dqkv, 0)
+    dqp[part(64 * (c // 2), 64), part(512 * lax.rem(c, 2), 512)] = dqs[part(64 * c, 64), :]
+
+    def await_dqkv(b):
+        for i in range(4):
+            to = 4 * b + i
+
+            @pl.when(to != c)
+            def _(to=to, i=i):
+                k = lax.rem(c - to + 16, 16)
+                place = dqp.at[part(64 * (2 * b + i // 2), 64), pl.ds(512 * (i % 2), 512)]
+                remote(place, place, cs.at[C_DQKV, k], cr.at[C_DQKV, k], {"ctx": lax.rem(c + k, 16)}).wait_recv()
+
+    for k in (1, 2, 3):
+        sum_copy(X_SUM2, k).wait_send()
+
+    def input_grad(k, carry):
+        b = lax.rem(x + k, 4)
+        await_dqkv(b)
+        give(3, X_SUM4, k, b, mm_nt(dqp[part(128 * b, 128), :], wqkv[...]))
+        return carry
+
+    lax.fori_loop(1, 5, input_grad, 0)
+    back, g_attn = norm_back(xall[my_rows, :].astype(F32), take(3, X_SUM4), gain_attn)
+    dx[...] = (mid[...] + back).astype(BF)
+    ggain[0:1, :] = g_attn
+
+    @pl.when(second)
+    def _():
+        for k in range(4):
+            dx_copy(k).start()
+
+    for n in range(2):
+        rows = slice(256 * n, 256 * n + 256)
+        att[rows, :] = jnp.concatenate(
+            [attp[rows, 128 * h : 128 * h + 96] for h in range(4)], axis=1
+        )
+        pieces = []
+        for h in range(8):
+            if h % 4 == 3:
+                pieces.append(dqp[rows, 128 * h : 128 * h + 96])
+            else:
+                pieces.append(dqp[rows, 128 * h : 128 * h + 48])
+                pieces.append(dqp[rows, 128 * h + 64 : 128 * h + 112])
+        dqkv[rows, :] = jnp.concatenate(pieces, axis=1)
+
+    def sent_c(k, carry):
+        to = lax.rem(c + k, 16)
+        place = qs.at[part(64 * to, 64)]
+        over_c(C_QKV, to, place, place).wait_send()
+        att_to(to).wait_send()
+        place = das.at[part(64 * to, 64)]
+        over_c(C_DATT, to, place, place).wait_send()
+        dqkv_to(to).wait_send()
+        return carry
+
+    lax.fori_loop(1, 16, sent_c, 0)
+    for k in (1, 2, 3):
+        for e in (X_SUM3, X_SUM4):
+            sum_copy(e, k).wait_send()
+        rows_to_all(X_N2, n2, k).wait_send()
+        rows_to_all(X_DBR, dbr, k).wait_send()
+
+    @pl.when(first)
+    def _():
+        for k in (1, 2, 3):
+            in_copy(k).wait_send()
+        for k in range(4):
+            out_copy(k).wait_send()
+
+    @pl.when(second)
+    def _():
+        for k in (1, 2, 3):
+            dy_copy(k).wait_send()
+        for k in range(4):
+            dx_copy(k).wait_send()
+
+
+def run_layer(xin, dyin, pos, freq, gains, wq, wk, wv, wo, wd, wg, wu, cid):
+    vm = pl.BlockSpec(memory_space=pltpu.VMEM)
+    hbm = pl.BlockSpec(memory_space=pl.ANY)
+    dma = pltpu.SemaphoreType.DMA
+    shapes = [
+        ((128, WIDTH), BF),
+        ((128, WIDTH), BF),
+        ((512, WIDTH), BF),
+        ((512, WIDTH), BF),
+        ((512, 2048), BF),
+        ((512, 768), BF),
+        ((512, 384), BF),
+        ((512, WIDTH), BF),
+        ((512, 1024), BF),
+        ((512, WIDTH), BF),
+        ((8, WIDTH), F32),
+    ]
+    scratch = [
+        ((4, 384, 1024), BF),
+        ((WIDTH, 1024), BF),
+        ((WIDTH, 1024), BF),
+        ((WIDTH, 1024), BF),
+        ((512, WIDTH), BF),
+        ((512, WIDTH), BF),
+        ((8, WIDTH), F32),
+        ((4, 8, 128), F32),
+        ((4, 2, 8, 128), F32),
+        ((16, 8, 128), F32),
+        ((8, 1024), F32),
+        ((1024, 128), F32),
+        ((512, 128), F32),
+        ((512, 128), F32),
+        ((1024, 128), F32),
+        ((1024, 128), F32),
+        ((512, 1024), BF),
+        ((1024, 512), BF),
+        ((128, 1024), BF),
+        ((128, 1024), BF),
+        ((8, 1024), F32),
+        ((1024, 256), BF),
+        ((512, 512), BF),
+        ((128, WIDTH), F32),
+        ((512, 1024), F32),
+        ((512, 1024), F32),
+        ((128, WIDTH), F32),
+        ((2, 4, 128, WIDTH), BF),
+        ((2, 4, 128, WIDTH), BF),
+        ((512, 512), BF),
+        ((1024, 256), BF),
+        ((1024, 128), F32),
+        ((1024, 128), F32),
+        ((1024, 512), BF),
+        ((512, 1024), BF),
+    ]
+    return pl.pallas_call(
+        layer_kernel,
+        out_shape=[jax.ShapeDtypeStruct(s, d) for s, d in shapes],
+        in_specs=[vm] * 10 + [hbm] * 2,
+        out_specs=[vm] * len(shapes),
+        scratch_shapes=[pltpu.VMEM(s, d) for s, d in scratch]
+        + [dma((13, 4)), dma((13, 4)), dma((5, 16)), dma((5, 16)), dma((2, 4)), dma((2, 4))],
+        name="layer",
+        compiler_params=pltpu.CompilerParams(
+            collective_id=cid, has_side_effects=True, vmem_limit_bytes=63 << 20
+        ),
+    )(xin, dyin, pos, freq, gains, wq, wk, wv, wo, wd, wg, wu)
+
+
 def local(
     inputs,
     positions,
@@ -520,136 +1096,32 @@
     w_up,
     w_down,
 ):
-    section = lax.axis_index("section")
-    x_idx = lax.axis_index("fsdp")
-    c_idx = lax.axis_index("ctx")
-    is_first = section == 0
-
-    pos8 = lax.all_gather(positions, "fsdp", axis=0, tiled=True)
-    pos_all = lax.all_gather(pos8, "ctx", axis=1, tiled=True)
-    pos_seq = lax.dynamic_index_in_dim(pos_all, c_idx // 2, 0, keepdims=False)
-    freq = THETA ** (-(jnp.arange(48, dtype=F32) * 2.0 / 96))
-
-    def table_of(p):
-        ang = p.reshape(-1).astype(F32)[:, None] * freq[None, :]
-        return jnp.cos(ang), jnp.sin(ang)
-
-    table_c = table_of(pos8)
-    table_s = table_of(pos_seq)
-    gains = lax.all_gather(jnp.concatenate([norm_attn, norm_mlp], 0), "fsdp", axis=1, tiled=True)
-    gain_attn, gain_mlp = gains[0].astype(F32), gains[1].astype(F32)
-
-    wqkv_shard = jnp.concatenate(
-        [
-            w_query[0].reshape(384, 8, 192),
-            key_weight[0].reshape(384, 8, 96),
-            value_weight[0].reshape(384, 8, 96),
-        ],
-        axis=2,
-    ).reshape(384, 4, 768)
-    wqkv_shard = wqkv_shard.transpose(1, 0, 2)
-
-    def cols(ref, p):
-        return ref.at[:, pl.ds(pl.multiple_of(p * 1024, 1024), 1024)]
-
-    def rows(ref, p):
-        return ref.at[pl.ds(pl.multiple_of(p * 384, 384), 384)]
-
-    wqkv, wg, wu = exchange(
-        [wqkv_shard, w_gate[0], w_up[0]],
-        [((1536, 768), slot, rows), ((1536, 1024), cols, rows), ((1536, 1024), cols, rows)],
-        "fsdp",
-        N_X,
-        None,
+    lane = jnp.arange(128)
+    index = jnp.where(lane < 64, lane, lane - 64)
+    freq = jnp.where(index < 48, THETA ** (-(index.astype(F32) * 2.0 / HEAD_SIZE)), 0.0)
+    freq = jnp.broadcast_to(freq[None], (8, 128))
+    pos = jnp.broadcast_to(positions.reshape(1, 128).astype(F32), (8, 128))
+    gains = jnp.concatenate([norm_attn, norm_mlp, jnp.zeros((6, 384), BF)], axis=0).astype(F32)
+    out, dx, nf, n2, dgu, dqkv, att, dbr, hidden, dyf, ggain = run_layer(
+        inputs.reshape(128, WIDTH),
+        out_grad.reshape(128, WIDTH),
+        pos,
+        freq,
+        gains,
+        w_query[0],
+        key_weight[0],
+        value_weight[0],
+        output_weight[0],
+        w_down[0],
+        w_gate[0],
+        w_up[0],
         0,
     )
-    wo = output_weight[0]
-    wd = w_down[0]
-
-    visible = pos_seq[:, None] >= pos_seq[None, :]
-    scale = HEAD_SIZE ** (-0.5)
-
-    def forward(stage, xin, base):
-        x32 = xin.astype(F32)
-        nf = gather_x(rms(x32, gain_attn).astype(BF), stage, base)
-        u = mm(nf, wqkv).reshape(512, 2, 384)
-        r = rotate(u, table_c, 1.0).astype(BF)
-        send = r.reshape(8, 64, 2, 384).transpose(0, 2, 1, 3).reshape(16, 64, 384)
-        qkv = swap_c(send, stage, base + 1).reshape(1024, 384)
-        q = qkv[:, :192].reshape(1024, 2, 96)
-        k = qkv[:, 192:288]
-        v = qkv[:, 288:]
-        scores = jnp.einsum("qgd,kd->gqk", q, k, preferred_element_type=F32) * scale
-        scores = jnp.where(visible[None], scores, -1e30)
-        top = jnp.max(scores, axis=-1, keepdims=True)
-        e = jnp.exp(scores - top)
-        total = jnp.sum(e, axis=-1, keepdims=True)
-        probs = (e / total).astype(BF)
-        lse = top + jnp.log(total)
-        att = jnp.einsum("gqk,kd->qgd", probs, v, preferred_element_type=F32).astype(BF)
-        att = swap_c(att.reshape(16, 64, 192), stage, base + 2)
-        att = att.reshape(8, 2, 64, 192).transpose(0, 2, 1, 3).reshape(512, 384)
-        mid = x32 + reduce_x(mm(att, wo), stage, base + 3)
-        n2 = gather_x(rms(mid, gain_mlp).astype(BF), stage, base + 4)
-        gate = mm(n2, wg)
-        up = mm(n2, wu)
-        hidden = (jax.nn.silu(gate) * up).astype(BF)
-        out = (mid + reduce_x(mm(hidden, wd), stage, base + 5)).astype(BF)
-        return out, (x32, nf, q, k, v, lse, att, mid, n2, gate, up, hidden)
-
-    def backward(stage, dy, kept, base):
-        x32, nf, q, k, v, lse, att, mid, n2, gate, up, hidden = kept
-        dyf = gather_x(dy, stage, base)
-        dhidden = mm_nt(dyf, wd)
-        sig = jax.nn.sigmoid(gate)
-        dgate = (dhidden * up * (sig * (1.0 + gate * (1.0 - sig)))).astype(BF)
-        dup = (dhidden * (gate * sig)).astype(BF)
-        dn2 = reduce_x(mm_nt(dgate, wg) + mm_nt(dup, wu), stage, base + 1)
-        _, back_mlp = jax.vjp(rms, mid, gain_mlp)
-        dmid, g_mlp = back_mlp(dn2)
-        dmid = dmid + dy.astype(F32)
-        dbr = gather_x(dmid.astype(BF), stage, base + 2)
-        datt = mm_nt(dbr, wo).astype(BF)
-        send = datt.reshape(8, 64, 2, 192).transpose(0, 2, 1, 3).reshape(16, 64, 192)
-        da = swap_c(send, stage, base + 3).reshape(1024, 2, 96)
-        scores = jnp.einsum("qgd,kd->gqk", q, k, preferred_element_type=F32) * scale
-        probs = jnp.exp(jnp.where(visible[None], scores, -1e30) - lse)
-        dprobs = jnp.einsum("qgd,kd->gqk", da, v, preferred_element_type=F32)
-        dv = jnp.einsum("gqk,qgd->kd", probs.astype(BF), da, preferred_element_type=F32)
-        dot = jnp.sum(probs * dprobs, axis=-1, keepdims=True)
-        ds = (probs * (dprobs - dot)).astype(BF)
-        dq = jnp.einsum("gqk,kd->qgd", ds, k, preferred_element_type=F32) * scale
-        dk = jnp.einsum("gqk,qgd->kd", ds, q, preferred_element_type=F32) * scale
-        dqkv = jnp.concatenate([dq.reshape(1024, 192), dk, dv], axis=1)
-        dqkv = rotate(dqkv[:, None], table_s, -1.0).astype(BF).reshape(16, 64, 384)
-        dqkv = swap_c(dqkv, stage, base + 4)
-        dqkv = dqkv.reshape(8, 2, 64, 384).transpose(0, 2, 1, 3).reshape(512, 768)
-        dn = reduce_x(mm_nt(dqkv, wqkv), stage, base + 5)
-        _, back_attn = jax.vjp(rms, x32, gain_attn)
-        dx, g_attn = back_attn(dn)
-        dx = (dx + dmid).astype(BF)
-        return dx, (g_attn, g_mlp, nf, dqkv, att, dbr, n2, dgate, dup, hidden, dyf)
-
-    def choose(a, b):
-        return jax.tree.map(lambda p, q: jnp.where(is_first, p, q), a, b)
-
-    x_own = inputs.reshape(128, WIDTH)
-    out0, kept0 = forward(0, x_own, 1)
-    out1, kept1 = forward(1, hop(out0, 0, 7), 8)
-    dx1, parts1 = backward(1, out_grad.reshape(128, WIDTH), kept1, 14)
-    dx0, parts0 = backward(0, hop(dx1, 1, 20), kept0, 21)
-    section_out = choose(out0, out1).reshape(1, 2, 64, WIDTH)
-    section_grad = choose(dx0, dx1).reshape(1, 2, 64, WIDTH)
-    g_attn, g_mlp, nf, dqkv, att, dbr, n2, dgate, dup, hidden, dyf = choose(parts0, parts1)
-
-    gains = jnp.concatenate([g_attn[None], g_mlp[None], jnp.zeros((6, WIDTH), F32)], axis=0)
-    *summed, g_gain = reduce_grads(
-        n2, nf, jnp.concatenate([dgate, dup], axis=1), dqkv, att, dbr, hidden, dyf, gains, 27
-    )
+    *summed, g_gain = reduce_grads(n2, nf, dgu, dqkv, att, dbr, hidden, dyf, ggain, 1)
     g_gate, g_up, g_query, g_key, g_value, g_out, g_down = widen(*summed)
     return (
-        section_out,
-        section_grad,
+        out.reshape(1, 2, 64, WIDTH),
+        dx.reshape(1, 2, 64, WIDTH),
         g_gain[0:1],
         g_query[None],
         g_key[None],

time: 898 us -> 551 us (0.61); the launches traced: 885 us -> 550 us
  matrix products: 102 us -> 0 us
  local copies, waits for them, and re-layouts: 101 us -> 4.21 us
  other arithmetic: 79.4 us -> 2.06 us
  blocking collectives: 45.5 us -> 0 us
  Pallas kernels: 555 us -> 543 us
    dot_general x32 -> x0, matrix products: 102 us -> none  [the longest x10 35 us: mm(): return jnp.dot(a, b, preferred_element_type=F32)]
    all_gather x3 -> x0, blocking collectives: 45.5 us -> none  [the longest x1 25.1 us: local(): pos_all = lax.all_gather(pos8, 'ctx', axis=1, tiled=True)]
    reshape x17 -> x0, local copies, waits for them, and re-layouts: 37.1 us -> none  [the longest x4 8.21 us: forward(): att = att.reshape(8, 2, 64, 192).transpose(0, 2, 1, 3).reshape(512, 384)]
    pallas_call x27 -> x1, Pallas kernels: 411 us -> 386 us  [run_layer(): pl.pallas_call(layer_kernel, out_shape=[jax.ShapeDtypeStruct(s, d) for s,...]
    reduce_sum x18 -> x0, other arithmetic: 24.8 us -> none  [the longest x8 15.3 us: reduce_x(): return jnp.sum(r.astype(F32), axis=0)]
    select_n x6 -> x1, other arithmetic: 17.2 us -> 0.01 us  [local(): jnp.where(index < 48, THETA ** (-(index.astype(F32) * 2.0 / HEAD_SIZE)),...]
    unnamed x183 -> x6, local copies, waits for them, and re-layouts: 17.9 us -> 1.5 us
    convert_element_type x12 -> x2, other arithmetic: 17.4 us -> 2.05 us  [the longest x1 1.37 us: local(): jnp.concatenate([norm_attn, norm_mlp, jnp.zeros((6, 384), BF)], axis=0)]
where the time goes in v3:
time: 551 us; the launch traced here: 550 us
  Pallas kernels  543 us (99%)
    pallas_call x1, Pallas kernels, run_layer(): pl.pallas_call(layer_kernel, out_shape=[jax.ShapeDtypeStruct(s, d) for s,...  386 us
    pallas_call x1, Pallas kernels, reduce_grads(): pl.pallas_call(grad_kernel, out_shape=[jax.ShapeDtypeStruct((4, 4) + s, B...  142 us
    pallas_call x1, Pallas kernels, widen(): pl.pallas_call(widen_kernel, grid=(steps,), out_shape=[shape(384, FF), sh...  14.6 us

profile of v3, /device:TPU:0, one launch (start us, length us, event | category | flops | bytes accessed | tf_op | source)
XLA Modules:
  0.0 550.1 jit_solution(5889736818462469246)
XLA Ops:
  0.7 0.1 pad.2.clone
  0.7 0.7 convert_element_type.21
  1.4 0.1 convert_element_type.22
  1.5 0.6 broadcast_in_dim.39.pos
  2.1 0.6 broadcast_in_dim.41.freq
  2.7 1.4 maximum_convert_fusion.gains
  4.1 386.3 %layer.1 = (bf16[128,1536]{1,0:T(8,128)(2,1)}, bf16[128,1536]{1,0:T(8,128)(2,1)}, bf16[512,1536]{1,0:T(8,128)(2,1)}, bf16[512,1536]{1,0:T(8,128)(2,1)}, bf16[512...) custom-call(bf16[128,1536]{1,0:T(8,128)(2,1)} %bitcast.27, ...), custom_call_target="tpu_custom_call" | custom-call | tf_op jit(solution)/shard_map/layer/pallas_call | solution.py:1071
  390.4 142.3 %reduce_grads.1 = (bf16[4,4,96,1024]{3,2,1,0:T(8,128)(2,1)}, bf16[4,4,96,1024]{3,2,1,0:T(8,128)(2,1)}, bf16[4,4,64,1536]{3,2,1,0:T(8,128)(2,1)}, bf16[4,4,96,768...) custom-call(bf16[512,1536]{1,0:T(8,128)(2,1)} %get-tuple-element.37.n2, ...), custom_call_target="tpu_custom_call" | custom-call | tf_op jit(solution)/shard_map/reduce_grads/pallas_call | solution.py:296
  532.7 1.4 fusion
  534.0 0.0 copy-start.1
  534.0 0.0 copy-start
  534.0 14.6 %widen.1 = (f32[384,4096]{1,0:T(8,128)}, f32[384,4096]{1,0:T(8,128)}, f32[384,1536]{1,0:T(8,128)}, f32[384,768]{1,0:T(8,128)}, f32[384,768]{1,0:T(8,128)}, /*index=5*/f32[384,1536]{1,0:T(8,128)}, f32[1024,1536]{1,0:T(8,128)}) custom-call(bf16[4,4,96,1024]{3,2,1,0:T(8,128)(2,1)} %get-tuple-element.47.w_gate, bf16[4,4,96,1024]{3,2,1,0:T(8,128)(2,1)} %get-tuple-element.48.w_up, ...), custom_call_target="tpu_custom_call" | custom-call | tf_op jit(solution)/shard_map/widen/pallas_call | solution.py:349
  548.6 0.0 copy-done.1
  548.6 0.7 copy.25
  549.4 0.0 copy-done
  549.4 0.7 copy.26
  (2 shorter events, 0.0 us)
Async XLA Ops:
  534.0 14.6 %copy-start.1 = (bf16[128,1536]{1,0:T(8,128)(2,1)S(1)}, bf16[128,1536]{1,0:T(8,128)(2,1)}, u32[]{:S(2)}) copy-start(bf16[128,1536]{1,0:T(8,128)(2,1)} %get-tuple-element.35) | copy-start | bytes 1179652
  534.0 15.3 %copy-start = (bf16[128,1536]{1,0:T(8,128)(2,1)S(1)}, bf16[128,1536]{1,0:T(8,128)(2,1)}, u32[]{:S(2)}) copy-start(bf16[128,1536]{1,0:T(8,128)(2,1)} %get-tuple-element.36) | copy-start | bytes 1179652

commit v4 on v3

--- a/solution.py
+++ b/solution.py
@@ -1,5 +1,6 @@
 import jax
 import jax.numpy as jnp
+import numpy as np
 from jax import lax
 from jax.experimental import pallas as pl
 from jax.experimental.pallas import tpu as pltpu
@@ -380,8 +381,7 @@
 
 
 X_GAIN, X_POS, X_IN, X_DY, X_QKV, X_GATE, X_UP, X_SUM1, X_N2, X_SUM2, X_SUM3, X_DBR, X_SUM4 = range(13)
-C_POS, C_QKV, C_ATT, C_DATT, C_DQKV = range(5)
-H_OUT, H_DX = range(2)
+C_POS, C_QKV, C_ATT, C_DATT, C_DQ, C_DKV = range(6)
 SCALE = HEAD_SIZE ** (-0.5)
 
 
@@ -407,14 +407,15 @@
 def layer_kernel(
     xin,
     dyin,
-    pos,
+    positions,
     freq,
-    gains,
+    norm_attn,
+    norm_mlp,
     wq,
     wk,
     wv,
-    wo,
-    wd,
+    wo_in,
+    wd_in,
     wg,
     wu,
     out,
@@ -433,7 +434,11 @@
     wgf,
     wuf,
     wop,
+    wd,
+    relay_s,
     xall,
+    gains,
+    pos,
     gain,
     posx,
     posv,
@@ -457,6 +462,7 @@
     own,
     psend,
     prec,
+    prec3,
     dsend,
     das,
     dk,
@@ -467,12 +473,15 @@
     xr,
     cs,
     cr,
-    hs,
-    hr,
+    ws,
+    wr,
+    ls,
+    go,
 ):
     section = lax.axis_index("section")
     x = lax.axis_index("fsdp")
     c = lax.axis_index("ctx")
+    y, z = lax.rem(c, 4), c // 4
     first, second = section == 0, section == 1
     my_rows = part(128 * x, 128)
 
@@ -511,43 +520,171 @@
         k = lax.rem(to - c + 16, 16)
         return remote(src, dst, cs.at[e, k], cr.at[e, k], {"ctx": to})
 
-    def across(e, k, src, dst):
-        return remote(
-            src, dst, hs.at[e, k], hr.at[e, k], {"section": 1 - section, "fsdp": ahead(k)}
-        )
-
-    def rows_to_all(e, ref, k):
-        return over_x(e, k, ref.at[my_rows], ref.at[my_rows])
-
-    def sum_copy(e, k):
-        n = (X_SUM1, X_SUM2, X_SUM3, X_SUM4).index(e)
-        return over_x(e, k, psend.at[n % 2, ahead(k)], prec.at[n % 2, k])
+    def piece(e, i, d, src, dst, flip=False):
+        device = {"fsdp": lax.rem(x + d + 4, 4)}
+        if flip:
+            device["section"] = 1 - section
+        return remote(src, dst, xs.at[e, i], xr.at[e, i], device)
+
+    def half(ref, b, n):
+        return ref.at[part(128 * b + 64 * n, 64)]
+
+    def gather(e, i, src, ref, flip=False):
+        if i == 6:
+            return piece(e, 6, 0, src, ref.at[my_rows], True)
+        if i >= 4:
+            place = half(ref, lax.rem(x + (3 if i == 4 else 1), 4), i - 4)
+            return piece(e, i, 1 if i == 4 else -1, place, place)
+        n = i % 2
+        return piece(e, i, 1 if i < 2 else -1, half(src, 0, n), half(ref, x, n), flip)
+
+    def gather_start(e, src, ref, flip=False):
+        for i in (0, 3, 1, 2):
+            gather(e, i, src, ref, flip).start()
+
+    def gather_pass(e, src, ref):
+        for i, n in ((0, 4), (3, 5)):
+            gather(e, i, src, ref).wait_recv()
+            gather(e, n, src, ref).start()
+        for i in (1, 2):
+            gather(e, i, src, ref).wait_recv()
+
+    def gather_far(e, src, ref):
+        for i in (4, 5):
+            gather(e, i, src, ref).wait_recv()
+
+    def gather_sent(e, src, ref, forwarded=True, started=True, flip=False):
+        for i in (0, 1, 2, 3) if started else ():
+            gather(e, i, src, ref, flip).wait_send()
+        for i in (4, 5) if forwarded else ():
+            gather(e, i, src, ref).wait_send()
+
+    def total(e, i):
+        n = (X_SUM1, X_SUM2, X_SUM3, X_SUM4).index(e) % 2
+        to = (2, 2, 1, 3, 1, 3)[i]
+        h = (0, 1, 1, 0, 0, 1)[i]
+        src = psend.at[n, lax.rem(x + to, 4), pl.ds(64 * h, 64)]
+        if i < 2:
+            dst = relay_s.at[n, i]
+        else:
+            dst = prec.at[n, 0 if to == 1 else 1, pl.ds(64 * h, 64)]
+        return piece(e, i, (1, -1, 1, -1, 1, -1)[i], src, dst)
+
+    def total_pass(e):
+        n = (X_SUM1, X_SUM2, X_SUM3, X_SUM4).index(e) % 2
+        for i in (0, 1):
+            total(e, i).wait_recv()
+            b, rows = lax.rem(x + (1, 3)[i], 4), slice(64 * i, 64 * i + 64)
+            psend[n, b, rows] = psend[n, b, rows] + relay_s[n, i]
+            total(e, 4 + i).start()
+
+    def total_take(e):
+        n = (X_SUM1, X_SUM2, X_SUM3, X_SUM4).index(e) % 2
+        for i in (2, 3, 4, 5):
+            total(e, i).wait_recv()
+        return own[...] + prec[n, 0].astype(F32) + prec[n, 1].astype(F32)
+
+    def total_sent(e):
+        for i in range(6):
+            total(e, i).wait_send()
+
+    def quarter(n):
+        return (z, y)[n % 2]
+
+    def weight(n, i):
+        dst = (wqkv, wqkv, wgf, wuf)[n]
+        cols = (pl.ds(0, 512), pl.ds(512, 512), pl.ds(0, 1024), pl.ds(0, 1024))[n]
+        q = quarter(n)
+        if i < 3:
+            to = lax.rem(x + i + 1, 4)
+            rows = part(96 * q, 96)
+            if n < 2:
+                src = wsend.at[to, rows, cols]
+            else:
+                src = (wg, wu)[n - 2].at[rows, part(1024 * to, 1024)]
+            place = dst.at[pl.ds(pl.multiple_of(384 * x + 96 * q, 96), 96), cols]
+            device = {"fsdp": to}
+        else:
+            b = lax.rem(x + 1 + i % 3, 4)
+            step = (1, -1, 1, -1)[i // 3 - 1]
+            if i < 9:
+                rows = pl.ds(pl.multiple_of(384 * b + 96 * q, 96), 96)
+            else:
+                far, h = lax.rem(q - step + 4, 4), i // 3 - 3
+                rows = pl.ds(pl.multiple_of(384 * b + 96 * far + 48 * h, 48), 48)
+            src = place = dst.at[rows, cols]
+            r = lax.rem(q + step + 4, 4)
+            device = {"ctx": 4 * r + y if n % 2 == 0 else 4 * z + r}
+        return remote(src, place, ws.at[n, i], wr.at[n, i], device)
+
+    def weight_each(which, items, act):
+        for i in items:
+            for n in which:
+                act(weight(n, i))
+
+    def begin(copy):
+        copy.start()
+
+    def arrive(copy):
+        copy.wait_recv()
+
+    def leave(copy):
+        copy.wait_send()
+
+    def weight_fetch(which):
+        weight_each(which, (1, 0, 2), begin)
+
+    def weight_share(which):
+        weight_each(which, range(3), arrive)
+        weight_each(which, range(3, 9), begin)
+
+    def weight_pass(which):
+        for k in range(3):
+            weight_each(which, (3 + k,), arrive)
+            weight_each(which, (9 + k,), begin)
+        for k in range(3):
+            weight_each(which, (6 + k,), arrive)
+            weight_each(which, (12 + k,), begin)
+
+    def weight_wait(which):
+        weight_each(which, range(9, 15), arrive)
+
+    heads, wide = (0, 1), (2, 3)
 
     def gain_copy(k):
-        place = gain.at[:, part(384 * x, 384)]
-        return over_x(X_GAIN, k, gains, place)
+        return over_x(X_GAIN, k, gains, gain.at[:, part(384 * x, 384)])
 
     def pos_copy(k):
         return over_x(X_POS, k, pos, posx.at[x])
 
-    def in_copy(k):
-        return over_x(X_IN, k, xin, xall.at[my_rows])
-
-    def dy_copy(k):
-        return over_x(X_DY, k, dyin, dyf.at[my_rows])
-
-    def qkv_copy(k):
-        return over_x(X_QKV, k, wsend.at[ahead(k)], wqkv.at[part(384 * x, 384)])
-
-    def wide_copy(e, k):
-        src, dst = (wg, wgf) if e == X_GATE else (wu, wuf)
-        return over_x(e, k, src.at[:, part(1024 * ahead(k), 1024)], dst.at[part(384 * x, 384)])
-
+    pos[...] = jnp.broadcast_to(
+        jnp.concatenate([positions[0:1, :], positions[1:2, :]], axis=1).astype(F32), (8, 128)
+    )
+    gains[...] = jnp.broadcast_to(norm_attn[...].astype(F32), (8, 384))
+    gains[1:2, :] = norm_mlp[...].astype(F32)
     for k in (2, 1, 3):
         pos_copy(k).start()
         gain_copy(k).start()
     gain[:, part(384 * x, 384)] = gains[...]
     posx[x] = pos[...]
+
+    @pl.when(first)
+    def _():
+        gather_start(X_IN, xin, xall)
+        xall[my_rows, :] = xin[...]
+
+    def local_copies():
+        yield pltpu.make_async_copy(
+            wg.at[:, part(1024 * x, 1024)], wgf.at[part(384 * x, 384)], ls.at[0]
+        )
+        yield pltpu.make_async_copy(
+            wu.at[:, part(1024 * x, 1024)], wuf.at[part(384 * x, 384)], ls.at[1]
+        )
+        yield pltpu.make_async_copy(wd_in, wd, ls.at[2])
+        for h in range(4):
+            yield pltpu.make_async_copy(
+                wo_in.at[pl.ds(96 * h, 96)], wop.at[pl.ds(128 * h, 96)], ls.at[3 + h]
+            )
 
     for b in range(4):
         pieces = []
@@ -559,34 +696,16 @@
                 jnp.zeros((384, 32), BF),
             ]
         wsend[b] = jnp.concatenate(pieces, axis=1)
-    for k in (2, 1, 3):
-        qkv_copy(k).start()
-    wqkv[part(384 * x, 384), :] = wsend[x]
 
     @pl.when(first)
     def _():
-        for k in (2, 1, 3):
-            in_copy(k).start()
-        xall[my_rows, :] = xin[...]
-
-    @pl.when(second)
-    def _():
-        for k in (2, 1, 3):
-            dy_copy(k).start()
-        dyf[my_rows, :] = dyin[...]
-
-    own_wide = [
-        pltpu.make_async_copy(
-            src.at[:, part(1024 * x, 1024)], dst.at[part(384 * x, 384)], xs.at[e, 0]
-        )
-        for e, src, dst in ((X_GATE, wg, wgf), (X_UP, wu, wuf))
-    ]
-    for copy in own_wide:
+        weight_fetch(heads)
+
+    for copy in local_copies():
         copy.start()
-
-    wop[...] = jnp.zeros_like(wop)
+    wqkv[part(384 * x, 384), :] = wsend[x]
     for h in range(4):
-        wop[128 * h : 128 * h + 96, :] = wo[96 * h : 96 * h + 96, :]
+        wop[128 * h + 96 : 128 * h + 128, :] = jnp.zeros((32, WIDTH), BF)
 
     lane = lax.broadcasted_iota(jnp.int32, (1, 128), 1)
     sign = jnp.where(lane < 64, -1.0, 1.0)
@@ -628,44 +747,58 @@
         sin_s[block, :] = jnp.sin(angle) * sign
         return carry
 
+    @pl.when(first)
+    def _():
+        weight_share(heads)
+        weight_fetch(wide)
+
     lax.fori_loop(0, 8, tables, 0)
     for k in (1, 3, 2):
         gain_copy(k).wait()
-    for k in (1, 3, 2):
-        qkv_copy(k).wait()
-    for k in (2, 1, 3):
-        wide_copy(X_GATE, k).start()
-        wide_copy(X_UP, k).start()
+
+    @pl.when(first)
+    def _():
+        weight_pass(heads)
+        gather_pass(X_IN, xin, xall)
+        gather_far(X_IN, xin, xall)
+        weight_wait(heads)
+        pl.semaphore_signal(go, inc=1, device_id={"section": 1}, device_id_type=MESH)
+
+    @pl.when(second)
+    def _():
+        gather_start(X_DY, dyin, dyf)
+        dyf[my_rows, :] = dyin[...]
+        gather_pass(X_DY, dyin, dyf)
+        pl.semaphore_wait(go, 1)
+        weight_fetch(heads + wide)
+        weight_share(heads + wide)
+        weight_pass(heads + wide)
+        weight_wait(heads + wide)
+
     gain_attn, gain_mlp = gain[0:1, :], gain[1:2, :]
-
-    def out_copy(k):
-        return across(H_OUT, k, out, xall.at[my_rows])
 
     def to_pair(ref, e, b, i, width, dst):
         src = ref.at[part(128 * b + 64 * (i // 2), 64), pl.ds(width * (i % 2), width)]
         return over_c(e, 4 * b + i, src, dst.at[part(64 * c, 64)])
 
-    def from_pairs(e, width, b):
-        for i in range(4):
-            to = 4 * b + i
-
-            @pl.when(to != c)
-            def _(to=to):
-                k = lax.rem(c - to + 16, 16)
-                place = (qs if width == 512 else das).at[part(64 * to, 64)]
-                pltpu.make_async_copy(place, place, cr.at[e, k]).wait()
-
-    def project(k, carry):
-        b = behind(k)
+    def in_order(n):
+        return behind(jnp.where(n == 2, 3, jnp.where(n == 3, 2, n)))
+
+    def project(n, carry):
+        b = in_order(n)
         rows = part(128 * b, 128)
 
-        @pl.when(jnp.logical_and(first, k > 0))
+        @pl.when(jnp.logical_and(second, n == 0))
         def _():
-            in_copy(k).wait_recv()
-
-        @pl.when(second)
+            gather(X_IN, 6, out, xall).wait_recv()
+
+        @pl.when(jnp.logical_and(second, n == 1))
         def _():
-            out_copy(k).wait_recv()
+            gather_pass(X_IN, xin, xall)
+
+        @pl.when(jnp.logical_and(second, n == 3))
+        def _():
+            gather_far(X_IN, xin, xall)
 
         value = xall[rows, :].astype(F32)
         normed = (
@@ -697,6 +830,11 @@
 
     lax.fori_loop(0, 4, project, 0)
 
+    @pl.when(first)
+    def _():
+        weight_share(wide)
+
+
     def await_qkv(k, carry):
         place = qs.at[part(64 * lax.rem(c - k + 16, 16), 64)]
         over_c(C_QKV, lax.rem(c + k, 16), place, place).wait_recv()
@@ -719,6 +857,7 @@
 
     def attend(n, carry):
         rows = part(256 * n, 256)
+
         for g in range(2):
             st = masked(qs[rows, 128 * g : 128 * g + 128], rows)
             top = jnp.max(st, axis=0, keepdims=True)
@@ -754,111 +893,128 @@
                 place = attp.at[part(64 * (2 * b + i // 2), 64), pl.ds(256 * (i % 2), 256)]
                 remote(place, place, cs.at[C_ATT, k], cr.at[C_ATT, k], {"ctx": lax.rem(c + k, 16)}).wait_recv()
 
-    def give(n, e, k, b, value):
-        @pl.when(k < 4)
+    def give(e, n, b, value):
+        place = psend.at[(X_SUM1, X_SUM2, X_SUM3, X_SUM4).index(e) % 2, b]
+
+        @pl.when(n < 3)
         def _():
-            psend[n % 2, b] = value.astype(BF)
-            sum_copy(e, k).start()
-
-        @pl.when(k == 4)
+            place[...] = value.astype(BF)
+
+        @pl.when(n == 0)
+        def _():
+            total(e, 0).start()
+            total(e, 1).start()
+
+        @pl.when(n == 1)
+        def _():
+            total(e, 2).start()
+
+        @pl.when(n == 2)
+        def _():
+            total(e, 3).start()
+            total_pass(e)
+
+        @pl.when(n == 3)
         def _():
             own[...] = value
 
-    def take(n, e):
-        total = own[...]
-        for k in (1, 3, 2):
-            sum_copy(e, k).wait_recv()
-            total = total + prec[n % 2, k].astype(F32)
-        return total
-
-    def combine(k, carry):
-        b = lax.rem(x + k, 4)
+    def far_first(n):
+        return lax.rem(x + jnp.where(n == 0, 2, jnp.where(n == 1, 1, jnp.where(n == 2, 3, 0))), 4)
+
+    def combine(n, carry):
+        b = far_first(n)
         await_att(b)
-        give(0, X_SUM1, k, b, mm(attp[part(128 * b, 128), :], wop[...]))
-        return carry
-
-    lax.fori_loop(1, 5, combine, 0)
-    middle = xall[my_rows, :].astype(F32) + take(0, X_SUM1)
+        give(X_SUM1, n, b, mm(attp[part(128 * b, 128), :], wop[...]))
+        return carry
+
+    @pl.when(first)
+    def _():
+        weight_pass(wide)
+
+    for copy in local_copies():
+        copy.wait()
+    lax.fori_loop(0, 4, combine, 0)
+    middle = xall[my_rows, :].astype(F32) + total_take(X_SUM1)
     mid[...] = middle
     n2[my_rows, :] = (
         middle * lax.rsqrt(jnp.mean(middle * middle, axis=-1, keepdims=True) + EPSILON) * gain_mlp
     ).astype(BF)
-    for k in (2, 1, 3):
-        rows_to_all(X_N2, n2, k).start()
-
-    for copy in own_wide:
-        copy.wait()
-    for k in (1, 3, 2):
-        wide_copy(X_GATE, k).wait()
-        wide_copy(X_UP, k).wait()
+    n2_own = n2.at[my_rows]
+    gather_start(X_N2, n2_own, n2)
+
+    @pl.when(first)
+    def _():
+        weight_wait(wide)
 
     def pair(blocks, ref):
         return jnp.concatenate([ref[part(128 * b, 128), :] for b in blocks], axis=0)
 
-    def feed(ks, final):
-        blocks = [behind(k) for k in ks]
+    def far_copy(d, b):
+        return piece(X_SUM2, d, d, psend.at[1, b], prec3.at[d - 1])
+
+    def feed(ds):
+        blocks = [lax.rem(x + d, 4) for d in ds]
         a = pair(blocks, n2)
         ga, u = mm(a, wgf[...]), mm(a, wuf[...])
         h = (ga * (1.0 / (1.0 + jnp.exp(-ga))) * u).astype(BF)
         result = mm(h, wd[...])
-        for n, (k, b) in enumerate(zip(ks, blocks)):
-            rows, piece = part(128 * b, 128), slice(128 * n, 128 * n + 128)
-            gate[rows, :] = ga[piece]
-            up[rows, :] = u[piece]
-            hidden[rows, :] = h[piece]
-            if k == 0:
-                own[...] = result[piece]
+        for n, (d, b) in enumerate(zip(ds, blocks)):
+            rows, cut = part(128 * b, 128), slice(128 * n, 128 * n + 128)
+            gate[rows, :] = ga[cut]
+            up[rows, :] = u[cut]
+            hidden[rows, :] = h[cut]
+            if d == 0:
+                own[...] = result[cut]
             else:
-                psend[1, b] = result[piece].astype(BF)
-                sum_copy(X_SUM2, 4 - k).start()
-
-    rows_to_all(X_N2, n2, 1).wait_recv()
-    feed((1, 0), False)
-    rows_to_all(X_N2, n2, 3).wait_recv()
-    rows_to_all(X_N2, n2, 2).wait_recv()
-    feed((2, 3), True)
-    out[...] = (mid[...] + take(1, X_SUM2)).astype(BF)
+                psend[1, b] = result[cut].astype(BF)
+                far_copy(d, b).start()
+
+    gather_pass(X_N2, n2_own, n2)
+    feed((1, 3))
+    gather_far(X_N2, n2_own, n2)
+    feed((2, 0))
+    result = mid[...] + own[...]
+    for d in (1, 3, 2):
+        far_copy(d, lax.rem(x + d, 4)).wait_recv()
+        result = result + prec3[d - 1].astype(F32)
+    out[...] = result.astype(BF)
 
     @pl.when(first)
     def _():
-        for k in range(4):
-            out_copy(k).start()
-
-    def dx_copy(k):
-        return across(H_DX, k, dx, dyf.at[my_rows])
+        gather_sent(X_IN, xin, xall, forwarded=False)
+        gather(X_IN, 6, out, xall).start()
+        gather_start(X_IN, out, xall, True)
 
     @pl.when(first)
     def _():
-        for k in range(4):
-            dx_copy(k).wait_recv()
-
-    @pl.when(second)
-    def _():
-        for k in (1, 3, 2):
-            dy_copy(k).wait_recv()
-
-    def feed_back(ks):
-        blocks = [ahead(k) for k in ks]
+        gather_pass(X_DY, dx, dyf)
+        gather(X_DY, 6, dx, dyf).wait_recv()
+
+    gather_far(X_DY, dx, dyf)
+
+    def feed_back(ds):
+        blocks = [lax.rem(x + d, 4) for d in ds]
         dh = mm_nt(pair(blocks, dyf), wd[...])
         ga, u = pair(blocks, gate), pair(blocks, up)
         s = 1.0 / (1.0 + jnp.exp(-ga))
         dga = (dh * u * (s * (1.0 + ga * (1.0 - s)))).astype(BF)
         du = (dh * (ga * s)).astype(BF)
         result = mm_nt(dga, wgf[...]) + mm_nt(du, wuf[...])
-        for n, (k, b) in enumerate(zip(ks, blocks)):
-            rows, piece = part(128 * b, 128), slice(128 * n, 128 * n + 128)
-            dgu[rows, 0:1024] = dga[piece]
-            dgu[rows, 1024:2048] = du[piece]
-            if k == 0:
-                own[...] = result[piece]
+        for n, (d, b) in enumerate(zip(ds, blocks)):
+            rows, cut = part(128 * b, 128), slice(128 * n, 128 * n + 128)
+            dgu[rows, 0:1024] = dga[cut]
+            dgu[rows, 1024:2048] = du[cut]
+            if d == 0:
+                own[...] = result[cut]
             else:
-                psend[0, b] = result[piece].astype(BF)
-                sum_copy(X_SUM3, k).start()
-
-    for k in (1, 2, 3):
-        sum_copy(X_SUM1, k).wait_send()
+                psend[0, b] = result[cut].astype(BF)
+                for i in {2: (0, 1), 1: (2,), 3: (3,)}[d]:
+                    total(X_SUM3, i).start()
+
+    total_sent(X_SUM1)
     feed_back((2, 1))
     feed_back((3, 0))
+    total_pass(X_SUM3)
 
     def norm_back(value, grad, gain_row):
         r = lax.rsqrt(jnp.mean(value * value, axis=-1, keepdims=True) + EPSILON)
@@ -867,22 +1023,26 @@
         back = r * (t - unit * jnp.mean(t * unit, axis=-1, keepdims=True))
         return back, jnp.sum(grad * unit, axis=0, keepdims=True)
 
-    back, g_mlp = norm_back(mid[...], take(2, X_SUM3), gain_mlp)
+    back, g_mlp = norm_back(mid[...], total_take(X_SUM3), gain_mlp)
     dmid = dyf[my_rows, :].astype(F32) + back
     mid[...] = dmid
     ggain[...] = jnp.zeros_like(ggain)
     ggain[1:2, :] = g_mlp
     dbr[my_rows, :] = dmid.astype(BF)
-    for k in (2, 1, 3):
-        rows_to_all(X_DBR, dbr, k).start()
-
-    def branch(k, carry):
-        b = behind(k)
+    dbr_own = dbr.at[my_rows]
+    gather_start(X_DBR, dbr_own, dbr)
+
+    def branch(n, carry):
+        b = in_order(n)
         rows = part(128 * b, 128)
 
-        @pl.when(k > 0)
+        @pl.when(n == 1)
         def _():
-            rows_to_all(X_DBR, dbr, k).wait_recv()
+            gather_pass(X_DBR, dbr_own, dbr)
+
+        @pl.when(n == 3)
+        def _():
+            gather_far(X_DBR, dbr_own, dbr)
 
         dsend[rows, :] = mm_nt(dbr[rows, :], wop[...]).astype(BF)
         for i in range(4):
@@ -909,6 +1069,13 @@
     lax.fori_loop(1, 16, await_das, 0)
     dk[...] = jnp.zeros_like(dk)
     dv[...] = jnp.zeros_like(dv)
+
+    def grad_place(h):
+        return dqp.at[part(64 * (c // 2), 64), part(512 * lax.rem(c, 2) + 256 * h, 256)]
+
+    def grad_to(e, to):
+        h = e - C_DQ
+        return over_c(e, to, dqs.at[part(64 * to, 64), pl.ds(256 * h, 256)], grad_place(h))
 
     def attend_back(n, carry):
         rows = part(256 * n, 256)
@@ -922,22 +1089,29 @@
             dk[...] += mm(ds, q)
             dq = mm(kt[...], ds).T * SCALE
             dqs[rows, cols] = turn(dq, cos_s[rows, :], -sin_s[rows, :]).astype(BF)
+        for i in range(4):
+            to = 4 * n + i
+
+            @pl.when(to != c)
+            def _(to=to):
+                grad_to(C_DQ, to).start()
+
+            @pl.when(to == c)
+            def _(to=to):
+                grad_place(0)[...] = dqs[part(64 * to, 64), 0:256]
+
         return carry
 
     lax.fori_loop(0, 4, attend_back, 0)
     dqs[:, 256:384] = turn(dk[...] * SCALE, cos_s[...], -sin_s[...]).astype(BF)
     dqs[:, 384:512] = dv[...].astype(BF)
 
-    def dqkv_to(to):
-        place = dqp.at[part(64 * (c // 2), 64), part(512 * lax.rem(c, 2), 512)]
-        return over_c(C_DQKV, to, dqs.at[part(64 * to, 64)], place)
-
-    def send_dqkv(k, carry):
-        dqkv_to(lax.rem(c + k, 16)).start()
-        return carry
-
-    lax.fori_loop(1, 16, send_dqkv, 0)
-    dqp[part(64 * (c // 2), 64), part(512 * lax.rem(c, 2), 512)] = dqs[part(64 * c, 64), :]
+    def send_dkv(k, carry):
+        grad_to(C_DKV, lax.rem(c + k, 16)).start()
+        return carry
+
+    lax.fori_loop(1, 16, send_dkv, 0)
+    grad_place(1)[...] = dqs[part(64 * c, 64), 256:512]
 
     def await_dqkv(b):
         for i in range(4):
@@ -946,27 +1120,34 @@
             @pl.when(to != c)
             def _(to=to, i=i):
                 k = lax.rem(c - to + 16, 16)
-                place = dqp.at[part(64 * (2 * b + i // 2), 64), pl.ds(512 * (i % 2), 512)]
-                remote(place, place, cs.at[C_DQKV, k], cr.at[C_DQKV, k], {"ctx": lax.rem(c + k, 16)}).wait_recv()
-
-    for k in (1, 2, 3):
-        sum_copy(X_SUM2, k).wait_send()
-
-    def input_grad(k, carry):
-        b = lax.rem(x + k, 4)
+                for h in range(2):
+                    place = dqp.at[
+                        part(64 * (2 * b + i // 2), 64), pl.ds(512 * (i % 2) + 256 * h, 256)
+                    ]
+                    e = C_DQ + h
+                    remote(
+                        place, place, cs.at[e, k], cr.at[e, k], {"ctx": lax.rem(c + k, 16)}
+                    ).wait_recv()
+
+    for d in (1, 2, 3):
+        far_copy(d, lax.rem(x + d, 4)).wait_send()
+
+    def input_grad(n, carry):
+        b = far_first(n)
         await_dqkv(b)
-        give(3, X_SUM4, k, b, mm_nt(dqp[part(128 * b, 128), :], wqkv[...]))
-        return carry
-
-    lax.fori_loop(1, 5, input_grad, 0)
-    back, g_attn = norm_back(xall[my_rows, :].astype(F32), take(3, X_SUM4), gain_attn)
+        give(X_SUM4, n, b, mm_nt(dqp[part(128 * b, 128), :], wqkv[...]))
+        return carry
+
+    lax.fori_loop(0, 4, input_grad, 0)
+    back, g_attn = norm_back(xall[my_rows, :].astype(F32), total_take(X_SUM4), gain_attn)
     dx[...] = (mid[...] + back).astype(BF)
     ggain[0:1, :] = g_attn
 
     @pl.when(second)
     def _():
-        for k in range(4):
-            dx_copy(k).start()
+        gather_sent(X_DY, dyin, dyf, forwarded=False)
+        gather(X_DY, 6, dx, dyf).start()
+        gather_start(X_DY, dx, dyf, True)
 
     for n in range(2):
         rows = slice(256 * n, 256 * n + 256)
@@ -989,32 +1170,31 @@
         att_to(to).wait_send()
         place = das.at[part(64 * to, 64)]
         over_c(C_DATT, to, place, place).wait_send()
-        dqkv_to(to).wait_send()
+        grad_to(C_DQ, to).wait_send()
+        grad_to(C_DKV, to).wait_send()
         return carry
 
     lax.fori_loop(1, 16, sent_c, 0)
-    for k in (1, 2, 3):
-        for e in (X_SUM3, X_SUM4):
-            sum_copy(e, k).wait_send()
-        rows_to_all(X_N2, n2, k).wait_send()
-        rows_to_all(X_DBR, dbr, k).wait_send()
+    total_sent(X_SUM3)
+    total_sent(X_SUM4)
+    weight_each(heads + wide, range(15), leave)
+    gather_sent(X_N2, n2_own, n2)
+    gather_sent(X_DBR, dbr_own, dbr)
+    gather_sent(X_IN, xin, xall, started=False)
+    gather_sent(X_DY, dyin, dyf, started=False)
 
     @pl.when(first)
     def _():
-        for k in (1, 2, 3):
-            in_copy(k).wait_send()
-        for k in range(4):
-            out_copy(k).wait_send()
+        gather_sent(X_IN, xin, xall, forwarded=False)
+        gather(X_IN, 6, out, xall).wait_send()
 
     @pl.when(second)
     def _():
-        for k in (1, 2, 3):
-            dy_copy(k).wait_send()
-        for k in range(4):
-            dx_copy(k).wait_send()
-
-
-def run_layer(xin, dyin, pos, freq, gains, wq, wk, wv, wo, wd, wg, wu, cid):
+        gather_sent(X_DY, dyin, dyf, forwarded=False)
+        gather(X_DY, 6, dx, dyf).wait_send()
+
+
+def run_layer(xin, dyin, positions, freq, norm_attn, norm_mlp, wq, wk, wv, wo, wd, wg, wu, cid):
     vm = pl.BlockSpec(memory_space=pltpu.VMEM)
     hbm = pl.BlockSpec(memory_space=pl.ANY)
     dma = pltpu.SemaphoreType.DMA
@@ -1037,7 +1217,11 @@
         ((WIDTH, 1024), BF),
         ((WIDTH, 1024), BF),
         ((512, WIDTH), BF),
+        ((1024, WIDTH), BF),
+        ((2, 2, 64, WIDTH), BF),
         ((512, WIDTH), BF),
+        ((8, 384), F32),
+        ((8, 128), F32),
         ((8, WIDTH), F32),
         ((4, 8, 128), F32),
         ((4, 2, 8, 128), F32),
@@ -1060,7 +1244,8 @@
         ((512, 1024), F32),
         ((128, WIDTH), F32),
         ((2, 4, 128, WIDTH), BF),
-        ((2, 4, 128, WIDTH), BF),
+        ((2, 2, 128, WIDTH), BF),
+        ((3, 128, WIDTH), BF),
         ((512, 512), BF),
         ((1024, 256), BF),
         ((1024, 128), F32),
@@ -1071,15 +1256,15 @@
     return pl.pallas_call(
         layer_kernel,
         out_shape=[jax.ShapeDtypeStruct(s, d) for s, d in shapes],
-        in_specs=[vm] * 10 + [hbm] * 2,
+        in_specs=[vm] * 9 + [hbm] * 4,
         out_specs=[vm] * len(shapes),
         scratch_shapes=[pltpu.VMEM(s, d) for s, d in scratch]
-        + [dma((13, 4)), dma((13, 4)), dma((5, 16)), dma((5, 16)), dma((2, 4)), dma((2, 4))],
+        + [dma((13, 7)), dma((13, 7)), dma((6, 16)), dma((6, 16)), dma((4, 15)), dma((4, 15)), dma((7,)), pltpu.SemaphoreType.REGULAR],
         name="layer",
         compiler_params=pltpu.CompilerParams(
             collective_id=cid, has_side_effects=True, vmem_limit_bytes=63 << 20
         ),
-    )(xin, dyin, pos, freq, gains, wq, wk, wv, wo, wd, wg, wu)
+    )(xin, dyin, positions, freq, norm_attn, norm_mlp, wq, wk, wv, wo, wd, wg, wu)
 
 
 def local(
@@ -1096,18 +1281,17 @@
     w_up,
     w_down,
 ):
-    lane = jnp.arange(128)
-    index = jnp.where(lane < 64, lane, lane - 64)
-    freq = jnp.where(index < 48, THETA ** (-(index.astype(F32) * 2.0 / HEAD_SIZE)), 0.0)
-    freq = jnp.broadcast_to(freq[None], (8, 128))
-    pos = jnp.broadcast_to(positions.reshape(1, 128).astype(F32), (8, 128))
-    gains = jnp.concatenate([norm_attn, norm_mlp, jnp.zeros((6, 384), BF)], axis=0).astype(F32)
+    lane = np.arange(128)
+    index = np.where(lane < 64, lane, lane - 64)
+    freq = np.where(index < 48, THETA ** (-2.0 * index / HEAD_SIZE), 0.0).astype(np.float32)
+    freq = jnp.asarray(np.broadcast_to(freq[None], (8, 128)))
     out, dx, nf, n2, dgu, dqkv, att, dbr, hidden, dyf, ggain = run_layer(
         inputs.reshape(128, WIDTH),
         out_grad.reshape(128, WIDTH),
-        pos,
+        positions,
         freq,
-        gains,
+        norm_attn,
+        norm_mlp,
         w_query[0],
         key_weight[0],
         value_weight[0],

time: 551 us -> 455 us (0.83)
  Pallas kernels: 543 us -> 448 us
    pallas_call x1, Pallas kernels: 386 us -> 291 us  [run_layer(): pl.pallas_call(layer_kernel, out_shape=[jax.ShapeDtypeStruct(s, d) for s,...]
where the time goes in v4:
time: 455 us; the launch traced here: 453 us
  Pallas kernels  448 us (98%)
    pallas_call x1, Pallas kernels, run_layer(): pl.pallas_call(layer_kernel, out_shape=[jax.ShapeDtypeStruct(s, d) for s,...  291 us
    pallas_call x1, Pallas kernels, reduce_grads(): pl.pallas_call(grad_kernel, out_shape=[jax.ShapeDtypeStruct((4, 4) + s, B...  142 us
    pallas_call x1, Pallas kernels, widen(): pl.pallas_call(widen_kernel, grid=(steps,), out_shape=[shape(384, FF), sh...  14.6 us

profile of v4, /device:TPU:0, one launch (start us, length us, event | category | flops | bytes accessed | tf_op | source)
XLA Modules:
  0.0 452.9 jit_solution(14998315701443518673)
XLA Ops:
  0.6 1.3 jit_solution_.3.freq
  1.9 291.3 %layer.1 = (bf16[128,1536]{1,0:T(8,128)(2,1)}, bf16[128,1536]{1,0:T(8,128)(2,1)}, bf16[512,1536]{1,0:T(8,128)(2,1)}, bf16[512,1536]{1,0:T(8,128)(2,1)}, bf16[512...) custom-call(bf16[128,1536]{1,0:T(8,128)(2,1)} %bitcast.27, ...), custom_call_target="tpu_custom_call" | custom-call | tf_op jit(solution)/shard_map/layer/pallas_call | solution.py:1256
  293.2 142.3 %reduce_grads.1 = (bf16[4,4,96,1024]{3,2,1,0:T(8,128)(2,1)}, bf16[4,4,96,1024]{3,2,1,0:T(8,128)(2,1)}, bf16[4,4,64,1536]{3,2,1,0:T(8,128)(2,1)}, bf16[4,4,96,768...) custom-call(bf16[512,1536]{1,0:T(8,128)(2,1)} %get-tuple-element.37.n2, ...), custom_call_target="tpu_custom_call" | custom-call | tf_op jit(solution)/shard_map/reduce_grads/pallas_call | solution.py:297
  435.4 1.4 fusion
  436.8 0.0 copy-start.1
  436.8 0.0 copy-start
  436.8 14.6 %widen.1 = (f32[384,4096]{1,0:T(8,128)}, f32[384,4096]{1,0:T(8,128)}, f32[384,1536]{1,0:T(8,128)}, f32[384,768]{1,0:T(8,128)}, f32[384,768]{1,0:T(8,128)}, /*index=5*/f32[384,1536]{1,0:T(8,128)}, f32[1024,1536]{1,0:T(8,128)}) custom-call(bf16[4,4,96,1024]{3,2,1,0:T(8,128)(2,1)} %get-tuple-element.47.w_gate, bf16[4,4,96,1024]{3,2,1,0:T(8,128)(2,1)} %get-tuple-element.48.w_up, ...), custom_call_target="tpu_custom_call" | custom-call | tf_op jit(solution)/shard_map/widen/pallas_call | solution.py:350
  451.4 0.0 copy-done.1
  451.4 0.7 copy.26
  452.1 0.0 copy-done
  452.1 0.7 copy.27
Async XLA Ops:
  436.8 14.6 %copy-start.1 = (bf16[128,1536]{1,0:T(8,128)(2,1)S(1)}, bf16[128,1536]{1,0:T(8,128)(2,1)}, u32[]{:S(2)}) copy-start(bf16[128,1536]{1,0:T(8,128)(2,1)} %get-tuple-element.35) | copy-start | bytes 1179652
  436.8 15.3 %copy-start = (bf16[128,1536]{1,0:T(8,128)(2,1)S(1)}, bf16[128,1536]{1,0:T(8,128)(2,1)}, u32[]{:S(2)}) copy-start(bf16[128,1536]{1,0:T(8,128)(2,1)} %get-tuple-element.36) | copy-start | bytes 1179652

commit v5 on v4

--- a/solution.py
+++ b/solution.py
@@ -42,300 +42,24 @@
     return pl.ds(pl.multiple_of(start, size), size)
 
 
-GRADS = {"gate": (96, 1024), "up": (96, 1024), "down": (64, 1536), "qkv": (96, 768), "out": (96, 384)}
-RINGS = {"gate": ("y", 1), "up": ("y", -1), "down": ("z", 1), "qkv": ("z", -1), "out": ("z", -1)}
-
-
-def grad_kernel(n2, nf, dgu, dqkv, att, dbr, hidden, dyf, gains, *refs):
-    names = list(GRADS)
-    held = dict(zip(names, refs[:5]))
-    o_gain = refs[5]
-    own = dict(zip(names, refs[6:11]))
-    first = dict(zip(names, refs[11:16]))
-    second = dict(zip(names, refs[16:21]))
-    gain_in, send, recv, local_sem, send_g, recv_g = refs[21:]
-    x = lax.axis_index("fsdp")
-    c = lax.axis_index("ctx")
-    y, z = lax.rem(c, 4), c // 4
-    where = {"x": x, "y": y, "z": z}
-
-    def near(axis, step):
-        if axis == "x":
-            return {"fsdp": lax.rem(x + step + 4, 4)}
-        if axis == "y":
-            return {"ctx": 4 * z + lax.rem(y + step + 4, 4)}
-        return {"ctx": 4 * lax.rem(z + step + 4, 4) + y}
-
-    mirror = {"y": {"fsdp": y, "ctx": 4 * z + x}, "z": {"fsdp": z, "ctx": 4 * x + y}}
-
-    barrier = pltpu.get_barrier_semaphore()
-    for axis in "xyz":
-        for step in (1, 2, 3):
-            pl.semaphore_signal(barrier, inc=1, device_id=near(axis, step), device_id_type=MESH)
-    for axis in "yz":
-        pl.semaphore_signal(barrier, inc=1, device_id=mirror[axis], device_id_type=MESH)
-    pl.semaphore_wait(barrier, 11)
-
-    def ring(name):
-        axis, d = RINGS[name]
-        other = "z" if axis == "y" else "y"
-        return names.index(name), axis, other, d, where[axis], where[other]
-
-    def at(i, d, s):
-        return lax.rem(i - d * s + 8, 4)
-
-    def copy_first(name, s, q):
-        f, axis, other, d, i, j = ring(name)
-        p = at(j, d, 1 + q)
-        return remote(
-            own[name].at[at(i, d, 1 + s), p],
-            first[name].at[s, p],
-            send.at[f, 4 * s + q],
-            recv.at[f, 4 * s + q],
-            near(axis, d),
-        )
-
-    def copy_second(name, s):
-        f, axis, other, d, i, j = ring(name)
-        return remote(
-            own[name].at[i, at(j, d, 1 + s)],
-            second[name].at[s],
-            send.at[f, 12 + s],
-            recv.at[f, 12 + s],
-            near(other, d),
-        )
-
-    def copy_mirror(name):
-        f, axis, other, d, i, j = ring(name)
-        return remote(
-            own[name].at[i, j], held[name].at[x, j], send.at[f, 15], recv.at[f, 15], mirror[axis]
-        )
-
-    def copy_own(name):
-        f, axis, other, d, i, j = ring(name)
-        group = x if name in ("gate", "up", "qkv") else i
-        return pltpu.make_async_copy(own[name].at[i, j], held[name].at[group, j], local_sem.at[f])
-
-    def copy_small(name, s):
-        f, axis, other, d, i, j = ring(name)
-        place = held[name].at[i, at(j, d, s)]
-        return remote(place, place, send.at[f, 16 + s], recv.at[f, 16 + s], near(other, d))
-
-    def copy_big(name, s, q):
-        f, axis, other, d, i, j = ring(name)
-        place = held[name].at[at(i, d, s), at(j, d, q)]
-        n = 20 + 4 * s + q
-        return remote(place, place, send.at[f, n], recv.at[f, n], near(axis, d))
-
-    def gain_copy(n, k):
-        axis = "xyz"[n]
-        if n == 0:
-            src = gains.at[:, part(lax.rem(x + k, 4) * 384, 384)]
-        else:
-            src = gain_in.at[n, 0]
-        return remote(src, gain_in.at[n, k], send_g.at[n, k], recv_g.at[n, k], near(axis, k))
-
-    def gain_start(n):
-        for k in (1, 2, 3):
-            gain_copy(n, k).start()
-
-    def gain_sum(n):
-        mine = gains[:, part(x * 384, 384)] if n == 0 else gain_in[n, 0]
-        for k in (1, 2, 3):
-            gain_copy(n, k).wait()
-        return mine + gain_in[n, 1] + gain_in[n, 2] + gain_in[n, 3]
-
-    gain_start(0)
-
-    total = mm_tn(att[...], dbr[...]).astype(BF)
-    for g in range(4):
-        for p in range(4):
-            own["out"][g, p] = total[96 * g : 96 * g + 96, 384 * p : 384 * p + 384]
-
-    def compute(s, carry):
-        def group(name):
-            f, axis, other, d, i, j = ring(name)
-            return at(i, d, 1 + s)
-
-        g = group("gate")
-        own["gate"][g] = mm_tn(n2[:, part(g * 384, 384)], dgu[:, :1024]).astype(BF).reshape(4, 96, 1024)
-        g = group("up")
-        own["up"][g] = mm_tn(n2[:, part(g * 384, 384)], dgu[:, 1024:]).astype(BF).reshape(4, 96, 1024)
-        g = group("down")
-        own["down"][g] = mm_tn(hidden[:, part(g * 256, 256)], dyf[...]).astype(BF).reshape(4, 64, 1536)
-        g = group("qkv")
-        own["qkv"][g] = mm_tn(nf[:, part(g * 384, 384)], dqkv[...]).astype(BF).reshape(4, 96, 768)
-
-        @pl.when(s == 0)
-        def _():
-            for q in range(4):
-                for name in names:
-                    copy_first(name, 0, q).start()
-
-        return carry
-
-    lax.fori_loop(0, 4, compute, 0)
-    gain_in[1, 0] = gain_sum(0)
-    gain_start(1)
-
-    def add_first(t, carry):
-        s, q = t // 4, lax.rem(t, 4)
-        for name in names:
-            f, axis, other, d, i, j = ring(name)
-            copy_first(name, s, q).wait_recv()
-            g, p = at(i, d, 2 + s), at(j, d, 1 + q)
-            own[name][g, p] = own[name][g, p] + first[name][s, p]
-
-            @pl.when(s < 2)
-            def _(name=name):
-                copy_first(name, s + 1, q).start()
-
-            @pl.when(t == 8)
-            def _(name=name):
-                copy_second(name, 0).start()
-
-        return carry
-
-    lax.fori_loop(0, 12, add_first, 0)
-    gain_in[2, 0] = gain_sum(1)
-    gain_start(2)
-
-    def add_second(s, carry):
-        for name in names:
-            f, axis, other, d, i, j = ring(name)
-            copy_second(name, s).wait_recv()
-            p = at(j, d, 2 + s)
-            own[name][i, p] = own[name][i, p] + second[name][s]
-
-            @pl.when(s < 2)
-            def _(name=name):
-                copy_second(name, s + 1).start()
-
-        return carry
-
-    lax.fori_loop(0, 3, add_second, 0)
-
-    for name in ("gate", "up", "qkv"):
-        axis = RINGS[name][0]
-
-        @pl.when(where[axis] != x)
-        def _(name=name):
-            copy_mirror(name).start()
-
-        @pl.when(where[axis] == x)
-        def _(name=name):
-            copy_own(name).start()
-
-    for name in ("down", "out"):
-        copy_own(name).start()
-    for name in ("down", "out"):
-        copy_own(name).wait()
-    for name in ("gate", "up", "qkv"):
-        axis = RINGS[name][0]
-
-        @pl.when(where[axis] != x)
-        def _(name=name):
-            copy_mirror(name).wait()
-
-        @pl.when(where[axis] == x)
-        def _(name=name):
-            copy_own(name).wait()
-
-    def hand_small(q, carry):
-        for name in names:
-
-            @pl.when(q > 0)
-            def _(name=name):
-                copy_small(name, q - 1).wait_recv()
-
-            @pl.when(q < 3)
-            def _(name=name):
-                copy_small(name, q).start()
-
-            copy_big(name, 0, q).start()
-        return carry
-
-    lax.fori_loop(0, 4, hand_small, 0)
-
-    def hand_big(t, carry):
-        s, q = t // 4, lax.rem(t, 4)
-        for name in names:
-            copy_big(name, s, q).wait_recv()
-
-            @pl.when(s < 2)
-            def _(name=name):
-                copy_big(name, s + 1, q).start()
-
-        return carry
-
-    lax.fori_loop(0, 12, hand_big, 0)
-    o_gain[...] = gain_sum(2)
-
-    def sent(t, carry):
-        s, q = t // 4, lax.rem(t, 4)
-        for name in names:
-            copy_first(name, s, q).wait_send()
-            copy_big(name, s, q).wait_send()
-        return carry
-
-    lax.fori_loop(0, 12, sent, 0)
-
-    def sent_small(s, carry):
-        for name in names:
-            copy_second(name, s).wait_send()
-            copy_small(name, s).wait_send()
-        return carry
-
-    lax.fori_loop(0, 3, sent_small, 0)
-
-
-def reduce_grads(n2, nf, dgu, dqkv, att, dbr, hidden, dyf, gains, cid):
-    vm = pl.BlockSpec(memory_space=pltpu.VMEM)
-    hbm = pl.BlockSpec(memory_space=pl.ANY)
-    dma = pltpu.SemaphoreType.DMA
-    sizes = list(GRADS.values())
-    return pl.pallas_call(
-        grad_kernel,
-        out_shape=[jax.ShapeDtypeStruct((4, 4) + s, BF) for s in sizes]
-        + [jax.ShapeDtypeStruct((8, 384), F32)],
-        in_specs=[vm] * 9,
-        out_specs=[hbm] * 5 + [vm],
-        scratch_shapes=[pltpu.VMEM((4, 4) + s, BF) for s in sizes]
-        + [pltpu.VMEM((3, 4) + s, BF) for s in sizes]
-        + [pltpu.VMEM((3,) + s, BF) for s in sizes]
-        + [
-            pltpu.VMEM((3, 4, 8, 384), F32),
-            dma((5, 32)),
-            dma((5, 32)),
-            dma((5,)),
-            dma((3, 4)),
-            dma((3, 4)),
-        ],
-        name="reduce_grads",
-        compiler_params=pltpu.CompilerParams(
-            collective_id=cid, has_side_effects=True, vmem_limit_bytes=60 << 20
-        ),
-    )(n2, nf, dgu, dqkv, att, dbr, hidden, dyf, gains)
-
-
-def widen_kernel(w_gate, w_up, w_down, w_qkv, w_out, gate, up, query, key, value, g_out, g_down):
+def widen_kernel(w_gate, w_up, w_down, w_out, w_a, w_b, gains, gate, up, query, key, value, g_out, g_down, g_attn, g_mlp):
+    g_attn[...] = gains[0:1, :]
+    g_mlp[...] = gains[1:2, :]
     g_down[...] = w_down[...].astype(F32)
     keys, values = [], []
     for x in range(N_X):
         gate[:, 1024 * x : 1024 * x + 1024] = w_gate[x, 0].astype(F32)
         up[:, 1024 * x : 1024 * x + 1024] = w_up[x, 0].astype(F32)
         g_out[:, 384 * x : 384 * x + 384] = w_out[0, x].astype(F32)
-        heads = w_qkv[x, 0].astype(F32)
-        query[:, 384 * x : 384 * x + 384] = jnp.concatenate(
-            [heads[:, :192], heads[:, 384:576]], axis=1
-        )
-        keys += [heads[:, 192:288], heads[:, 576:672]]
-        values += [heads[:, 288:384], heads[:, 672:768]]
+        a, b = w_a[x, 0].astype(F32), w_b[x, 0].astype(F32)
+        query[:, 384 * x : 384 * x + 384] = jnp.concatenate([a[:, :192], b[:, :192]], axis=1)
+        keys += [a[:, 192:288], b[:, 192:288]]
+        values += [a[:, 288:], b[:, 288:]]
     key[...] = jnp.concatenate(keys, axis=1)
     value[...] = jnp.concatenate(values, axis=1)
 
 
-def widen(gate, up, down, qkv, out):
+def widen(gate, up, down, out, heads_a, heads_b, gains):
     steps = 8
 
     def spec(r, cols):
@@ -358,13 +82,17 @@
             shape(384, 768),
             shape(384, 1536),
             shape(1024, 1536),
+            shape(1, 384),
+            shape(1, 384),
         ],
         in_specs=[
             blocks(1024),
             blocks(1024),
             spec(128, 1536),
-            blocks(768),
             pl.BlockSpec((1, 4, 48, 384), lambda i: (i // 2, 0, i % 2, 0)),
+            blocks(384),
+            blocks(384),
+            pl.BlockSpec((8, 384), lambda i: (0, 0)),
         ],
         out_specs=[
             spec(48, FF),
@@ -374,15 +102,28 @@
             spec(48, 768),
             spec(48, 1536),
             spec(128, 1536),
+            pl.BlockSpec((1, 384), lambda i: (0, 0)),
+            pl.BlockSpec((1, 384), lambda i: (0, 0)),
         ],
         name="widen",
         compiler_params=pltpu.CompilerParams(vmem_limit_bytes=60 << 20),
-    )(gate, up, down.reshape(1024, 1536), qkv, out)
+    )(gate, up, down.reshape(1024, 1536), out, heads_a, heads_b, gains)
 
 
 X_GAIN, X_POS, X_IN, X_DY, X_QKV, X_GATE, X_UP, X_SUM1, X_N2, X_SUM2, X_SUM3, X_DBR, X_SUM4 = range(13)
 C_POS, C_QKV, C_ATT, C_DATT, C_DQ, C_DKV = range(6)
 SCALE = HEAD_SIZE ** (-0.5)
+FLOWS = {
+    "gate": ("y", 1, 96, 1024),
+    "up": ("y", -1, 96, 1024),
+    "down": ("z", 1, 64, 1536),
+    "out": ("z", -1, 96, 384),
+    "heads_a": ("y", 1, 96, 384),
+    "heads_b": ("z", -1, 96, 384),
+}
+NAMES = list(FLOWS)
+EARLY, LATE = NAMES[:4], NAMES[4:]
+SMALL = NAMES[3:]
 
 
 def spread(w, heads):
@@ -420,15 +161,29 @@
     wu,
     out,
     dx,
+    h_gate,
+    h_up,
+    h_down,
+    h_out,
+    h_heads_a,
+    h_heads_b,
+    o_gain,
     nf,
-    n2,
+    rows2,
     dgu,
     dqkv,
     att,
     dbr,
     hidden,
-    dyf,
     ggain,
+    arrive_down,
+    arrive_out,
+    arrive_a,
+    arrive_b,
+    second_out,
+    second_a,
+    second_b,
+    gain_in,
     wsend,
     wqkv,
     wgf,
@@ -477,6 +232,11 @@
     wr,
     ls,
     go,
+    fs,
+    fr,
+    gs,
+    gr,
+    os,
 ):
     section = lax.axis_index("section")
     x = lax.axis_index("fsdp")
@@ -484,6 +244,17 @@
     y, z = lax.rem(c, 4), c // 4
     first, second = section == 0, section == 1
     my_rows = part(128 * x, 128)
+    n2, dyf = rows2.at[0], rows2.at[1]
+    where = {"x": x, "y": y, "z": z}
+
+    def near(axis, step):
+        if axis == "x":
+            return {"fsdp": lax.rem(x + step + 4, 4)}
+        if axis == "y":
+            return {"ctx": 4 * z + lax.rem(y + step + 4, 4)}
+        return {"ctx": 4 * lax.rem(z + step + 4, 4) + y}
+
+    mirror = {"y": {"fsdp": y, "ctx": 4 * z + x}, "z": {"fsdp": z, "ctx": 4 * x + y}}
 
     barrier = pltpu.get_barrier_semaphore()
     for k in range(1, 4):
@@ -505,7 +276,9 @@
         return carry
 
     lax.fori_loop(1, 16, greet, 0)
-    pl.semaphore_wait(barrier, 22)
+    for axis in "yz":
+        pl.semaphore_signal(barrier, inc=1, device_id=mirror[axis], device_id_type=MESH)
+    pl.semaphore_wait(barrier, 24)
 
     def ahead(k):
         return lax.rem(x + k, 4)
@@ -617,6 +390,13 @@
             device = {"ctx": 4 * r + y if n % 2 == 0 else 4 * z + r}
         return remote(src, place, ws.at[n, i], wr.at[n, i], device)
 
+    def fetch_to(n, b):
+        i, q = lax.rem(b - x + 3, 4), quarter(n)
+        cols = pl.ds(512 * n, 512)
+        rows = pl.ds(pl.multiple_of(384 * x + 96 * q, 96), 96)
+        src = wsend.at[b, part(96 * q, 96), cols]
+        return remote(src, wqkv.at[rows, cols], ws.at[n, i], wr.at[n, i], {"fsdp": b})
+
     def weight_each(which, items, act):
         for i in items:
             for n in which:
@@ -667,11 +447,6 @@
         gain_copy(k).start()
     gain[:, part(384 * x, 384)] = gains[...]
     posx[x] = pos[...]
-
-    @pl.when(first)
-    def _():
-        gather_start(X_IN, xin, xall)
-        xall[my_rows, :] = xin[...]
 
     def local_copies():
         yield pltpu.make_async_copy(
@@ -686,24 +461,41 @@
                 wo_in.at[pl.ds(96 * h, 96)], wop.at[pl.ds(128 * h, 96)], ls.at[3 + h]
             )
 
+    def head_columns(b, j, rows):
+        w_q = wq[rows, 384 * b + 192 * j : 384 * b + 192 * j + 192]
+        w_k = wk[rows, 96 * (2 * b + j) : 96 * (2 * b + j) + 96]
+        w_v = wv[rows, 96 * (2 * b + j) : 96 * (2 * b + j) + 96]
+        blank = jnp.zeros((w_v.shape[0], 32), BF)
+        return jnp.concatenate(spread(w_q, (0, 1)) + spread(w_k, (0,)) + [w_v, blank], axis=1)
+
     for b in range(4):
-        pieces = []
-        for j in range(2):
-            pieces += spread(wq[:, 384 * b + 192 * j : 384 * b + 192 * j + 192], (0, 1))
-            pieces += spread(wk[:, 96 * (2 * b + j) : 96 * (2 * b + j) + 96], (0,))
-            pieces += [
-                wv[:, 96 * (2 * b + j) : 96 * (2 * b + j) + 96],
-                jnp.zeros((384, 32), BF),
-            ]
-        wsend[b] = jnp.concatenate(pieces, axis=1)
+
+        @pl.when(b != x)
+        def _(b=b):
+            for j in heads:
+                rows = part(96 * quarter(j), 96)
+                wsend[b, rows, 512 * j : 512 * j + 512] = head_columns(b, j, rows)
+
+                @pl.when(first)
+                def _(j=j):
+                    fetch_to(j, b).start()
 
     @pl.when(first)
     def _():
-        weight_fetch(heads)
+        gather_start(X_IN, xin, xall)
+        xall[my_rows, :] = xin[...]
+
+    for b in range(4):
+
+        @pl.when(b == x)
+        def _(b=b):
+            for j in heads:
+                wqkv[384 * b : 384 * b + 384, 512 * j : 512 * j + 512] = head_columns(
+                    b, j, slice(0, 384)
+                )
 
     for copy in local_copies():
         copy.start()
-    wqkv[part(384 * x, 384), :] = wsend[x]
     for h in range(4):
         wop[128 * h + 96 : 128 * h + 128, :] = jnp.zeros((32, WIDTH), BF)
 
@@ -725,34 +517,37 @@
 
     lax.fori_loop(1, 16, send_pos, 0)
     posc[c] = posv[c // 4, lax.rem(c, 4) // 2]
+
+    @pl.when(first)
+    def _():
+        weight_share(heads)
+
     for b in range(4):
         angle = as_column(posx[b][0:1, :]) * freq[0:1, :]
         cos_c[128 * b : 128 * b + 128, :] = jnp.cos(angle)
         sin_c[128 * b : 128 * b + 128, :] = jnp.sin(angle) * sign
 
-    def await_pos(k, carry):
-        pos_to(lax.rem(c + k, 16)).wait()
-        return carry
-
-    lax.fori_loop(1, 16, await_pos, 0)
-
-    def tables(i, carry):
-        row = jnp.where(lane < 64, posc[2 * i][0:1, :], pltpu.roll(posc[2 * i + 1], 64, 1)[0:1, :])
-        block = part(128 * i, 128)
-        posr[0:1, block] = row
-        column = as_column(row)
-        posk[block, :] = jnp.broadcast_to(column, (128, 128))
-        angle = column * freq[0:1, :]
-        cos_s[block, :] = jnp.cos(angle)
-        sin_s[block, :] = jnp.sin(angle) * sign
-        return carry
-
-    @pl.when(first)
-    def _():
-        weight_share(heads)
-        weight_fetch(wide)
-
-    lax.fori_loop(0, 8, tables, 0)
+    def tables():
+        def await_pos(k, carry):
+            pos_to(lax.rem(c + k, 16)).wait()
+            return carry
+
+        def table(i, carry):
+            row = jnp.where(
+                lane < 64, posc[2 * i][0:1, :], pltpu.roll(posc[2 * i + 1], 64, 1)[0:1, :]
+            )
+            block = part(128 * i, 128)
+            posr[0:1, block] = row
+            column = as_column(row)
+            posk[block, :] = jnp.broadcast_to(column, (128, 128))
+            angle = column * freq[0:1, :]
+            cos_s[block, :] = jnp.cos(angle)
+            sin_s[block, :] = jnp.sin(angle) * sign
+            return carry
+
+        lax.fori_loop(1, 16, await_pos, 0)
+        lax.fori_loop(0, 8, table, 0)
+
     for k in (1, 3, 2):
         gain_copy(k).wait()
 
@@ -760,12 +555,12 @@
     def _():
         weight_pass(heads)
         gather_pass(X_IN, xin, xall)
-        gather_far(X_IN, xin, xall)
+        weight_fetch(wide)
         weight_wait(heads)
-        pl.semaphore_signal(go, inc=1, device_id={"section": 1}, device_id_type=MESH)
 
     @pl.when(second)
     def _():
+        tables()
         gather_start(X_DY, dyin, dyf)
         dyf[my_rows, :] = dyin[...]
         gather_pass(X_DY, dyin, dyf)
@@ -796,7 +591,7 @@
         def _():
             gather_pass(X_IN, xin, xall)
 
-        @pl.when(jnp.logical_and(second, n == 3))
+        @pl.when(n == 3)
         def _():
             gather_far(X_IN, xin, xall)
 
@@ -832,7 +627,9 @@
 
     @pl.when(first)
     def _():
-        weight_share(wide)
+        tables()
+
+    weight_each(heads, range(3), leave)
 
 
     def await_qkv(k, carry):
@@ -841,6 +638,11 @@
         return carry
 
     lax.fori_loop(1, 16, await_qkv, 0)
+
+    @pl.when(first)
+    def _():
+        weight_share(wide)
+        pl.semaphore_signal(go, inc=1, device_id={"section": 1}, device_id_type=MESH)
 
     vt[...] = qs[:, 384:512].T
     kt[...] = qs[:, 256:384].T
@@ -883,6 +685,11 @@
 
     lax.fori_loop(0, 4, attend, 0)
 
+    @pl.when(first)
+    def _():
+        weight_pass(wide)
+
+
     def await_att(b):
         for i in range(4):
             to = 4 * b + i
@@ -926,10 +733,6 @@
         await_att(b)
         give(X_SUM1, n, b, mm(attp[part(128 * b, 128), :], wop[...]))
         return carry
-
-    @pl.when(first)
-    def _():
-        weight_pass(wide)
 
     for copy in local_copies():
         copy.wait()
@@ -960,8 +763,8 @@
         result = mm(h, wd[...])
         for n, (d, b) in enumerate(zip(ds, blocks)):
             rows, cut = part(128 * b, 128), slice(128 * n, 128 * n + 128)
-            gate[rows, :] = ga[cut]
-            up[rows, :] = u[cut]
+            gate[rows, :] = ga[cut].astype(BF)
+            up[rows, :] = u[cut].astype(BF)
             hidden[rows, :] = h[cut]
             if d == 0:
                 own[...] = result[cut]
@@ -985,6 +788,234 @@
         gather(X_IN, 6, out, xall).start()
         gather_start(X_IN, out, xall, True)
 
+    held = dict(zip(NAMES, (h_gate, h_up, h_down, h_out, h_heads_a, h_heads_b)))
+
+    def ring(name):
+        axis, d, _, _ = FLOWS[name]
+        other = "z" if axis == "y" else "y"
+        return NAMES.index(name), axis, other, d, where[axis], where[other]
+
+    def at(i, d, s):
+        return lax.rem(i - d * s + 8, 4)
+
+    def partial(name, g, p):
+        if name == "down":
+            return wd.at[part(256 * g + 64 * p, 64)]
+        if name == "out":
+            return wop.at[part(96 * g, 96), part(384 * p, 384)]
+        rows = pl.ds(pl.multiple_of(384 * g + 96 * p, 96), 96)
+        if name in LATE:
+            return wqkv.at[rows, pl.ds(384 * LATE.index(name), 384)]
+        return (wgf if name == "gate" else wuf).at[rows]
+
+    def arrival(name, s, q):
+        n = 4 * (s - 1) + q
+        if name == "gate":
+            return wsend.at[s, part(96 * q, 96)]
+        if name == "up":
+            return wsend.at[3, part(96 * q, 96)] if s == 0 else dgu.at[part(96 * n, 96)]
+        if name == "down":
+            return arrive_down.at[q] if s == 0 else n2.at[part(64 * n, 64)]
+        return arrive_out.at[s, q]
+
+    def arrival2(name, s):
+        if name in ("gate", "up"):
+            return (gate if name == "gate" else up).at[part(96 * s, 96)]
+        if name == "down":
+            return prec3.at[s, pl.ds(0, 64)]
+        return (second_out, second_a, second_b)[SMALL.index(name)].at[s]
+
+    def flow(name, n, src, dst, device):
+        f = NAMES.index(name)
+        return remote(src, dst, fs.at[f, n], fr.at[f, n], device)
+
+    def copy_first(name, s, q):
+        f, axis, other, d, i, j = ring(name)
+        src = partial(name, at(i, d, 1 + s), at(j, d, 1 + q))
+        return flow(name, 4 * s + q, src, arrival(name, s, q), near(axis, d))
+
+    def copy_second(name, s):
+        f, axis, other, d, i, j = ring(name)
+        src = partial(name, i, at(j, d, 1 + s))
+        return flow(name, 12 + s, src, arrival2(name, s), near(other, d))
+
+    def copy_mirror(name):
+        f, axis, other, d, i, j = ring(name)
+        n = 6 if name in LATE else 15
+        return flow(name, n, partial(name, i, j), held[name].at[x, j], mirror[axis])
+
+    def copy_own(name):
+        f, axis, other, d, i, j = ring(name)
+        group = i if name in ("down", "out") else x
+        return pltpu.make_async_copy(partial(name, i, j), held[name].at[group, j], os.at[f])
+
+    def copy_small(name, s):
+        f, axis, other, d, i, j = ring(name)
+        place = held[name].at[i, at(j, d, s)]
+        return flow(name, 16 + s, place, place, near(other, d))
+
+    def copy_big(name, s, q):
+        f, axis, other, d, i, j = ring(name)
+        place = held[name].at[at(i, d, s), at(j, d, q)]
+        return flow(name, 20 + 4 * s + q, place, place, near(axis, d))
+
+    def first_start(names):
+        def body(q, carry):
+            for name in names:
+                copy_first(name, 0, q).start()
+            return carry
+
+        lax.fori_loop(0, 4, body, 0)
+
+    def first_step(names, s):
+        def body(q, carry):
+            for name in names:
+                f, axis, other, d, i, j = ring(name)
+                copy_first(name, s, q).wait_recv()
+                place = partial(name, at(i, d, 2 + s), at(j, d, 1 + q))
+                place[...] = place[...] + arrival(name, s, q)[...]
+                if s < 2:
+                    copy_first(name, s + 1, q).start()
+                else:
+
+                    @pl.when(q == 0)
+                    def _(name=name):
+                        copy_second(name, 0).start()
+
+            return carry
+
+        lax.fori_loop(0, 4, body, 0)
+
+    def second_step(names, s):
+        for name in names:
+            f, axis, other, d, i, j = ring(name)
+            copy_second(name, s).wait_recv()
+            place = partial(name, i, at(j, d, 2 + s))
+            place[...] = place[...] + arrival2(name, s)[...]
+            if s < 2:
+                copy_second(name, s + 1).start()
+
+    def mirror_step(names, act):
+        for name in names:
+            if name in ("down", "out"):
+                act(copy_own(name))
+                continue
+            axis = FLOWS[name][0]
+
+            @pl.when(where[axis] != x)
+            def _(name=name):
+                act(copy_mirror(name))
+
+            @pl.when(where[axis] == x)
+            def _(name=name):
+                act(copy_own(name))
+
+    def finish_copy(copy):
+        copy.wait()
+
+    def small_step(names, q):
+        for name in names:
+            if q > 0:
+                copy_small(name, q - 1).wait_recv()
+            if q < 3:
+                copy_small(name, q).start()
+        for name in names:
+            copy_big(name, 0, q).start()
+
+    def big_step(names, s, low, high):
+        def body(q, carry):
+            for name in names:
+                copy_big(name, s, q).wait_recv()
+                if s < 2:
+                    copy_big(name, s + 1, q).start()
+            return carry
+
+        lax.fori_loop(low, high, body, 0)
+
+    def gain_sum_copy(n, k):
+        axis = "xyz"[n]
+        if n == 0:
+            src = ggain.at[:, part(lax.rem(x + k, 4) * 384, 384)]
+        else:
+            src = gain_in.at[n, 0]
+        return remote(src, gain_in.at[n, k], gs.at[n, k], gr.at[n, k], near(axis, k))
+
+    def gain_start(n):
+        for k in (1, 2, 3):
+            gain_sum_copy(n, k).start()
+
+    def gain_sum(n):
+        mine = ggain[:, part(x * 384, 384)] if n == 0 else gain_in[n, 0]
+        for k in (1, 2, 3):
+            gain_sum_copy(n, k).wait()
+        return mine + gain_in[n, 1] + gain_in[n, 2] + gain_in[n, 3]
+
+    def late(name, n):
+        f, axis, other, d, i, j = ring(name)
+        cols = pl.ds(384 * LATE.index(name), 384)
+        k = (n if n < 6 else n - 1) % 3 + 1
+        if n < 3:
+            src = wqkv.at[part(384 * lax.rem(i + k, 4), 384), cols]
+            return flow(name, n, src, (arrive_a, arrive_b)[f - 4].at[k - 1], near(axis, k))
+        if n < 6:
+            src = partial(name, i, lax.rem(j + k, 4))
+            return flow(name, n, src, arrival2(name, k - 1), near(other, k))
+        if n < 10:
+            place = held[name].at[i, j]
+            return flow(name, n, place, place, near(other, k))
+        place = held[name].at[i]
+        return flow(name, n, place, place, near(axis, k))
+
+    def late_each(items, act):
+        for n in items:
+            for name in LATE:
+                act(late(name, n))
+
+    def late_first():
+        late_each(range(3), arrive)
+        for name in LATE:
+            f, axis, other, d, i, j = ring(name)
+            rows, cols = part(384 * i, 384), pl.ds(384 * LATE.index(name), 384)
+            got = (arrive_a, arrive_b)[f - 4]
+            sums = wqkv[rows, cols].astype(F32)
+            for k in range(3):
+                sums = sums + got[k].astype(F32)
+            wqkv[rows, cols] = sums.astype(BF)
+        late_each(range(3, 6), begin)
+
+    def late_second():
+        late_each(range(3, 6), arrive)
+        for name in LATE:
+            f, axis, other, d, i, j = ring(name)
+            place = partial(name, i, j)
+            sums = place[...].astype(F32)
+            for k in range(3):
+                sums = sums + arrival2(name, k)[...].astype(F32)
+            place[...] = sums.astype(BF)
+        mirror_step(LATE, begin)
+
+    def late_small():
+        mirror_step(LATE, finish_copy)
+        late_each(range(7, 10), begin)
+
+    def late_big():
+        late_each(range(7, 10), arrive)
+        late_each(range(10, 13), begin)
+
+    def feed_grads(s, carry):
+        rows = part(384 * at(y, 1, 1 + s), 384)
+        wgf[rows, :] = mm_tn(n2[:, rows], dgu[0:512, :]).astype(BF)
+        rows = part(384 * at(y, -1, 1 + s), 384)
+        wuf[rows, :] = mm_tn(n2[:, rows], dgu[512:1024, :]).astype(BF)
+        rows = part(256 * at(z, 1, 1 + s), 256)
+        wd[rows, :] = mm_tn(hidden[:, rows], dyf[...]).astype(BF)
+
+        @pl.when(s == 0)
+        def _():
+            first_start(EARLY[:3])
+
+        return carry
+
     @pl.when(first)
     def _():
         gather_pass(X_DY, dx, dyf)
@@ -995,15 +1026,15 @@
     def feed_back(ds):
         blocks = [lax.rem(x + d, 4) for d in ds]
         dh = mm_nt(pair(blocks, dyf), wd[...])
-        ga, u = pair(blocks, gate), pair(blocks, up)
+        ga, u = pair(blocks, gate).astype(F32), pair(blocks, up).astype(F32)
         s = 1.0 / (1.0 + jnp.exp(-ga))
         dga = (dh * u * (s * (1.0 + ga * (1.0 - s)))).astype(BF)
         du = (dh * (ga * s)).astype(BF)
         result = mm_nt(dga, wgf[...]) + mm_nt(du, wuf[...])
         for n, (d, b) in enumerate(zip(ds, blocks)):
             rows, cut = part(128 * b, 128), slice(128 * n, 128 * n + 128)
-            dgu[rows, 0:1024] = dga[cut]
-            dgu[rows, 1024:2048] = du[cut]
+            dgu[rows, :] = dga[cut]
+            dgu[part(512 + 128 * b, 128), :] = du[cut]
             if d == 0:
                 own[...] = result[cut]
             else:
@@ -1015,7 +1046,13 @@
     feed_back((2, 1))
     feed_back((3, 0))
     total_pass(X_SUM3)
-
+    weight_each(heads, range(3, 15), leave)
+    weight_each(wide, range(15), leave)
+    gather_sent(X_N2, n2_own, n2)
+    gather_sent(X_DY, dyin, dyf, started=False)
+    for d in (1, 2, 3):
+        far_copy(d, lax.rem(x + d, 4)).wait_send()
+    lax.fori_loop(0, 4, feed_grads, 0)
     def norm_back(value, grad, gain_row):
         r = lax.rsqrt(jnp.mean(value * value, axis=-1, keepdims=True) + EPSILON)
         unit = value * r
@@ -1060,6 +1097,13 @@
         return carry
 
     lax.fori_loop(0, 4, branch, 0)
+    for n in range(2):
+        rows = slice(256 * n, 256 * n + 256)
+        att[rows, :] = jnp.concatenate(
+            [attp[rows, 128 * h : 128 * h + 96] for h in range(4)], axis=1
+        )
+    wop[0:384, :] = mm_tn(att[...], dbr[...]).astype(BF)
+    first_start(("out",))
 
     def await_das(k, carry):
         place = das.at[part(64 * lax.rem(c - k + 16, 16), 64)]
@@ -1067,6 +1111,7 @@
         return carry
 
     lax.fori_loop(1, 16, await_das, 0)
+    first_step(EARLY, 0)
     dk[...] = jnp.zeros_like(dk)
     dv[...] = jnp.zeros_like(dv)
 
@@ -1112,6 +1157,7 @@
 
     lax.fori_loop(1, 16, send_dkv, 0)
     grad_place(1)[...] = dqs[part(64 * c, 64), 256:512]
+    first_step(EARLY, 1)
 
     def await_dqkv(b):
         for i in range(4):
@@ -1129,9 +1175,6 @@
                         place, place, cs.at[e, k], cr.at[e, k], {"ctx": lax.rem(c + k, 16)}
                     ).wait_recv()
 
-    for d in (1, 2, 3):
-        far_copy(d, lax.rem(x + d, 4)).wait_send()
-
     def input_grad(n, carry):
         b = far_first(n)
         await_dqkv(b)
@@ -1139,21 +1182,8 @@
         return carry
 
     lax.fori_loop(0, 4, input_grad, 0)
-    back, g_attn = norm_back(xall[my_rows, :].astype(F32), total_take(X_SUM4), gain_attn)
-    dx[...] = (mid[...] + back).astype(BF)
-    ggain[0:1, :] = g_attn
-
-    @pl.when(second)
-    def _():
-        gather_sent(X_DY, dyin, dyf, forwarded=False)
-        gather(X_DY, 6, dx, dyf).start()
-        gather_start(X_DY, dx, dyf, True)
-
     for n in range(2):
         rows = slice(256 * n, 256 * n + 256)
-        att[rows, :] = jnp.concatenate(
-            [attp[rows, 128 * h : 128 * h + 96] for h in range(4)], axis=1
-        )
         pieces = []
         for h in range(8):
             if h % 4 == 3:
@@ -1162,6 +1192,47 @@
                 pieces.append(dqp[rows, 128 * h : 128 * h + 48])
                 pieces.append(dqp[rows, 128 * h + 64 : 128 * h + 112])
         dqkv[rows, :] = jnp.concatenate(pieces, axis=1)
+
+    def head_grads(g, carry):
+        rows = part(384 * g, 384)
+        wqkv[rows, 0:768] = mm_tn(nf[:, rows], dqkv[...]).astype(BF)
+        return carry
+
+    lax.fori_loop(0, 4, head_grads, 0)
+    late_each(range(3), begin)
+    back, g_attn = norm_back(xall[my_rows, :].astype(F32), total_take(X_SUM4), gain_attn)
+    dx[...] = (mid[...] + back).astype(BF)
+    ggain[0:1, :] = g_attn
+
+    @pl.when(second)
+    def _():
+        gather_sent(X_DY, dyin, dyf, forwarded=False)
+        gather(X_DY, 6, dx, dyf).start()
+        gather_start(X_DY, dx, dyf, True)
+
+    gain_start(0)
+    first_step(EARLY, 2)
+    second_step(EARLY, 0)
+    gain_in[1, 0] = gain_sum(0)
+    gain_start(1)
+    second_step(EARLY, 1)
+    late_first()
+    second_step(EARLY, 2)
+    mirror_step(EARLY, begin)
+    gain_in[2, 0] = gain_sum(1)
+    gain_start(2)
+    late_second()
+    mirror_step(EARLY, finish_copy)
+    small_step(EARLY, 0)
+    late_small()
+    small_step(EARLY, 1)
+    late_big()
+    small_step(EARLY, 2)
+    small_step(EARLY, 3)
+    for n in range(3):
+        big_step(EARLY, n, 0, 4)
+    late_each(range(10, 13), arrive)
+    o_gain[...] = gain_sum(2)
 
     def sent_c(k, carry):
         to = lax.rem(c + k, 16)
@@ -1177,11 +1248,22 @@
     lax.fori_loop(1, 16, sent_c, 0)
     total_sent(X_SUM3)
     total_sent(X_SUM4)
-    weight_each(heads + wide, range(15), leave)
-    gather_sent(X_N2, n2_own, n2)
     gather_sent(X_DBR, dbr_own, dbr)
     gather_sent(X_IN, xin, xall, started=False)
-    gather_sent(X_DY, dyin, dyf, started=False)
+
+    def sent_first(q, carry):
+        for name in EARLY:
+            for n in range(3):
+                copy_first(name, n, q).wait_send()
+                copy_big(name, n, q).wait_send()
+        return carry
+
+    lax.fori_loop(0, 4, sent_first, 0)
+    late_each((0, 1, 2, 3, 4, 5, 7, 8, 9, 10, 11, 12), leave)
+    for name in EARLY:
+        for n in range(3):
+            copy_second(name, n).wait_send()
+            copy_small(name, n).wait_send()
 
     @pl.when(first)
     def _():
@@ -1201,17 +1283,23 @@
     shapes = [
         ((128, WIDTH), BF),
         ((128, WIDTH), BF),
+        *(((4, 4, r, w), BF) for _, _, r, w in FLOWS.values()),
+        ((8, 384), F32),
+    ]
+    scratch = [
         ((512, WIDTH), BF),
-        ((512, WIDTH), BF),
-        ((512, 2048), BF),
+        ((2, 512, WIDTH), BF),
+        ((1024, 1024), BF),
         ((512, 768), BF),
         ((512, 384), BF),
         ((512, WIDTH), BF),
         ((512, 1024), BF),
-        ((512, WIDTH), BF),
         ((8, WIDTH), F32),
-    ]
-    scratch = [
+        ((4, 64, WIDTH), BF),
+        ((3, 4, 96, 384), BF),
+        *(((3, 384, 384), BF),) * 2,
+        *(((3, 96, 384), BF),) * 3,
+        ((3, 4, 8, 384), F32),
         ((4, 384, 1024), BF),
         ((WIDTH, 1024), BF),
         ((WIDTH, 1024), BF),
@@ -1240,8 +1328,8 @@
         ((1024, 256), BF),
         ((512, 512), BF),
         ((128, WIDTH), F32),
-        ((512, 1024), F32),
-        ((512, 1024), F32),
+        ((512, 1024), BF),
+        ((512, 1024), BF),
         ((128, WIDTH), F32),
         ((2, 4, 128, WIDTH), BF),
         ((2, 2, 128, WIDTH), BF),
@@ -1257,9 +1345,10 @@
         layer_kernel,
         out_shape=[jax.ShapeDtypeStruct(s, d) for s, d in shapes],
         in_specs=[vm] * 9 + [hbm] * 4,
-        out_specs=[vm] * len(shapes),
+        out_specs=[vm] * 2 + [hbm] * len(FLOWS) + [vm],
         scratch_shapes=[pltpu.VMEM(s, d) for s, d in scratch]
-        + [dma((13, 7)), dma((13, 7)), dma((6, 16)), dma((6, 16)), dma((4, 15)), dma((4, 15)), dma((7,)), pltpu.SemaphoreType.REGULAR],
+        + [dma((13, 7)), dma((13, 7)), dma((6, 16)), dma((6, 16)), dma((4, 15)), dma((4, 15)), dma((7,)), pltpu.SemaphoreType.REGULAR]
+        + [dma((6, 32)), dma((6, 32)), dma((3, 4)), dma((3, 4)), dma((6,))],
         name="layer",
         compiler_params=pltpu.CompilerParams(
             collective_id=cid, has_side_effects=True, vmem_limit_bytes=63 << 20
@@ -1285,7 +1374,7 @@
     index = np.where(lane < 64, lane, lane - 64)
     freq = np.where(index < 48, THETA ** (-2.0 * index / HEAD_SIZE), 0.0).astype(np.float32)
     freq = jnp.asarray(np.broadcast_to(freq[None], (8, 128)))
-    out, dx, nf, n2, dgu, dqkv, att, dbr, hidden, dyf, ggain = run_layer(
+    out, dx, *summed, g_gain = run_layer(
         inputs.reshape(128, WIDTH),
         out_grad.reshape(128, WIDTH),
         positions,
@@ -1301,17 +1390,16 @@
         w_up[0],
         0,
     )
-    *summed, g_gain = reduce_grads(n2, nf, dgu, dqkv, att, dbr, hidden, dyf, ggain, 1)
-    g_gate, g_up, g_query, g_key, g_value, g_out, g_down = widen(*summed)
+    g_gate, g_up, g_query, g_key, g_value, g_out, g_down, g_attn, g_mlp = widen(*summed, g_gain)
     return (
         out.reshape(1, 2, 64, WIDTH),
         dx.reshape(1, 2, 64, WIDTH),
-        g_gain[0:1],
+        g_attn,
         g_query[None],
         g_key[None],
         g_value[None],
         g_out[None],
-        g_gain[1:2],
+        g_mlp,
         g_gate[None],
         g_up[None],
         g_down[None],

time: 455 us -> 411 us (0.903)
  Pallas kernels: 448 us -> 407 us
    pallas_call x1 -> x0, Pallas kernels: 142 us -> none  [reduce_grads(): pl.pallas_call(grad_kernel, out_shape=[jax.ShapeDtypeStruct((4, 4) + s, B...]
    pallas_call x1, Pallas kernels: 291 us -> 392 us  [run_layer(): pl.pallas_call(layer_kernel, out_shape=[jax.ShapeDtypeStruct(s, d) for s,...]
where the time goes in v5:
time: 411 us
  Pallas kernels  407 us (99%)
    pallas_call x1, Pallas kernels, run_layer(): pl.pallas_call(layer_kernel, out_shape=[jax.ShapeDtypeStruct(s, d) for s,...  392 us
    pallas_call x1, Pallas kernels, widen(): pl.pallas_call(widen_kernel, grid=(steps,), out_shape=[shape(384, FF), sh...  14.8 us

profile of v5, /device:TPU:0, one launch (start us, length us, event | category | flops | bytes accessed | tf_op | source)
XLA Modules:
  0.0 410.6 jit_solution(1065726388171899989)
XLA Ops:
  0.6 1.3 jit_solution_.3.freq
  1.9 392.4 %layer.1 = (bf16[128,1536]{1,0:T(8,128)(2,1)}, bf16[128,1536]{1,0:T(8,128)(2,1)}, bf16[4,4,96,1024]{3,2,1,0:T(8,128)(2,1)}, bf16[4,4,96,1024]{3,2,1,0:T(8,128)(2...) custom-call(bf16[128,1536]{1,0:T(8,128)(2,1)} %bitcast.27, ...), custom_call_target="tpu_custom_call" | custom-call | tf_op jit(solution)/shard_map/layer/pallas_call | solution.py:1344
  394.3 0.0 copy-start.1
  394.3 0.0 copy-start
  394.3 14.8 %widen.1 = (f32[384,4096]{1,0:T(8,128)}, f32[384,4096]{1,0:T(8,128)}, f32[384,1536]{1,0:T(8,128)}, f32[384,768]{1,0:T(8,128)}, f32[384,768]{1,0:T(8,128)}, /*ind...) custom-call(bf16[4,4,96,1024]{3,2,1,0:T(8,128)(2,1)} %get-tuple-element.31.w_gate, ...), custom_call_target="tpu_custom_call" | custom-call | tf_op jit(solution)/shard_map/widen/pallas_call | solution.py:74
  409.1 0.0 copy-done.1
  409.1 0.7 copy.26
  409.9 0.0 copy-done
  409.9 0.7 copy.27
Async XLA Ops:
  394.3 14.8 %copy-start.1 = (bf16[128,1536]{1,0:T(8,128)(2,1)S(1)}, bf16[128,1536]{1,0:T(8,128)(2,1)}, u32[]{:S(2)}) copy-start(bf16[128,1536]{1,0:T(8,128)(2,1)} %get-tuple-element.29) | copy-start | bytes 1179652
  394.3 15.6 %copy-start = (bf16[128,1536]{1,0:T(8,128)(2,1)S(1)}, bf16[128,1536]{1,0:T(8,128)(2,1)}, u32[]{:S(2)}) copy-start(bf16[128,1536]{1,0:T(8,128)(2,1)} %get-tuple-element.30) | copy-start | bytes 1179652

commit v6 on v5

--- a/solution.py
+++ b/solution.py
@@ -113,17 +113,28 @@
 X_GAIN, X_POS, X_IN, X_DY, X_QKV, X_GATE, X_UP, X_SUM1, X_N2, X_SUM2, X_SUM3, X_DBR, X_SUM4 = range(13)
 C_POS, C_QKV, C_ATT, C_DATT, C_DQ, C_DKV = range(6)
 SCALE = HEAD_SIZE ** (-0.5)
+SCALE2 = SCALE * 1.4426950408889634
 FLOWS = {
-    "gate": ("y", 1, 96, 1024),
-    "up": ("y", -1, 96, 1024),
-    "down": ("z", 1, 64, 1536),
-    "out": ("z", -1, 96, 384),
-    "heads_a": ("y", 1, 96, 384),
-    "heads_b": ("z", -1, 96, 384),
+    "gate": ("y", 1, "gate", 0, 96, 896),
+    "up": ("y", -1, "up", 0, 96, 896),
+    "down": ("z", 1, "down", 0, 64, 1280),
+    "out": ("z", -1, "out", 0, 96, 384),
+    "gate_rest": ("z", -1, "gate", 896, 96, 128),
+    "up_rest": ("z", -1, "up", 896, 96, 128),
+    "down_rest": ("z", -1, "down", 1280, 64, 256),
+    "heads_a": ("y", 1, "heads_a", 0, 96, 384),
+    "heads_b": ("z", -1, "heads_b", 0, 96, 384),
+}
+ARRAYS = {
+    "gate": (96, 1024),
+    "up": (96, 1024),
+    "down": (64, 1536),
+    "out": (96, 384),
+    "heads_a": (96, 384),
+    "heads_b": (96, 384),
 }
 NAMES = list(FLOWS)
-EARLY, LATE = NAMES[:4], NAMES[4:]
-SMALL = NAMES[3:]
+EARLY, LATE = NAMES[:7], NAMES[7:]
 
 
 def spread(w, heads):
@@ -648,7 +659,7 @@
     kt[...] = qs[:, 256:384].T
 
     def masked(q, cols):
-        st = mm_nt(qs[:, 256:384], q) * SCALE
+        st = mm_nt(qs[:, 256:384], q)
         return jnp.where(posk[:, 0:1] <= posr[0:1, cols], st, -1e30)
 
     def att_place():
@@ -663,11 +674,11 @@
         for g in range(2):
             st = masked(qs[rows, 128 * g : 128 * g + 128], rows)
             top = jnp.max(st, axis=0, keepdims=True)
-            e = jnp.exp(st - top)
-            total = jnp.sum(e, axis=0, keepdims=True)
-            lse[g : g + 1, rows] = top + jnp.log(total)
-            pt = (e * (1.0 / total)).astype(BF)
-            osend[rows, 128 * g : 128 * g + 128] = mm(vt[...], pt).T.astype(BF)
+            e = jnp.exp2((st - top) * SCALE2)
+            sums = jnp.sum(e, axis=0, keepdims=True)
+            lse[g : g + 1, rows] = top * SCALE2 + jnp.log2(sums)
+            result = mm(vt[...], e.astype(BF)) * (1.0 / sums)
+            osend[rows, 128 * g : 128 * g + 128] = result.T.astype(BF)
         for i in range(4):
             to = 4 * n + i
 
@@ -788,42 +799,52 @@
         gather(X_IN, 6, out, xall).start()
         gather_start(X_IN, out, xall, True)
 
-    held = dict(zip(NAMES, (h_gate, h_up, h_down, h_out, h_heads_a, h_heads_b)))
+    held = dict(zip(ARRAYS, (h_gate, h_up, h_down, h_out, h_heads_a, h_heads_b)))
 
     def ring(name):
-        axis, d, _, _ = FLOWS[name]
+        axis, d = FLOWS[name][:2]
         other = "z" if axis == "y" else "y"
         return NAMES.index(name), axis, other, d, where[axis], where[other]
 
     def at(i, d, s):
         return lax.rem(i - d * s + 8, 4)
 
+    def columns(name):
+        return pl.ds(FLOWS[name][3], FLOWS[name][5])
+
+    def place_of(name, g, p):
+        return held[FLOWS[name][2]].at[g, p, :, columns(name)]
+
     def partial(name, g, p):
-        if name == "down":
-            return wd.at[part(256 * g + 64 * p, 64)]
-        if name == "out":
+        array, cols = FLOWS[name][2], columns(name)
+        if array == "down":
+            return wd.at[part(256 * g + 64 * p, 64), cols]
+        if array == "out":
             return wop.at[part(96 * g, 96), part(384 * p, 384)]
         rows = pl.ds(pl.multiple_of(384 * g + 96 * p, 96), 96)
         if name in LATE:
             return wqkv.at[rows, pl.ds(384 * LATE.index(name), 384)]
-        return (wgf if name == "gate" else wuf).at[rows]
+        return (wgf if array == "gate" else wuf).at[rows, cols]
 
     def arrival(name, s, q):
         n = 4 * (s - 1) + q
-        if name == "gate":
-            return wsend.at[s, part(96 * q, 96)]
-        if name == "up":
-            return wsend.at[3, part(96 * q, 96)] if s == 0 else dgu.at[part(96 * n, 96)]
-        if name == "down":
-            return arrive_down.at[q] if s == 0 else n2.at[part(64 * n, 64)]
+        array, cols = FLOWS[name][2], columns(name)
+        if array == "gate":
+            return wsend.at[s, part(96 * q, 96), cols]
+        if array == "up":
+            slot = wsend.at[3, part(96 * q, 96), cols]
+            return slot if s == 0 else dgu.at[part(96 * n, 96), cols]
+        if array == "down":
+            return arrive_down.at[q, :, cols] if s == 0 else n2.at[part(64 * n, 64), cols]
         return arrive_out.at[s, q]
 
     def arrival2(name, s):
-        if name in ("gate", "up"):
-            return (gate if name == "gate" else up).at[part(96 * s, 96)]
-        if name == "down":
-            return prec3.at[s, pl.ds(0, 64)]
-        return (second_out, second_a, second_b)[SMALL.index(name)].at[s]
+        array, cols = FLOWS[name][2], columns(name)
+        if array in ("gate", "up"):
+            return (gate if array == "gate" else up).at[part(96 * s, 96), cols]
+        if array == "down":
+            return prec3.at[s, pl.ds(0, 64), cols]
+        return {"out": second_out, "heads_a": second_a, "heads_b": second_b}[array].at[s]
 
     def flow(name, n, src, dst, device):
         f = NAMES.index(name)
@@ -842,21 +863,21 @@
     def copy_mirror(name):
         f, axis, other, d, i, j = ring(name)
         n = 6 if name in LATE else 15
-        return flow(name, n, partial(name, i, j), held[name].at[x, j], mirror[axis])
+        return flow(name, n, partial(name, i, j), place_of(name, x, j), mirror[axis])
 
     def copy_own(name):
         f, axis, other, d, i, j = ring(name)
-        group = i if name in ("down", "out") else x
-        return pltpu.make_async_copy(partial(name, i, j), held[name].at[group, j], os.at[f])
+        group = i if FLOWS[name][2] in ("down", "out") else x
+        return pltpu.make_async_copy(partial(name, i, j), place_of(name, group, j), os.at[f])
 
     def copy_small(name, s):
         f, axis, other, d, i, j = ring(name)
-        place = held[name].at[i, at(j, d, s)]
+        place = place_of(name, i, at(j, d, s))
         return flow(name, 16 + s, place, place, near(other, d))
 
     def copy_big(name, s, q):
         f, axis, other, d, i, j = ring(name)
-        place = held[name].at[at(i, d, s), at(j, d, q)]
+        place = place_of(name, at(i, d, s), at(j, d, q))
         return flow(name, 20 + 4 * s + q, place, place, near(axis, d))
 
     def first_start(names):
@@ -897,7 +918,7 @@
 
     def mirror_step(names, act):
         for name in names:
-            if name in ("down", "out"):
+            if FLOWS[name][2] in ("down", "out"):
                 act(copy_own(name))
                 continue
             axis = FLOWS[name][0]
@@ -956,7 +977,7 @@
         k = (n if n < 6 else n - 1) % 3 + 1
         if n < 3:
             src = wqkv.at[part(384 * lax.rem(i + k, 4), 384), cols]
-            return flow(name, n, src, (arrive_a, arrive_b)[f - 4].at[k - 1], near(axis, k))
+            return flow(name, n, src, (arrive_a, arrive_b)[LATE.index(name)].at[k - 1], near(axis, k))
         if n < 6:
             src = partial(name, i, lax.rem(j + k, 4))
             return flow(name, n, src, arrival2(name, k - 1), near(other, k))
@@ -976,7 +997,7 @@
         for name in LATE:
             f, axis, other, d, i, j = ring(name)
             rows, cols = part(384 * i, 384), pl.ds(384 * LATE.index(name), 384)
-            got = (arrive_a, arrive_b)[f - 4]
+            got = (arrive_a, arrive_b)[LATE.index(name)]
             sums = wqkv[rows, cols].astype(F32)
             for k in range(3):
                 sums = sums + got[k].astype(F32)
@@ -1012,7 +1033,7 @@
 
         @pl.when(s == 0)
         def _():
-            first_start(EARLY[:3])
+            first_start(("gate", "up", "down"))
 
         return carry
 
@@ -1053,6 +1074,7 @@
     for d in (1, 2, 3):
         far_copy(d, lax.rem(x + d, 4)).wait_send()
     lax.fori_loop(0, 4, feed_grads, 0)
+    first_start(("gate_rest", "up_rest", "down_rest"))
     def norm_back(value, grad, gain_row):
         r = lax.rsqrt(jnp.mean(value * value, axis=-1, keepdims=True) + EPSILON)
         unit = value * r
@@ -1127,7 +1149,7 @@
         for g in range(2):
             cols = slice(128 * g, 128 * g + 128)
             q, da = qs[rows, cols], das[rows, cols]
-            p = jnp.exp(masked(q, rows) - lse[g : g + 1, rows])
+            p = jnp.exp2(masked(q, rows) * SCALE2 - lse[g : g + 1, rows])
             dp = mm_nt(qs[:, 384:512], da)
             dv[...] += mm(p.astype(BF), da)
             ds = (p * (dp - jnp.sum(p * dp, axis=0, keepdims=True))).astype(BF)
@@ -1182,6 +1204,10 @@
         return carry
 
     lax.fori_loop(0, 4, input_grad, 0)
+    @pl.when(first)
+    def _():
+        first_step(EARLY, 2)
+
     for n in range(2):
         rows = slice(256 * n, 256 * n + 256)
         pieces = []
@@ -1211,7 +1237,11 @@
         gather_start(X_DY, dx, dyf, True)
 
     gain_start(0)
-    first_step(EARLY, 2)
+
+    @pl.when(second)
+    def _():
+        first_step(EARLY, 2)
+
     second_step(EARLY, 0)
     gain_in[1, 0] = gain_sum(0)
     gain_start(1)
@@ -1283,7 +1313,7 @@
     shapes = [
         ((128, WIDTH), BF),
         ((128, WIDTH), BF),
-        *(((4, 4, r, w), BF) for _, _, r, w in FLOWS.values()),
+        *(((4, 4) + shape, BF) for shape in ARRAYS.values()),
         ((8, 384), F32),
     ]
     scratch = [
@@ -1345,10 +1375,10 @@
         layer_kernel,
         out_shape=[jax.ShapeDtypeStruct(s, d) for s, d in shapes],
         in_specs=[vm] * 9 + [hbm] * 4,
-        out_specs=[vm] * 2 + [hbm] * len(FLOWS) + [vm],
+        out_specs=[vm] * 2 + [hbm] * len(ARRAYS) + [vm],
         scratch_shapes=[pltpu.VMEM(s, d) for s, d in scratch]
         + [dma((13, 7)), dma((13, 7)), dma((6, 16)), dma((6, 16)), dma((4, 15)), dma((4, 15)), dma((7,)), pltpu.SemaphoreType.REGULAR]
-        + [dma((6, 32)), dma((6, 32)), dma((3, 4)), dma((3, 4)), dma((6,))],
+        + [dma((9, 32)), dma((9, 32)), dma((3, 4)), dma((3, 4)), dma((9,))],
         name="layer",
         compiler_params=pltpu.CompilerParams(
             collective_id=cid, has_side_effects=True, vmem_limit_bytes=63 << 20

time: 411 us -> 398 us (0.968)
  Pallas kernels: 407 us -> 394 us
    pallas_call x1, Pallas kernels: 392 us -> 379 us  [run_layer(): pl.pallas_call(layer_kernel, out_shape=[jax.ShapeDtypeStruct(s, d) for s,...]
where the time goes in v6:
time: 398 us; the launch traced here: 397 us
  Pallas kernels  394 us (99%)
    pallas_call x1, Pallas kernels, run_layer(): pl.pallas_call(layer_kernel, out_shape=[jax.ShapeDtypeStruct(s, d) for s,...  379 us
    pallas_call x1, Pallas kernels, widen(): pl.pallas_call(widen_kernel, grid=(steps,), out_shape=[shape(384, FF), sh...  14.8 us

profile of v6, /device:TPU:0, one launch (start us, length us, event | category | flops | bytes accessed | tf_op | source)
XLA Modules:
  0.0 397.3 jit_solution(12335342156171848345)
XLA Ops:
  0.6 1.3 jit_solution_.3.freq
  1.9 379.1 %layer.1 = (bf16[128,1536]{1,0:T(8,128)(2,1)}, bf16[128,1536]{1,0:T(8,128)(2,1)}, bf16[4,4,96,1024]{3,2,1,0:T(8,128)(2,1)}, bf16[4,4,96,1024]{3,2,1,0:T(8,128)(2...) custom-call(bf16[128,1536]{1,0:T(8,128)(2,1)} %bitcast.27, ...), custom_call_target="tpu_custom_call" | custom-call | tf_op jit(solution)/shard_map/layer/pallas_call | solution.py:1374
  381.0 0.0 copy-start.1
  381.0 0.0 copy-start
  381.0 14.8 %widen.1 = (f32[384,4096]{1,0:T(8,128)}, f32[384,4096]{1,0:T(8,128)}, f32[384,1536]{1,0:T(8,128)}, f32[384,768]{1,0:T(8,128)}, f32[384,768]{1,0:T(8,128)}, /*ind...) custom-call(bf16[4,4,96,1024]{3,2,1,0:T(8,128)(2,1)} %get-tuple-element.31.w_gate, ...), custom_call_target="tpu_custom_call" | custom-call | tf_op jit(solution)/shard_map/widen/pallas_call | solution.py:74
  395.8 0.0 copy-done.1
  395.8 0.7 copy.26
  396.6 0.0 copy-done
  396.6 0.7 copy.27
Async XLA Ops:
  381.0 14.8 %copy-start.1 = (bf16[128,1536]{1,0:T(8,128)(2,1)S(1)}, bf16[128,1536]{1,0:T(8,128)(2,1)}, u32[]{:S(2)}) copy-start(bf16[128,1536]{1,0:T(8,128)(2,1)} %get-tuple-element.29) | copy-start | bytes 1179652
  381.0 15.6 %copy-start = (bf16[128,1536]{1,0:T(8,128)(2,1)S(1)}, bf16[128,1536]{1,0:T(8,128)(2,1)}, u32[]{:S(2)}) copy-start(bf16[128,1536]{1,0:T(8,128)(2,1)} %get-tuple-element.30) | copy-start | bytes 1179652

commit v7 on v6

--- a/solution.py
+++ b/solution.py
@@ -1,6 +1,5 @@
 import jax
 import jax.numpy as jnp
-import numpy as np
 from jax import lax
 from jax.experimental import pallas as pl
 from jax.experimental.pallas import tpu as pltpu
@@ -114,6 +113,7 @@
 C_POS, C_QKV, C_ATT, C_DATT, C_DQ, C_DKV = range(6)
 SCALE = HEAD_SIZE ** (-0.5)
 SCALE2 = SCALE * 1.4426950408889634
+STEP2 = -2.0 / HEAD_SIZE * 16.609640474436812
 FLOWS = {
     "gate": ("y", 1, "gate", 0, 96, 896),
     "up": ("y", -1, "up", 0, 96, 896),
@@ -135,6 +135,7 @@
 }
 NAMES = list(FLOWS)
 EARLY, LATE = NAMES[:7], NAMES[7:]
+STAY = ("down", "out", "down_rest")
 
 
 def spread(w, heads):
@@ -160,7 +161,6 @@
     xin,
     dyin,
     positions,
-    freq,
     norm_attn,
     norm_mlp,
     wq,
@@ -265,7 +265,6 @@
             return {"ctx": 4 * z + lax.rem(y + step + 4, 4)}
         return {"ctx": 4 * lax.rem(z + step + 4, 4) + y}
 
-    mirror = {"y": {"fsdp": y, "ctx": 4 * z + x}, "z": {"fsdp": z, "ctx": 4 * x + y}}
 
     barrier = pltpu.get_barrier_semaphore()
     for k in range(1, 4):
@@ -287,9 +286,7 @@
         return carry
 
     lax.fori_loop(1, 16, greet, 0)
-    for axis in "yz":
-        pl.semaphore_signal(barrier, inc=1, device_id=mirror[axis], device_id_type=MESH)
-    pl.semaphore_wait(barrier, 24)
+    pl.semaphore_wait(barrier, 22)
 
     def ahead(k):
         return lax.rem(x + k, 4)
@@ -512,6 +509,8 @@
 
     lane = lax.broadcasted_iota(jnp.int32, (1, 128), 1)
     sign = jnp.where(lane < 64, -1.0, 1.0)
+    index = jnp.where(lane < 64, lane, lane - 64)
+    freq = jnp.where(index < 48, jnp.exp2(index.astype(F32) * STEP2), 0.0)
     for k in (1, 3, 2):
         pos_copy(k).wait()
     for b in range(4):
@@ -534,7 +533,7 @@
         weight_share(heads)
 
     for b in range(4):
-        angle = as_column(posx[b][0:1, :]) * freq[0:1, :]
+        angle = as_column(posx[b][0:1, :]) * freq
         cos_c[128 * b : 128 * b + 128, :] = jnp.cos(angle)
         sin_c[128 * b : 128 * b + 128, :] = jnp.sin(angle) * sign
 
@@ -551,7 +550,7 @@
             posr[0:1, block] = row
             column = as_column(row)
             posk[block, :] = jnp.broadcast_to(column, (128, 128))
-            angle = column * freq[0:1, :]
+            angle = column * freq
             cos_s[block, :] = jnp.cos(angle)
             sin_s[block, :] = jnp.sin(angle) * sign
             return carry
@@ -804,7 +803,14 @@
     def ring(name):
         axis, d = FLOWS[name][:2]
         other = "z" if axis == "y" else "y"
-        return NAMES.index(name), axis, other, d, where[axis], where[other]
+        group = where[axis] if name in STAY else lax.rem(x + where[axis], 4)
+        return NAMES.index(name), axis, other, d, group, where[other]
+
+    def hand(name):
+        axis, d = FLOWS[name][:2]
+        if name in STAY:
+            return where[axis], d
+        return lax.rem(x - where[axis] + 4, 4), -d
 
     def at(i, d, s):
         return lax.rem(i - d * s + 8, 4)
@@ -863,21 +869,22 @@
     def copy_mirror(name):
         f, axis, other, d, i, j = ring(name)
         n = 6 if name in LATE else 15
-        return flow(name, n, partial(name, i, j), place_of(name, x, j), mirror[axis])
+        device = {"fsdp": lax.rem(x + where[axis], 4)}
+        return flow(name, n, partial(name, i, j), place_of(name, x, j), device)
 
     def copy_own(name):
         f, axis, other, d, i, j = ring(name)
-        group = i if FLOWS[name][2] in ("down", "out") else x
+        group = i if name in STAY else x
         return pltpu.make_async_copy(partial(name, i, j), place_of(name, group, j), os.at[f])
 
     def copy_small(name, s):
         f, axis, other, d, i, j = ring(name)
-        place = place_of(name, i, at(j, d, s))
+        place = place_of(name, hand(name)[0], at(j, d, s))
         return flow(name, 16 + s, place, place, near(other, d))
 
     def copy_big(name, s, q):
         f, axis, other, d, i, j = ring(name)
-        place = place_of(name, at(i, d, s), at(j, d, q))
+        place = place_of(name, at(*hand(name), s), at(j, d, q))
         return flow(name, 20 + 4 * s + q, place, place, near(axis, d))
 
     def first_start(names):
@@ -918,16 +925,16 @@
 
     def mirror_step(names, act):
         for name in names:
-            if FLOWS[name][2] in ("down", "out"):
+            if name in STAY:
                 act(copy_own(name))
                 continue
             axis = FLOWS[name][0]
 
-            @pl.when(where[axis] != x)
+            @pl.when(where[axis] != 0)
             def _(name=name):
                 act(copy_mirror(name))
 
-            @pl.when(where[axis] == x)
+            @pl.when(where[axis] == 0)
             def _(name=name):
                 act(copy_own(name))
 
@@ -982,9 +989,9 @@
             src = partial(name, i, lax.rem(j + k, 4))
             return flow(name, n, src, arrival2(name, k - 1), near(other, k))
         if n < 10:
-            place = held[name].at[i, j]
+            place = held[name].at[hand(name)[0], j]
             return flow(name, n, place, place, near(other, k))
-        place = held[name].at[i]
+        place = held[name].at[hand(name)[0]]
         return flow(name, n, place, place, near(axis, k))
 
     def late_each(items, act):
@@ -1024,16 +1031,12 @@
         late_each(range(10, 13), begin)
 
     def feed_grads(s, carry):
-        rows = part(384 * at(y, 1, 1 + s), 384)
+        rows = part(384 * at(ring("gate")[4], 1, 1 + s), 384)
         wgf[rows, :] = mm_tn(n2[:, rows], dgu[0:512, :]).astype(BF)
-        rows = part(384 * at(y, -1, 1 + s), 384)
+        rows = part(384 * at(ring("up")[4], -1, 1 + s), 384)
         wuf[rows, :] = mm_tn(n2[:, rows], dgu[512:1024, :]).astype(BF)
         rows = part(256 * at(z, 1, 1 + s), 256)
         wd[rows, :] = mm_tn(hidden[:, rows], dyf[...]).astype(BF)
-
-        @pl.when(s == 0)
-        def _():
-            first_start(("gate", "up", "down"))
 
         return carry
 
@@ -1066,14 +1069,16 @@
     total_sent(X_SUM1)
     feed_back((2, 1))
     feed_back((3, 0))
-    total_pass(X_SUM3)
     weight_each(heads, range(3, 15), leave)
     weight_each(wide, range(15), leave)
     gather_sent(X_N2, n2_own, n2)
     gather_sent(X_DY, dyin, dyf, started=False)
     for d in (1, 2, 3):
         far_copy(d, lax.rem(x + d, 4)).wait_send()
-    lax.fori_loop(0, 4, feed_grads, 0)
+    lax.fori_loop(0, 1, feed_grads, 0)
+    first_start(("gate", "up", "down"))
+    total_pass(X_SUM3)
+    lax.fori_loop(1, 4, feed_grads, 0)
     first_start(("gate_rest", "up_rest", "down_rest"))
     def norm_back(value, grad, gain_row):
         r = lax.rsqrt(jnp.mean(value * value, axis=-1, keepdims=True) + EPSILON)
@@ -1246,11 +1251,11 @@
     gain_in[1, 0] = gain_sum(0)
     gain_start(1)
     second_step(EARLY, 1)
-    late_first()
     second_step(EARLY, 2)
     mirror_step(EARLY, begin)
     gain_in[2, 0] = gain_sum(1)
     gain_start(2)
+    late_first()
     late_second()
     mirror_step(EARLY, finish_copy)
     small_step(EARLY, 0)
@@ -1306,7 +1311,7 @@
         gather(X_DY, 6, dx, dyf).wait_send()
 
 
-def run_layer(xin, dyin, positions, freq, norm_attn, norm_mlp, wq, wk, wv, wo, wd, wg, wu, cid):
+def run_layer(xin, dyin, positions, norm_attn, norm_mlp, wq, wk, wv, wo, wd, wg, wu, cid):
     vm = pl.BlockSpec(memory_space=pltpu.VMEM)
     hbm = pl.BlockSpec(memory_space=pl.ANY)
     dma = pltpu.SemaphoreType.DMA
@@ -1374,7 +1379,7 @@
     return pl.pallas_call(
         layer_kernel,
         out_shape=[jax.ShapeDtypeStruct(s, d) for s, d in shapes],
-        in_specs=[vm] * 9 + [hbm] * 4,
+        in_specs=[vm] * 8 + [hbm] * 4,
         out_specs=[vm] * 2 + [hbm] * len(ARRAYS) + [vm],
         scratch_shapes=[pltpu.VMEM(s, d) for s, d in scratch]
         + [dma((13, 7)), dma((13, 7)), dma((6, 16)), dma((6, 16)), dma((4, 15)), dma((4, 15)), dma((7,)), pltpu.SemaphoreType.REGULAR]
@@ -1383,7 +1388,7 @@
         compiler_params=pltpu.CompilerParams(
             collective_id=cid, has_side_effects=True, vmem_limit_bytes=63 << 20
         ),
-    )(xin, dyin, positions, freq, norm_attn, norm_mlp, wq, wk, wv, wo, wd, wg, wu)
+    )(xin, dyin, positions, norm_attn, norm_mlp, wq, wk, wv, wo, wd, wg, wu)
 
 
 def local(
@@ -1400,15 +1405,10 @@
     w_up,
     w_down,
 ):
-    lane = np.arange(128)
-    index = np.where(lane < 64, lane, lane - 64)
-    freq = np.where(index < 48, THETA ** (-2.0 * index / HEAD_SIZE), 0.0).astype(np.float32)
-    freq = jnp.asarray(np.broadcast_to(freq[None], (8, 128)))
     out, dx, *summed, g_gain = run_layer(
         inputs.reshape(128, WIDTH),
         out_grad.reshape(128, WIDTH),
         positions,
-        freq,
         norm_attn,
         norm_mlp,
         w_query[0],

time: 398 us -> 383 us (0.962)
  Pallas kernels: 394 us -> 380 us
    pallas_call x1, Pallas kernels: 379 us -> 365 us  [run_layer(): pl.pallas_call(layer_kernel, out_shape=[jax.ShapeDtypeStruct(s, d) for s,...]
where the time goes in v7:
time: 383 us; the launch traced here: 382 us
  Pallas kernels  380 us (99%)
    pallas_call x1, Pallas kernels, run_layer(): pl.pallas_call(layer_kernel, out_shape=[jax.ShapeDtypeStruct(s, d) for s,...  365 us
    pallas_call x1, Pallas kernels, widen(): pl.pallas_call(widen_kernel, grid=(steps,), out_shape=[shape(384, FF), sh...  14.8 us

profile of v7, /device:TPU:0, one launch (start us, length us, event | category | flops | bytes accessed | tf_op | source)
XLA Modules:
  0.0 382.4 jit_solution(6258180250367483470)
XLA Ops:
  0.6 365.4 %layer.1 = (bf16[128,1536]{1,0:T(8,128)(2,1)}, bf16[128,1536]{1,0:T(8,128)(2,1)}, bf16[4,4,96,1024]{3,2,1,0:T(8,128)(2,1)}, bf16[4,4,96,1024]{3,2,1,0:T(8,128)(2...) custom-call(bf16[128,1536]{1,0:T(8,128)(2,1)} %bitcast.27, ...), custom_call_target="tpu_custom_call" | custom-call | tf_op jit(solution)/shard_map/layer/pallas_call | solution.py:1379
  366.0 0.0 copy-start.1
  366.1 0.0 copy-start
  366.1 14.8 %widen.1 = (f32[384,4096]{1,0:T(8,128)}, f32[384,4096]{1,0:T(8,128)}, f32[384,1536]{1,0:T(8,128)}, f32[384,768]{1,0:T(8,128)}, f32[384,768]{1,0:T(8,128)}, /*ind...) custom-call(bf16[4,4,96,1024]{3,2,1,0:T(8,128)(2,1)} %get-tuple-element.31.w_gate, ...), custom_call_target="tpu_custom_call" | custom-call | tf_op jit(solution)/shard_map/widen/pallas_call | solution.py:73
  380.9 0.0 copy-done.1
  380.9 0.7 copy.25
  381.6 0.0 copy-done
  381.6 0.7 copy.26
Async XLA Ops:
  366.0 14.8 %copy-start.1 = (bf16[128,1536]{1,0:T(8,128)(2,1)S(1)}, bf16[128,1536]{1,0:T(8,128)(2,1)}, u32[]{:S(2)}) copy-start(bf16[128,1536]{1,0:T(8,128)(2,1)} %get-tuple-element.29) | copy-start | bytes 1179652
  366.1 15.6 %copy-start = (bf16[128,1536]{1,0:T(8,128)(2,1)S(1)}, bf16[128,1536]{1,0:T(8,128)(2,1)}, u32[]{:S(2)}) copy-start(bf16[128,1536]{1,0:T(8,128)(2,1)} %get-tuple-element.30) | copy-start | bytes 1179652

commit v8 on v7

--- a/solution.py
+++ b/solution.py
@@ -59,7 +59,7 @@
 
 
 def widen(gate, up, down, out, heads_a, heads_b, gains):
-    steps = 8
+    steps = 4
 
     def spec(r, cols):
         return pl.BlockSpec((r, cols), lambda i: (i, 0))
@@ -68,7 +68,7 @@
         return jax.ShapeDtypeStruct((r, cols), F32)
 
     def blocks(cols):
-        return pl.BlockSpec((4, 1, 48, cols), lambda i: (0, i // 2, i % 2, 0))
+        return pl.BlockSpec((4, 1, 96, cols), lambda i: (0, i, 0, 0))
 
     return pl.pallas_call(
         widen_kernel,
@@ -87,20 +87,20 @@
         in_specs=[
             blocks(1024),
             blocks(1024),
-            spec(128, 1536),
-            pl.BlockSpec((1, 4, 48, 384), lambda i: (i // 2, 0, i % 2, 0)),
+            spec(256, 1536),
+            pl.BlockSpec((1, 4, 96, 384), lambda i: (i, 0, 0, 0)),
             blocks(384),
             blocks(384),
             pl.BlockSpec((8, 384), lambda i: (0, 0)),
         ],
         out_specs=[
-            spec(48, FF),
-            spec(48, FF),
-            spec(48, 1536),
-            spec(48, 768),
-            spec(48, 768),
-            spec(48, 1536),
-            spec(128, 1536),
+            spec(96, FF),
+            spec(96, FF),
+            spec(96, 1536),
+            spec(96, 768),
+            spec(96, 768),
+            spec(96, 1536),
+            spec(256, 1536),
             pl.BlockSpec((1, 384), lambda i: (0, 0)),
             pl.BlockSpec((1, 384), lambda i: (0, 0)),
         ],
@@ -135,6 +135,7 @@
 }
 NAMES = list(FLOWS)
 EARLY, LATE = NAMES[:7], NAMES[7:]
+MAIN = [name for name in EARLY if name != "out"]
 STAY = ("down", "out", "down_rest")
 
 
@@ -1138,7 +1139,7 @@
         return carry
 
     lax.fori_loop(1, 16, await_das, 0)
-    first_step(EARLY, 0)
+    first_step(MAIN, 0)
     dk[...] = jnp.zeros_like(dk)
     dv[...] = jnp.zeros_like(dv)
 
@@ -1184,7 +1185,8 @@
 
     lax.fori_loop(1, 16, send_dkv, 0)
     grad_place(1)[...] = dqs[part(64 * c, 64), 256:512]
-    first_step(EARLY, 1)
+    first_step(MAIN, 1)
+    first_step(("out",), 0)
 
     def await_dqkv(b):
         for i in range(4):
@@ -1211,8 +1213,9 @@
     lax.fori_loop(0, 4, input_grad, 0)
     @pl.when(first)
     def _():
-        first_step(EARLY, 2)
-
+        first_step(MAIN, 2)
+
+    first_step(("out",), 1)
     for n in range(2):
         rows = slice(256 * n, 256 * n + 256)
         pieces = []
@@ -1245,8 +1248,9 @@
 
     @pl.when(second)
     def _():
-        first_step(EARLY, 2)
-
+        first_step(MAIN, 2)
+
+    first_step(("out",), 2)
     second_step(EARLY, 0)
     gain_in[1, 0] = gain_sum(0)
     gain_start(1)

time: 383 us -> 380 us (level)
  no operation moved by 1% of the time
where the time goes in v8:
time: 380 us
  Pallas kernels  378 us (99%)
    pallas_call x1, Pallas kernels, run_layer(): pl.pallas_call(layer_kernel, out_shape=[jax.ShapeDtypeStruct(s, d) for s,...  365 us
    pallas_call x1, Pallas kernels, widen(): pl.pallas_call(widen_kernel, grid=(steps,), out_shape=[shape(384, FF), sh...  13 us

profile of v8, /device:TPU:0, one launch (start us, length us, event | category | flops | bytes accessed | tf_op | source)
XLA Modules:
  0.0 380.3 jit_solution(10499881606789751460)
XLA Ops:
  0.6 365.1 %layer.1 = (bf16[128,1536]{1,0:T(8,128)(2,1)}, bf16[128,1536]{1,0:T(8,128)(2,1)}, bf16[4,4,96,1024]{3,2,1,0:T(8,128)(2,1)}, bf16[4,4,96,1024]{3,2,1,0:T(8,128)(2...) custom-call(bf16[128,1536]{1,0:T(8,128)(2,1)} %bitcast.27, ...), custom_call_target="tpu_custom_call" | custom-call | tf_op jit(solution)/shard_map/layer/pallas_call | solution.py:1383
  365.8 0.0 copy-start.1
  365.8 0.0 copy-start
  365.8 13.0 %widen.1 = (f32[384,4096]{1,0:T(8,128)}, f32[384,4096]{1,0:T(8,128)}, f32[384,1536]{1,0:T(8,128)}, f32[384,768]{1,0:T(8,128)}, f32[384,768]{1,0:T(8,128)}, /*ind...) custom-call(bf16[4,4,96,1024]{3,2,1,0:T(8,128)(2,1)} %get-tuple-element.31.w_gate, ...), custom_call_target="tpu_custom_call" | custom-call | tf_op jit(solution)/shard_map/widen/pallas_call | solution.py:73
  378.8 0.0 copy-done.1
  378.8 0.7 copy.25
  379.5 0.0 copy-done
  379.5 0.7 copy.26
Async XLA Ops:
  365.8 13.0 %copy-start.1 = (bf16[128,1536]{1,0:T(8,128)(2,1)S(1)}, bf16[128,1536]{1,0:T(8,128)(2,1)}, u32[]{:S(2)}) copy-start(bf16[128,1536]{1,0:T(8,128)(2,1)} %get-tuple-element.29) | copy-start | bytes 1179652
  365.8 13.7 %copy-start = (bf16[128,1536]{1,0:T(8,128)(2,1)S(1)}, bf16[128,1536]{1,0:T(8,128)(2,1)}, u32[]{:S(2)}) copy-start(bf16[128,1536]{1,0:T(8,128)(2,1)} %get-tuple-element.30) | copy-start | bytes 1179652
